TPU v7x, 128 devices: a whole 4x4x4 slice. The times are simulated.
128 devices in a mesh: seq: 8 (over y_hi, z), res: 16 (over y_lo, x, core).
Axes of the slice: x: 4, y: 4 (y_hi: 2, y_lo: 2; y = y_hi * 2 + y_lo), z: 4, core: 2. Of those that a mesh axis runs over, the one named last changes fastest.
Arguments:
- homolog_stack: bfloat16 [384, 512, 256], P('seq', 'res'), may hold values from -64 to 64
- entry_exists_flags: int32 [384, 512], P('seq', 'res'), may hold values from 0 to 1, as said below
- genuine_amino_flags: int32 [512], replicated, may hold values 0 or 1
- couplings_tensor: bfloat16 [512, 512, 128], P('res', 'seq'), may hold values from -1.5 to 1.5
- product_source_weights: bfloat16 [256, 32], replicated, may hold values from -0.375 to 0.375
- product_target_weights: bfloat16 [256, 32], replicated, may hold values from -0.375 to 0.375
- product_final_weights: bfloat16 [1024, 128], replicated, may hold values from -0.5625 to 0.5625
- coupling_logit_offset: bfloat16 [128, 8], replicated, may hold values from -1.1953125 to 1.1953125
- horizontal_asking_weights: bfloat16 [256, 256], replicated, may hold values from -0.6 to 0.6
- horizontal_lookup_weights: bfloat16 [256, 256], replicated, may hold values from -0.6 to 0.6
- horizontal_content_weights: bfloat16 [256, 256], replicated, may hold values from -0.375 to 0.375
- horizontal_sigmoid_weights: bfloat16 [256, 256], replicated, may hold values from -0.375 to 0.375
- horizontal_final_weights: bfloat16 [256, 256], replicated, may hold values from -1.5 to 1.5
- vertical_asking_weights: bfloat16 [256, 256], replicated, may hold values from -0.6 to 0.6
- vertical_lookup_weights: bfloat16 [256, 256], replicated, may hold values from -0.6 to 0.6
- vertical_content_weights: bfloat16 [256, 256], replicated, may hold values from -0.375 to 0.375
- vertical_sigmoid_weights: bfloat16 [256, 256], replicated, may hold values from -0.375 to 0.375
- vertical_final_weights: bfloat16 [256, 256], replicated, may hold values from -1.5 to 1.5
Outputs:
- alignment_output: bfloat16 [384, 512, 256], P('seq', 'res')
- pair_output: bfloat16 [512, 512, 128], P('res', 'seq')
Inputs may be any that keep to these rules, and one draw needn't show every extreme that they name: `entry_exists_flags`: sequence 0 is present at every residue; every other sequence is present on exactly one contiguous run of residues.
All inputs are finite; a program needn't handle non-finite values.
Results may differ from a plain program's by a relative error of at most 0.02.
Values may be sent and summed in bfloat16 or wider, within the bound.
No kernel may reach another device: no remote copies, remote signals or barrier semaphores. Data moves between devices by JAX's collectives and lax.ppermute only.
A program may use at most 128 MiB of HBM per device.

v0:
```python
import math

import jax
import jax.numpy as jnp
from jax import lax
from jax.sharding import PartitionSpec as P

ATTENTION_HEADS = 8
HEAD_SIZE = 32


def standardize_features(sampled_values):
    sampled_values = sampled_values.astype(jnp.float32)
    center = sampled_values - jnp.mean(sampled_values, axis=-1, keepdims=True)
    spread = jnp.mean(center * center, axis=-1, keepdims=True)
    return center * lax.rsqrt(spread + 1e-05)


def linear_project(sampled_values, weight):
    return jnp.dot(sampled_values, weight, preferred_element_type=jnp.float32)


def softmax_last(scores):
    top = jnp.max(scores, axis=-1, keepdims=True)
    expo = jnp.exp(scores - top)
    return expo / jnp.sum(expo, axis=-1, keepdims=True)


def combine_pair(pair_rows, opm_sum, pair_count, row_mask, col_mask):
    factor = row_mask[:, None] * col_mask[None, :] / (pair_count + 0.001)
    return (pair_rows.astype(jnp.float32) + factor[..., None] * opm_sum).astype(jnp.bfloat16)


def bias_heads(pair_rows, weight):
    ln_pair = standardize_features(pair_rows).astype(jnp.bfloat16)
    return jnp.transpose(linear_project(ln_pair, weight).astype(jnp.bfloat16), (2, 0, 1))


def fold_left(left_rows, final_cube):
    folded_left = jnp.einsum(
        "sic,cdo->sdio", left_rows, final_cube, preferred_element_type=jnp.float32
    ).astype(jnp.bfloat16)
    depth, inner, rows, width = folded_left.shape
    return folded_left.reshape(depth * inner, rows, width)


def contract_right(folded_flat, right_rows):
    depth, cols, inner = right_rows.shape
    right_flat = jnp.transpose(right_rows, (0, 2, 1)).reshape(depth * inner, cols)
    return jnp.einsum("kio,kj->ijo", folded_flat, right_flat, preferred_element_type=jnp.float32)


def body(
    homolog_stack,
    entry_exists_flags,
    genuine_amino_flags,
    couplings_tensor,
    product_source_weights,
    product_target_weights,
    product_final_weights,
    coupling_logit_offset,
    horizontal_asking_weights,
    horizontal_lookup_weights,
    horizontal_content_weights,
    horizontal_sigmoid_weights,
    horizontal_final_weights,
    vertical_asking_weights,
    vertical_lookup_weights,
    vertical_content_weights,
    vertical_sigmoid_weights,
    vertical_final_weights,
):
    sequence_width = lax.axis_size("seq")
    seq_index = lax.axis_index("seq")
    res_index = lax.axis_index("res")
    homolog_number, amino_positions, homolog_feature_depth = homolog_stack.shape
    residues = genuine_amino_flags.shape[0]
    pair_cols = couplings_tensor.shape[1]
    opm_width = product_source_weights.shape[1]
    pair_width = product_final_weights.shape[1]
    score_scale = HEAD_SIZE ** (-0.5)
    mask_float = entry_exists_flags.astype(jnp.bfloat16)
    rmask = genuine_amino_flags.astype(jnp.float32)
    final_cube = product_final_weights.reshape(opm_width, opm_width, pair_width)
    standardized_homologs = standardize_features(homolog_stack).astype(jnp.bfloat16)
    left_projected = (
        linear_project(standardized_homologs, product_source_weights) * mask_float[..., None]
    ).astype(jnp.bfloat16)
    right_projected = (
        linear_project(standardized_homologs, product_target_weights) * mask_float[..., None]
    ).astype(jnp.bfloat16)
    far_right, far_mask = (
        lax.all_gather(
            right_projected.reshape(homolog_number, amino_positions * opm_width),
            "res",
            axis=1,
            tiled=True,
        ),
        lax.all_gather(mask_float, "res", axis=1, tiled=True),
    )
    row_mask = lax.dynamic_slice_in_dim(rmask, res_index * amino_positions, amino_positions)
    right_all = far_right.reshape(homolog_number, residues, opm_width)
    partial_terms = contract_right(fold_left(left_projected, final_cube), right_all)
    count_part = jnp.dot(mask_float.T, far_mask, preferred_element_type=jnp.float32)
    partial_terms, count_part = (partial_terms, count_part)
    opm_sum, pair_count = (
        lax.psum_scatter(partial_terms, "seq", scatter_dimension=1, tiled=True),
        lax.psum_scatter(count_part, "seq", scatter_dimension=1, tiled=True),
    )
    col_mask = lax.dynamic_slice_in_dim(rmask, seq_index * pair_cols, pair_cols)
    pair_output = combine_pair(couplings_tensor, opm_sum, pair_count, row_mask, col_mask)
    bias_rows = lax.all_gather(
        bias_heads(pair_output, coupling_logit_offset), "seq", axis=2, tiled=True
    )
    row_query_heads = (
        linear_project(standardized_homologs, horizontal_asking_weights) * score_scale
    ).astype(jnp.bfloat16)
    row_key_heads = linear_project(standardized_homologs, horizontal_lookup_weights).astype(
        jnp.bfloat16
    )
    row_value_heads = linear_project(standardized_homologs, horizontal_content_weights).astype(
        jnp.bfloat16
    )
    row_gate_values = jax.nn.sigmoid(
        linear_project(standardized_homologs, horizontal_sigmoid_weights)
    )
    query_heads = row_query_heads.reshape(
        homolog_number, amino_positions, ATTENTION_HEADS, HEAD_SIZE
    )
    running = jnp.full((homolog_number, ATTENTION_HEADS, amino_positions), -jnp.inf, jnp.float32)
    totals = jnp.zeros((homolog_number, ATTENTION_HEADS, amino_positions), jnp.float32)
    accum = jnp.zeros((homolog_number, ATTENTION_HEADS, amino_positions, HEAD_SIZE), jnp.float32)
    key_piece = lax.all_gather(row_key_heads, "res", axis=1, tiled=True)
    value_piece = lax.all_gather(row_value_heads, "res", axis=1, tiled=True)
    mask_piece = lax.all_gather(mask_float, "res", axis=1, tiled=True)
    width = key_piece.shape[1]
    sub = math.gcd(width, 128)
    for part_index in range(width // sub):
        low = part_index * sub
        key_block = key_piece[:, low : low + sub].reshape(
            homolog_number, sub, ATTENTION_HEADS, HEAD_SIZE
        )
        value_block = value_piece[:, low : low + sub].reshape(
            homolog_number, sub, ATTENTION_HEADS, HEAD_SIZE
        )
        mask_block = mask_piece[:, low : low + sub]
        bias_block = lax.dynamic_slice_in_dim(bias_rows, low, sub, 2).astype(jnp.float32)
        scores = (
            jnp.einsum(
                "sihd,sjhd->shij", query_heads, key_block, preferred_element_type=jnp.float32
            )
            + bias_block[None]
        )
        scores = jnp.where(mask_block[:, None, None, :] > 0, scores, -1000000000.0)
        newest = jnp.maximum(running, jnp.max(scores, axis=-1))
        correction = jnp.exp(running - newest)
        expo = jnp.exp(scores - newest[..., None])
        totals = totals * correction + jnp.sum(expo, axis=-1)
        accum = accum * correction[..., None] + jnp.einsum(
            "shij,sjhd->shid", expo, value_block.astype(jnp.float32)
        )
        running = newest
    running, totals, accum = (running, totals, accum)
    attended = jnp.transpose(accum / totals[..., None], (0, 2, 1, 3)).reshape(
        homolog_number, amino_positions, ATTENTION_HEADS * HEAD_SIZE
    )
    row_gated = (row_gate_values * attended).astype(jnp.bfloat16)
    horizontal_increment = linear_project(row_gated, horizontal_final_weights).astype(jnp.bfloat16)
    homolog_intermediate = (
        homolog_stack.astype(jnp.float32) + horizontal_increment.astype(jnp.float32)
    ).astype(jnp.bfloat16)
    normalized_middle = standardize_features(homolog_intermediate).astype(jnp.bfloat16)
    normalized_blocks = normalized_middle.reshape(
        homolog_number, sequence_width, amino_positions // sequence_width, homolog_feature_depth
    )
    mask_blocks = mask_float.reshape(
        homolog_number, sequence_width, amino_positions // sequence_width
    )
    ln_cols = lax.all_to_all(normalized_blocks, "seq", split_axis=1, concat_axis=0, tiled=True)[
        :, 0
    ]
    mask_cols = lax.all_to_all(mask_blocks, "seq", split_axis=1, concat_axis=0, tiled=True)[:, 0]
    depth, item_count = mask_cols.shape
    query_cols = (
        (linear_project(ln_cols, vertical_asking_weights) * score_scale)
        .astype(jnp.bfloat16)
        .reshape(depth, item_count, ATTENTION_HEADS, HEAD_SIZE)
    )
    key_cols = (
        linear_project(ln_cols, vertical_lookup_weights)
        .astype(jnp.bfloat16)
        .reshape(depth, item_count, ATTENTION_HEADS, HEAD_SIZE)
    )
    value_cols = (
        linear_project(ln_cols, vertical_content_weights)
        .astype(jnp.bfloat16)
        .reshape(depth, item_count, ATTENTION_HEADS, HEAD_SIZE)
    )
    gate_cols = jax.nn.sigmoid(linear_project(ln_cols, vertical_sigmoid_weights))

    def one_column(pick):
        query_one = lax.dynamic_index_in_dim(query_cols, pick, 1, False)
        key_one = lax.dynamic_index_in_dim(key_cols, pick, 1, False)
        value_one = lax.dynamic_index_in_dim(value_cols, pick, 1, False)
        mask_one = lax.dynamic_index_in_dim(mask_cols, pick, 1, False)
        scores = jnp.einsum("shd,thd->hst", query_one, key_one, preferred_element_type=jnp.float32)
        scores = jnp.where(mask_one[None, None, :] > 0, scores, -1000000000.0)
        weights = softmax_last(scores)
        return jnp.einsum("hst,thd->shd", weights, value_one.astype(jnp.float32)).reshape(
            depth, ATTENTION_HEADS * HEAD_SIZE
        )

    columns = lax.map(one_column, jnp.arange(item_count, dtype=jnp.int32))
    attended = jnp.transpose(columns, (1, 0, 2))
    gated = (gate_cols * attended).astype(jnp.bfloat16)
    full_cols = linear_project(gated, vertical_final_weights).astype(jnp.bfloat16)[:, None]
    column_restored = lax.all_to_all(full_cols, "seq", split_axis=0, concat_axis=1, tiled=True)
    column_delta = column_restored.reshape(homolog_number, amino_positions, homolog_feature_depth)
    alignment_output = (
        homolog_intermediate.astype(jnp.float32) + column_delta.astype(jnp.float32)
    ).astype(jnp.bfloat16)
    return (alignment_output, pair_output)


def solution(mesh):
    in_specs = (
        P("seq", "res", None),
        P("seq", "res"),
        P(),
        P("res", "seq", None),
        P(),
        P(),
        P(),
        P(),
        P(),
        P(),
        P(),
        P(),
        P(),
        P(),
        P(),
        P(),
        P(),
        P(),
    )
    out_specs = (P("seq", "res", None), P("res", "seq", None))
    return jax.shard_map(body, mesh=mesh, in_specs=in_specs, out_specs=out_specs, check_vma=False)
```

profile of v0, /device:TPU:8, one launch (start us, length us, event | category | flops | bytes accessed | tf_op | source)
XLA Modules:
  0.0 551.9 jit_solution(524889456139746779)
XLA Ops:
  16.3 19.4 %all_gather.16 = bf16[48,512]{0,1:T(8,128)(2,1)S(1)} all-gather(bf16[48,32]{0,1:T(8,128)(2,1)} %convert_element_type.126), channel_id=1, replica_groups=mesh['seq'=8,'res'=16] {'res'}, dimensions={1}, use_global_device_ids=true | all-gather | bytes 52224 | tf_op jit(solution)/shard_map/all_gather | solution.py:135
  38.2 6.4 %convert_bitcast_fusion = bf16[48,32,32,128]{3,0,1,2:T(8,128)(2,1)} fusion(bf16[48,32,32,1]{2,1,0,3:T(8,128)(2,1)S(1)} %fusion.79, bf16[32,32,128]{2,1,0:T(8,128)(2,1)S(1)} %bitcast.255), kind=kOutput, calls=%fused_computation.23 | convolution fusion | flops 408944640 | bytes 12943360 | tf_op jit(solution)/shard_map/sic,cdo->sdio/dot_general | solution.py:40
  44.6 6.9 %all-gather.6.cloned.1.call-done = bf16[48,16384]{1,0:T(8,128)(2,1)} async-done(((bf16[48,1024]{1,0:T(8,128)(2,1)}), bf16[48,16384]{1,0:T(8,128)(2,1)}) %all-gather.6.cloned.1.call-update) | async-done | bytes 1572880 | tf_op jit(solution)/shard_map/all_gather | solution.py:93
  51.5 7.5 %reshape.212 = bf16[48,512,32]{2,1,0:T(8,128)(2,1)} reshape(bf16[48,16384]{1,0:T(8,128)(2,1)} %all-gather.6.cloned.1.call-done) | data formatting | bytes 3145728 | tf_op jit(solution)/shard_map/reshape | solution.py:102
  59.0 5.1 copy.226
  64.2 12.1 %fusion.35 = f32[32,512,128]{2,1,0:T(8,128)} fusion(bf16[48,32,32,128]{3,0,1,2:T(8,128)(2,1)} %convert_bitcast_fusion, bf16[48,512,32]{1,2,0:T(8,128)(2,1)S(1)} %copy.226), kind=kOutput, calls=%fused_computation.52 | convolution fusion | flops 6442450944 | bytes 22544384 | tf_op jit(solution)/shard_map/kio,kj->ijo/dot_general | solution.py:50
  80.2 6.3 %all-to-all-start.1 = ((bf16[48,8,4]{0,2,1:T(4,128)(2,1)}), bf16[48,8,4]{0,2,1:T(4,128)(2,1)}, u32[]{:S(2)}, u32[]{:S(2)}) async-start(bf16[48,8,4]{0,2,1:T(4,128)(2,1)} %bitcast.50), calls=%async_computation.2 | async-start | bytes 16384 | tf_op jit(solution)/shard_map/all_to_all | solution.py:182
  88.6 3.4 reshape.209
  93.2 18.1 %reduce-scatter.7.cloned.1.call-done = f32[64,32]{1,0:T(8,128)} async-done(((f32[512,32]{1,0:T(8,128)}), f32[64,32]{1,0:T(8,128)}) %reduce-scatter.7.cloned.1.call-update) | async-done | bytes 8208
  112.2 160.6 %reduce-scatter.5.cloned.1.call-done = f32[32,64,128]{2,1,0:T(8,128)} async-done(((f32[32,512,128]{2,1,0:T(8,128)}), f32[32,64,128]{2,1,0:T(8,128)}) %reduce-scatter.5.cloned.1.call-update) | async-done | bytes 1048592 | tf_op jit(solution)/shard_map/reduce_scatter | solution.py:107
  272.9 2.0 convert_reduce_fusion.2
  276.6 36.3 %all_gather.19 = bf16[8,32,512]{1,0,2:T(8,128)(2,1)S(1)} all-gather(bf16[8,32,64]{1,0,2:T(8,128)(2,1)S(1)} %copy.230), channel_id=1, replica_groups=mesh['seq'=8,'res'=16] {'seq'}, dimensions={2}, use_global_device_ids=true | all-gather | bytes 294912 | tf_op jit(solution)/shard_map/all_gather | solution.py:112
  325.2 9.2 %fusion.129 = (bf16[48,128,256]{2,1,0:T(8,128)(2,1)}, bf16[48,128,256]{2,1,0:T(8,128)(2,1)}, bf16[48,128,256]{2,1,0:T(8,128)(2,1)}, bf16[48,128,256]{2,1,0:T(8,128)(2,1)}) fusion(bf16[48,512,256]{2,1,0:T(8,128)(2,1)} %all-gather.4.cloned.1.call-done), kind=kLoop, calls=%fused_computation.177 | loop fusion | bytes 25165824 | tf_op jit(solution)/shard_map/slice | solution.py:140
  334.3 4.7 copy.234
  339.0 9.3 %fusion.128 = (bf16[48,128,256]{2,1,0:T(8,128)(2,1)}, bf16[48,128,256]{2,1,0:T(8,128)(2,1)}, bf16[48,128,256]{2,1,0:T(8,128)(2,1)}, bf16[48,128,256]{2,1,0:T(8,128)(2,1)}) fusion(bf16[48,512,256]{2,1,0:T(8,128)(2,1)} %all-gather.8.cloned.1.call-done), kind=kLoop, calls=%fused_computation.176 | loop fusion | bytes 25165824 | tf_op jit(solution)/shard_map/slice | solution.py:143
  348.3 4.7 copy.247
  353.0 4.7 copy.242
  357.7 4.6 copy.237
  362.3 4.7 copy.232
  367.0 4.7 copy.244
  371.6 4.7 copy.239
  376.3 4.7 copy.223
  381.0 4.0 fusion.26
  385.1 1.9 fusion.23
  387.0 1.9 fusion.25
  388.9 3.9 fusion.24
  393.7 5.4 fusion.32
  399.0 20.5 %fusion.29 = (f32[48,8,32]{2,1,0:T(8,128)}, f32[48,8,32]{2,1,0:T(8,128)}) fusion(f32[48,8,32,128]{3,2,1,0:T(8,128)S(1)} %get-tuple-element.89, f32[48,8,32]{2,1,0:T(8,128)} %get-tuple-element.60, f32[8,32,128]{2,1,0:T(8,128)S(1)} %copy-done.12, pred[48,128]{1,0:T(8,128)(4,1)S(1)} %broadcast_compare_fusion.2, f32[48,8,32]{2,1,0:T(8,128)} %copy-done.15, ...), kind=kLoop, calls=%fused_computation.46 | loop fusion | flops 12558336 | bytes 13053952 | tf_op jit(solution)/shard_map/reduce_sum | solution.py:158
  419.6 5.5 %fusion.30 = f32[48,8,32,32]{3,2,1,0:T(8,128)} fusion(bf16[48,128,8,32]{1,3,2,0:T(8,128)(2,1)S(1)} %bitcast.234, f32[48,8,32,128]{3,2,1,0:T(8,128)S(1)} %get-tuple-element.89, f32[48,8,32]{2,1,0:T(8,128)} %get-tuple-element.60, f32[8,32,128]{2,1,0:T(8,128)} %convert_element_type.143, pred[48,128]{1,0:T(8,128)(4,1)S(1)} %broadcast_compare_fusion.2), kind=kOutput, calls=%fused_computation.47 | convolution fusion | flops 105381888 | bytes 11196416 | tf_op jit(solution)/shard_map/shij,sjhd->shid/dot_general | solution.py:159
  425.1 4.2 fusion.28
  429.4 8.9 %fusion.27 = (f32[48,8,32]{2,1,0:T(8,128)S(1)}, f32[48,8,32]{2,1,0:T(8,128)S(1)}) fusion(f32[48,8,32,128]{3,2,1,0:T(8,128)S(1)} %get-tuple-element.87, f32[48,8,32]{2,1,0:T(8,128)S(1)} %get-tuple-element.86, f32[8,32,128]{2,1,0:T(8,128)S(1)} %copy-done.10, pred[48,128]{1,0:T(8,128)(4,1)S(1)} %broadcast_compare_fusion.3, f32[48,8,32]{2,1,0:T(8,128)} %get-tuple-element.58, ...), kind=kLoop, calls=%fused_computation.44 | loop fusion | flops 12558336 | bytes 13053952 | tf_op jit(solution)/shard_map/reduce_sum | solution.py:158
  439.8 10.1 %fusion.19 = f32[48,32,8,32]{3,1,2,0:T(8,128)S(1)} fusion(f32[48,8,32,32]{3,2,1,0:T(8,128)S(1)} %bitcast.246, f32[48,8,32,32]{3,2,1,0:T(8,128)S(1)} %bitcast.248, f32[48,8,32,32]{3,2,1,0:T(8,128)S(1)} %copy-done.5, f32[48,32,8]{1,2,0:T(8,128)S(1)} %get-tuple-element.54, f32[48,32,8]{1,2,0:T(8,128)S(1)} %get-tuple-element.57, ...), kind=kOutput, calls=%fused_computation.25 | convolution fusion | flops 108527616 | bytes 16160768 | tf_op jit(solution)/shard_map/shij,sjhd->shid/dot_general | solution.py:159
  449.9 8.7 %copy.248 = f32[48,32,8,32]{3,2,1,0:T(8,128)} copy(f32[48,32,8,32]{3,1,2,0:T(8,128)S(1)} %fusion.19) | data formatting | bytes 3145728 | tf_op jit(solution)/shard_map/div | solution.py:164
  458.7 5.4 reshape.221
  464.1 2.3 convert_reduce_fusion
  468.9 4.8 all-to-all-start
  474.4 10.0 %all-to-all-done = bf16[48,8,4,256]{3,2,0,1:T(4,128)(2,1)S(1)} async-done(((bf16[48,8,4,256]{3,2,0,1:T(4,128)(2,1)}), bf16[48,8,4,256]{3,2,0,1:T(4,128)(2,1)S(1)}, u32[]{:S(2)}, u32[]{:S(2)}) %all-to-all-start) | async-done | bytes 786464 | tf_op jit(solution)/shard_map/all_to_all | solution.py:179
  487.7 34.6 %while.10 = (s32[]{:T(128)}, f32[4,384,256]{2,1,0:T(8,128)}, s32[4]{0:T(128)S(1)}, bf16[384,4,8,32]{0,3,2,1:T(8,128)(2,1)}, bf16[384,4]{0,1:T(4,128)(2,1)S(1)}, ...) while((s32[]{:T(128)}, f32[4,384,256]{2,1,0:T(8,128)}, ...), condition=%wide.region_19.20_spmd, body=%wide.region_16.19_spmd.sunk | while | flops 160427136 | bytes 16776743 | solution.py:213
  490.4 1.9 select_reduce_fusion.2
  493.3 2.1 fusion.158
  499.1 1.9 select_reduce_fusion.2
  501.9 2.1 fusion.158
  507.7 1.9 select_reduce_fusion.2
  510.5 2.1 fusion.158
  516.4 1.9 select_reduce_fusion.2
  519.2 2.1 fusion.158
  522.2 2.1 fusion.74
  525.0 14.8 %all_to_all.39 = bf16[384,1,4,256]{3,2,1,0:T(4,128)(2,1)S(1)} all-to-all(bf16[384,1,4,256]{3,2,1,0:T(4,128)(2,1)S(1)} %copy.256), channel_id=1, replica_groups=mesh['seq'=8,'res'=16] {'seq'}, dimensions={0} | all-to-all | bytes 1572864 | tf_op jit(solution)/shard_map/all_to_all | solution.py:217
  (186 shorter events, 56.6 us)
Async XLA Ops:
  8.0 456.1 %copy-start = (bf16[256,256]{1,0:T(8,128)(2,1)S(1)}, bf16[256,256]{1,0:T(8,128)(2,1)}, u32[]{:S(2)}) copy-start(bf16[256,256]{1,0:T(8,128)(2,1)} %param.32) | copy-start | bytes 393220
  8.0 29.3 %copy-start.7 = (bf16[48,32,256]{2,1,0:T(8,128)(2,1)S(1)}, bf16[48,32,256]{2,1,0:T(8,128)(2,1)}, u32[]{:S(2)}) copy-start(bf16[48,32,256]{2,1,0:T(8,128)(2,1)} %param.20) | copy-start | bytes 2359300
  8.0 29.3 %copy-start.39 = (bf16[256,32]{0,1:T(8,128)(2,1)S(1)}, bf16[256,32]{0,1:T(8,128)(2,1)}, u32[]{:S(2)}) copy-start(bf16[256,32]{0,1:T(8,128)(2,1)} %param.24) | copy-start | bytes 49156
  8.0 43.5 %all-gather.6.cloned.1.call-start = ((), (), s32[]{:S(2)}) async-start(), calls=%async_computation.6 | async-start | bytes 1671168 | tf_op jit(solution)/shard_map/all_gather | solution.py:93
  11.7 75.4 %copy-start.27 = (f32[48,32]{1,0:T(8,128)}, f32[48,32]{1,0:T(8,128)S(1)}, u32[]{:S(2)}) copy-start(f32[48,32]{1,0:T(8,128)S(1)} %broadcast_multiply_fusion.1) | copy-start | bytes 18436
  11.7 26.5 %copy-start.22 = (bf16[1024,128]{1,0:T(8,128)(2,1)S(1)}, bf16[1024,128]{1,0:T(8,128)(2,1)}, u32[]{:S(2)}) copy-start(bf16[1024,128]{1,0:T(8,128)(2,1)} %param.26) | copy-start | bytes 786436
  13.4 73.7 %copy-start.30 = (f32[48,32]{1,0:T(8,128)}, f32[48,32]{1,0:T(8,128)S(1)}, u32[]{:S(2)}) copy-start(f32[48,32]{1,0:T(8,128)S(1)} %add_rsqrt_fusion.1) | copy-start | bytes 18436
  16.3 95.1 %reduce-scatter.7.cloned.1.call-start = ((), (), s32[]{:S(2)}) async-start(), calls=%async_computation.9 | async-start | bytes 294912
  37.3 235.6 %reduce-scatter.5.cloned.1.call-start = ((), (), s32[]{:S(2)}) async-start(), calls=%async_computation.7 | async-start | bytes 9437184 | tf_op jit(solution)/shard_map/reduce_scatter | solution.py:107
  76.3 2.5 copy-start.34
  76.3 10.3 %copy-start.32 = (s32[512]{0:T(512)S(1)}, s32[512]{0:T(512)}, u32[]{:S(2)}) copy-start(s32[512]{0:T(512)} %param.22) | copy-start | bytes 6148
  76.3 10.8 %copy-start.35 = (bf16[256,256]{1,0:T(8,128)(2,1)S(1)}, bf16[256,256]{1,0:T(8,128)(2,1)}, u32[]{:S(2)}) copy-start(bf16[256,256]{1,0:T(8,128)(2,1)} %param.28) | copy-start | bytes 393220
  76.3 248.8 %all-gather.4.cloned.1.call-start = ((), (), s32[]{:S(2)}) async-start(), calls=%async_computation.5 | async-start | bytes 13369344 | tf_op jit(solution)/shard_map/all_gather | solution.py:133
  78.7 260.4 %all-gather.8.cloned.1.call-start = ((), (), s32[]{:S(2)}) async-start(), calls=%async_computation.8 | async-start | bytes 13369344 | tf_op jit(solution)/shard_map/all_gather | solution.py:134
  80.2 388.6 %all-to-all-start.1 = ((bf16[48,8,4]{0,2,1:T(4,128)(2,1)}), bf16[48,8,4]{0,2,1:T(4,128)(2,1)}, u32[]{:S(2)}, u32[]{:S(2)}) async-start(bf16[48,8,4]{0,2,1:T(4,128)(2,1)} %bitcast.50), calls=%async_computation.2 | async-start | bytes 16384 | tf_op jit(solution)/shard_map/all_to_all | solution.py:182
  88.6 187.1 %copy-start.40 = (bf16[128,8]{0,1:T(8,128)(2,1)S(1)}, bf16[128,8]{0,1:T(8,128)(2,1)}, u32[]{:S(2)}) copy-start(bf16[128,8]{0,1:T(8,128)(2,1)} %param.27) | copy-start | bytes 6148
  325.1 55.9 %copy-start.19 = (f32[8,32,128]{2,1,0:T(8,128)}, f32[8,32,128]{2,1,0:T(8,128)S(1)}, u32[]{:S(2)}) copy-start(f32[8,32,128]{2,1,0:T(8,128)S(1)} %convert_element_type.145) | copy-start | bytes 393220
  376.3 4.7 copy-start.29
  381.0 4.0 copy-start.4
  381.0 4.0 copy-start.9
  385.1 7.8 %copy-start.16 = (f32[48,8,32]{2,1,0:T(8,128)}, f32[48,8,32]{2,1,0:T(8,128)S(1)}, u32[]{:S(2)}) copy-start(f32[48,8,32]{2,1,0:T(8,128)S(1)} %get-tuple-element.82) | copy-start | bytes 147460
  385.1 2.0 copy-start.3
  385.1 1.9 copy-start.13
  385.1 1.9 copy-start.26
  388.9 3.9 copy-start.17
  393.6 5.4 copy-start.15
  393.7 5.4 copy-start.12
  399.0 20.5 %copy-start.2 = (bf16[48,128,256]{1,2,0:T(8,128)(2,1)S(1)}, bf16[48,128,256]{1,2,0:T(8,128)(2,1)}, u32[]{:S(2)}) copy-start(bf16[48,128,256]{1,2,0:T(8,128)(2,1)} %copy.237) | copy-start | bytes 9437188
  419.6 5.6 %copy-start.1 = (bf16[48,128,256]{1,2,0:T(8,128)(2,1)S(1)}, bf16[48,128,256]{1,2,0:T(8,128)(2,1)}, u32[]{:S(2)}) copy-start(bf16[48,128,256]{1,2,0:T(8,128)(2,1)} %copy.232) | copy-start | bytes 9437188
  419.6 5.6 %copy-start.10 = (f32[8,32,128]{2,1,0:T(8,128)S(1)}, f32[8,32,128]{2,1,0:T(8,128)}, u32[]{:S(2)}) copy-start(f32[8,32,128]{2,1,0:T(8,128)} %convert_element_type.141) | copy-start | bytes 393220
  425.1 14.6 %slice-start = ((s8[6291456]{0:T(1024)(128)(4,1)}), s8[4194304]{0:T(1024)(128)(4,1)S(1)}, s32[]{:S(2)}) async-start(s8[6291456]{0:T(1024)(128)(4,1)} %bitcast.245), calls=%async_computation.10 | async-start | bytes 8388608
  425.1 14.6 %slice-start.2 = ((s8[6291456]{0:T(1024)(128)(4,1)}), s8[2097152]{0:T(1024)(128)(4,1)S(1)}, s32[]{:S(2)}) async-start(s8[6291456]{0:T(1024)(128)(4,1)} %bitcast.247), calls=%async_computation.12 | async-start | bytes 4194304
  429.3 10.4 %slice-start.1 = ((s8[6291456]{0:T(1024)(128)(4,1)}), s8[2097152]{0:T(1024)(128)(4,1)S(1)}, s32[]{:S(2)}) async-start(s8[6291456]{0:T(1024)(128)(4,1)} %bitcast.245), calls=%async_computation.11 | async-start | bytes 4194304
  429.3 10.4 %slice-start.3 = ((s8[6291456]{0:T(1024)(128)(4,1)}), s8[4194304]{0:T(1024)(128)(4,1)S(1)}, s32[]{:S(2)}) async-start(s8[6291456]{0:T(1024)(128)(4,1)} %bitcast.247), calls=%async_computation.13 | async-start | bytes 8388608
  429.3 10.5 %copy-start.5 = (f32[48,8,32,32]{3,2,1,0:T(8,128)S(1)}, f32[48,8,32,32]{3,2,1,0:T(8,128)}, u32[]{:S(2)}) copy-start(f32[48,8,32,32]{3,2,1,0:T(8,128)} %fusion.28) | copy-start | bytes 4718596
  429.3 10.5 %copy-start.6 = (bf16[48,128,256]{1,2,0:T(8,128)(2,1)S(1)}, bf16[48,128,256]{1,2,0:T(8,128)(2,1)}, u32[]{:S(2)}) copy-start(bf16[48,128,256]{1,2,0:T(8,128)(2,1)} %copy.247) | copy-start | bytes 9437188
  429.3 10.5 %copy-start.20 = (f32[8,32,128]{2,1,0:T(8,128)S(1)}, f32[8,32,128]{2,1,0:T(8,128)}, u32[]{:S(2)}) copy-start(f32[8,32,128]{2,1,0:T(8,128)} %copy-done.19) | copy-start | bytes 393220
  429.4 10.5 %copy-start.21 = (f32[48,8,32]{2,1,0:T(8,128)S(1)}, f32[48,8,32]{2,1,0:T(8,128)}, u32[]{:S(2)}) copy-start(f32[48,8,32]{2,1,0:T(8,128)} %get-tuple-element.58) | copy-start | bytes 147460
  458.7 5.4 copy-start.8
  458.7 5.4 copy-start.28
  458.7 5.4 copy-start.31
  458.7 5.4 copy-start.36
  467.5 17.1 %copy-start.23 = (bf16[256,256]{1,0:T(8,128)(2,1)S(1)}, bf16[256,256]{1,0:T(8,128)(2,1)}, u32[]{:S(2)}) copy-start(bf16[256,256]{1,0:T(8,128)(2,1)} %param.34) | copy-start | bytes 393220
  467.7 17.4 %copy-start.24 = (bf16[256,256]{1,0:T(8,128)(2,1)S(1)}, bf16[256,256]{1,0:T(8,128)(2,1)}, u32[]{:S(2)}) copy-start(bf16[256,256]{1,0:T(8,128)(2,1)} %param.33) | copy-start | bytes 393220
  468.8 17.5 %copy-start.25 = (bf16[256,256]{1,0:T(8,128)(2,1)S(1)}, bf16[256,256]{1,0:T(8,128)(2,1)}, u32[]{:S(2)}) copy-start(bf16[256,256]{1,0:T(8,128)(2,1)} %param.35) | copy-start | bytes 393220
  468.9 15.6 %all-to-all-start = ((bf16[48,8,4,256]{3,2,0,1:T(4,128)(2,1)}), bf16[48,8,4,256]{3,2,0,1:T(4,128)(2,1)S(1)}, u32[]{:S(2)}, u32[]{:S(2)}) async-start(bf16[48,8,4,256]{3,2,0,1:T(4,128)(2,1)} %copy.249), calls=%async_computation.1 | async-start | bytes 1572864 | tf_op jit(solution)/shard_map/all_to_all | solution.py:179
  487.7 34.6 %copy-start.37 = (bf16[256,256]{1,0:T(8,128)(2,1)S(1)}, bf16[256,256]{1,0:T(8,128)(2,1)}, u32[]{:S(2)}) copy-start(bf16[256,256]{1,0:T(8,128)(2,1)} %param.37) | copy-start | bytes 393220
  487.7 34.6 %copy-start.38 = (bf16[256,256]{1,0:T(8,128)(2,1)S(1)}, bf16[256,256]{1,0:T(8,128)(2,1)}, u32[]{:S(2)}) copy-start(bf16[256,256]{1,0:T(8,128)(2,1)} %param.36) | copy-start | bytes 393220
  (4 other events, 4.4 us)
Sparse Core Ops, SparseCore 0:
  16.4 35.0 all-gather.5
  78.8 87.7 all-gather.3
  168.8 105.1 all-gather.7
Sparse Core Ops, SparseCore 1:
  37.4 73.9 reduce-scatter.6
  115.0 157.8 reduce-scatter.4
where the time goes:
time: 562 us; the launch traced here: 552 us
  waiting for transfers between devices  196 us (35%)
  local copies, waits for them, and re-layouts  108 us (19%)
  matrix products  88.2 us (16%)
  blocking collectives  70.5 us (13%)
  other arithmetic  52.9 us (9%)
  between operations  16.4 us (3%)
  starting transfers between devices  11.3 us (2%)
  loops' own time  8.38 us (1%)
    reduce_scatter x1, waiting for transfers between devices, body(): lax.psum_scatter(partial_terms, 'seq', scatter_dimension=1, tiled=True)  161 us
    all_gather x1, blocking collectives, body(): lax.all_gather(bias_heads(pair_output, coupling_logit_offset), 'seq', axi...  36.3 us
    reduce_sum x2, other arithmetic, body(): totals = totals * correction + jnp.sum(expo, axis=-1)  29.5 us
    slice x5, local copies, waits for them, and re-layouts, body(): value_piece[:, low:low + sub]  28 us
    slice x5, local copies, waits for them, and re-layouts, body(): key_piece[:, low:low + sub]  27.9 us
    dot_general x4, matrix products, body(): jnp.einsum('shij,sjhd->shid', expo, value_block.astype(jnp.float32))  25.2 us
    all_gather x1, blocking collectives, body(): mask_piece = lax.all_gather(mask_float, 'res', axis=1, tiled=True)  19.4 us
    unnamed x6, waiting for transfers between devices  18.2 us
  transfers between devices with their start and end apart: 7, of which 4 were waited for; matrix products, arithmetic and copies ran while one was open for 37% of the time, Pallas kernels for 0%

commit v1 on v0

v1 whole, which is shorter than its diff:
```python
import math

import jax
import jax.numpy as jnp
from jax import lax
from jax.experimental import pallas as pl
from jax.experimental.pallas import tpu as pltpu
from jax.sharding import Mesh
from jax.sharding import PartitionSpec as P

HEADS = 8
HEAD = 32
F32 = jnp.float32
BF16 = jnp.bfloat16
NEG = -1e9
STEP = 3
PICK = 2
SEQ = ("yh", "z")
RES = ("yl", "xh", "xl", "core")
ALL = SEQ + RES
TEAM = ("yl", "xh")
PLANE = SEQ + TEAM
NT = (((1,), (1,)), ((), ()))
TN = (((0,), (0,)), ((), ()))
VMEM_LIMIT = 24 * 1024 * 1024
LOG2E = math.log2(math.e)


def normalize(values):
    values = values.astype(F32)
    center = values - jnp.mean(values, axis=-1, keepdims=True)
    spread = jnp.mean(center * center, axis=-1, keepdims=True)
    return (center * lax.rsqrt(spread + 1e-5)).astype(BF16)


def project(values, weight):
    return jnp.dot(values, weight, preferred_element_type=F32)


class Attention:
    def __init__(self, query_t, key, value_t, bias_of, mask_lanes, lane):
        self.query_t, self.key, self.value_t = query_t, key, value_t
        self.bias_of, self.mask_lanes, self.lane = bias_of, mask_lanes, lane
        self.count = query_t.shape[1]
        self.found = []

    def score(self, pair):
        part = slice(pair // 2 * 128, pair // 2 * 128 + 128)
        own = self.query_t[part]
        row = lax.broadcasted_iota(jnp.int32, own.shape, 0)
        one = jnp.where(row == self.lane, 1.0, 0.0).astype(BF16)
        stacked = []
        for h in range(2):
            mine = row // HEAD == pair % 2 * 2 + h
            stacked.append(jnp.concatenate([jnp.where(mine, own, jnp.zeros_like(own)), one], axis=0))
        keys = jnp.concatenate([self.key[:, part], self.mask_lanes], axis=1)
        return project(keys, jnp.concatenate(stacked, axis=1))

    def weigh(self, pair, scores):
        weights = []
        for h in range(2):
            extra = self.bias_of(pair * 2 + h)
            for low in range(0, self.count, 128):
                tile = scores[:, h * self.count + low : h * self.count + low + 128]
                if extra is not None:
                    tile = tile + extra[:, low : low + 128]
                weights.append(jnp.exp2(tile - jnp.max(tile, axis=0, keepdims=True)).astype(BF16))
        return jnp.concatenate(weights, axis=1)

    def mix(self, pair, weights):
        ones = jnp.ones((16, self.value_t.shape[1]), BF16)
        values = jnp.concatenate([self.value_t[pair * 64 : pair * 64 + 64], ones], axis=0)
        mixed = project(values, weights)
        for h in range(2):
            cols = slice(h * self.count, (h + 1) * self.count)
            self.found.append(mixed[h * HEAD : (h + 1) * HEAD, cols] / mixed[64:65, cols])

    def result(self):
        return jnp.concatenate(self.found, axis=0)


def run_pipelined(attentions, finish):
    units = [(a, pair) for a in attentions for pair in range(4)]
    ahead = units[0][0].score(0)
    for place, (attention, pair) in enumerate(units):
        scores = ahead
        if place + 1 < len(units):
            ahead = units[place + 1][0].score(units[place + 1][1])
        attention.mix(pair, attention.weigh(pair, scores))
        if pair == 3:
            finish(attentions.index(attention), attention.result())


def mask_columns(mask_row):
    shape = (128, mask_row.shape[1])
    top = lax.broadcasted_iota(jnp.int32, shape, 0) == 0
    return jnp.where(top, jnp.broadcast_to(mask_row, shape), 0.0).astype(BF16).T


def factor_kernel(x_ref, mask_ref, source_ref, target_ref, left_ref, right_ref, lefts, rights):
    ln = normalize(x_ref[...].reshape(1536, 256))
    mask = mask_ref[...].astype(F32).T
    lefts[:, :32] = lax.dot_general(ln, source_ref[...], NT, preferred_element_type=F32)
    turned = lax.dot_general(target_ref[...], ln, NT, preferred_element_type=F32)
    for s in range(48):
        rights[s * 32 : (s + 1) * 32, :32] = turned[:, s * 32 : (s + 1) * 32]
    wide = jnp.concatenate([mask] * 4, axis=1)
    for tile in range(8):
        lanes = slice(tile * 128, (tile + 1) * 128)
        spots = [pl.ds(tile * 4 + e, 48, stride=32) for e in range(4)]
        parts = [lefts[spot, :][:, :32] for spot in spots]
        parts = [p * mask[:, tile * 4 + e : tile * 4 + e + 1] for e, p in enumerate(parts)]
        left_ref[:, lanes] = jnp.concatenate(parts, axis=1).astype(BF16)
        parts = [rights[spot, :][:, :32] for spot in spots]
        right_ref[:, lanes] = (jnp.concatenate(parts, axis=1) * wide).astype(BF16)
    tail = jnp.concatenate([mask, jnp.zeros((48, 96), F32)], axis=1).astype(BF16)
    left_ref[:, 1024:] = tail
    right_ref[:, 1024:] = tail


def pair_kernel(at_ref, *refs):
    left_pieces = refs[:4]
    mine_ref, other_ref, pair_ref, rows_ref, cols_ref, final_ref, offset_ref = refs[4:11]
    out_ref, bias_ref, column_ref, left_hold, right_hold, hold = refs[11:]
    seq_at, core = at_ref[0], at_ref[1]
    right_hold[core] = mine_ref[...]
    right_hold[1 - core] = other_ref[...]
    for k in range(8):
        left_hold[seq_at ^ k] = left_pieces[k % 4][k // 4]
    left_all = left_hold[...].reshape(384, 1152)
    right = [right_hold[p].reshape(384, 1152) for p in range(2)]
    left_mask = left_all[:, 1024:1056]
    picks = lax.broadcasted_iota(jnp.int32, (8, 32), 0) + seq_at * 4
    picks = (picks == lax.broadcasted_iota(jnp.int32, (8, 32), 1)).astype(BF16)
    present = lax.dot_general(picks, left_mask, NT, preferred_element_type=F32)
    column_ref[...] = (present - 1.0) * -NEG
    count = jnp.concatenate(
        [
            lax.dot_general(r[:, 1024:1056], left_mask, TN, preferred_element_type=F32)
            for r in right
        ],
        axis=0,
    )
    factor = cols_ref[...] * rows_ref[...] / (count + 0.001)
    offset = offset_ref[...]
    def outer_of(block):
        left = left_all[:, block * 256 : (block + 1) * 256]
        return [
            lax.dot_general(left, r[:, :1024], TN, preferred_element_type=F32).astype(BF16)
            for r in right
        ]

    ahead = outer_of(0)
    for block in range(4):
        outer = ahead
        if block < 3:
            ahead = outer_of(block + 1)
        turned = []
        for i in range(8):
            for p in range(2):
                rows = outer[p][i * 32 : (i + 1) * 32]
                tiles = [rows[:, t * 128 : (t + 1) * 128] for t in range(8)]
                turned.append(jnp.concatenate(tiles, axis=0).T)
        terms = None
        for e in range(4):
            lhs = jnp.concatenate([t[e * 32 : (e + 1) * 32] for t in turned], axis=0)
            part = project(lhs, final_ref[e])
            terms = part if terms is None else terms + part
        for i in range(8):
            at = block * 8 + i
            sums = terms[i * 64 : (i + 1) * 64]
            fresh = pair_ref[at].astype(F32) + factor[:, at : at + 1] * sums
            fresh = fresh.astype(BF16)
            out_ref[at] = fresh
            bias = lax.dot_general(offset, normalize(fresh), NT, preferred_element_type=F32)
            hold[:, at : at + 1, :] = bias[:, None, :]
    for h in range(8):
        turned = hold[h].T
        quarters = [turned[q * 16 : (q + 1) * 16] for q in range(4)]
        block = jnp.concatenate(quarters, axis=1).astype(BF16)
        for reader in range(32):
            bias_ref[reader, h] = block


def ready_kernel(at_ref, *refs):
    x_ref, xc_ref, xx_ref, xxc_ref = refs[:4]
    tails = refs[4:8]
    wq_ref, wk_ref, wv_ref, wg_ref = refs[8:12]
    query_ref, key_ref, value_ref, gate_ref, mask_ref, ordered, columns = refs[12:]
    xl, core = at_ref[0], at_ref[1]

    @pl.when(pl.program_id(0) == 0)
    def _():
        columns[...] = jnp.zeros_like(columns)
        places = [(xl, core), (xl, 1 - core), (1 - xl, core), (1 - xl, 1 - core)]
        for tail_ref, (a, b) in zip(tails, places):
            for u in range(4):
                absent = ((tail_ref[u, :, :128].astype(F32) - 1.0) * -NEG).T
                columns[u, a, b, :, :16] = absent[:32]
        mask_ref[...] = columns[...].reshape(512, 128).astype(BF16)

    for t in range(STEP):
        rows = slice(t * 32, (t + 1) * 32)
        asked = normalize(x_ref[:, rows].reshape(128, 256))
        ordered[t, :, xl, core] = asked.reshape(4, 32, 256)
        ordered[t, :, xl, 1 - core] = normalize(xc_ref[:, rows])
        ordered[t, :, 1 - xl, core] = normalize(xx_ref[:, rows])
        ordered[t, :, 1 - xl, 1 - core] = normalize(xxc_ref[:, rows])
        keys = ordered[t].reshape(512, 256)
        query_ref[t] = (project(asked, wq_ref[...]) * (HEAD**-0.5 * LOG2E)).T.astype(BF16)
        key_ref[t] = project(keys, wk_ref[...]).astype(BF16)
        value_ref[t] = project(keys, wv_ref[...]).astype(BF16).T
        gate_ref[t] = jax.nn.sigmoid(project(asked, wg_ref[...])).T


def row_kernel(
    x_ref, query_ref, key_ref, value_ref, gate_ref, mask_ref, bias_ref, wo_ref, out_ref, held
):
    @pl.when(pl.program_id(0) == 0)
    def _():
        for a in range(8):
            for j in range(4):
                low = a * 64 + j * 16
                parts = [bias_ref[a, q, :, :, j * 32 : (j + 1) * 32] for q in range(4)]
                part = jnp.concatenate(parts, axis=2).astype(F32)
                held[:, low : low + 16] = part * LOG2E

    def finish(t, found):
        gated = (gate_ref[t] * found).astype(BF16)
        update = lax.dot_general(gated, wo_ref[...], TN, preferred_element_type=F32).astype(BF16)
        raw = x_ref[:, t * 32 : (t + 1) * 32].reshape(128, 256)
        out_ref[t] = (raw.astype(F32) + update.astype(F32)).astype(BF16)

    attentions = [
        Attention(
            query_ref[t],
            key_ref[t],
            value_ref[t],
            lambda h: held[h],
            mask_ref[...],
            pl.program_id(0) * STEP + t,
        )
        for t in range(STEP)
    ]
    run_pipelined(attentions, finish)


def column_kernel(x_ref, mask_ref, wq_ref, wk_ref, wv_ref, wg_ref, wo_ref, out_ref):
    gates, attentions = [], []
    for r in range(PICK):
        keys = normalize(x_ref[r])
        keys_t = keys.T

        def turned(weight_ref):
            return lax.dot_general(weight_ref[...], keys_t, TN, preferred_element_type=F32)

        query_t = (turned(wq_ref) * (HEAD**-0.5 * LOG2E)).astype(BF16)
        key = project(keys, wk_ref[...]).astype(BF16)
        value_t = turned(wv_ref).astype(BF16)
        gates.append(jax.nn.sigmoid(turned(wg_ref)))
        mask = mask_columns(mask_ref[pl.ds(pl.program_id(0) * PICK + r, 1), :])
        attentions.append(Attention(query_t, key, value_t, lambda h: None, mask, 0))

    def finish(r, found):
        gated = (gates[r] * found).astype(BF16)
        update = lax.dot_general(gated, wo_ref[...], TN, preferred_element_type=F32).astype(BF16)
        out_ref[r] = (x_ref[r].astype(F32) + update.astype(F32)).astype(BF16)

    run_pipelined(attentions, finish)


def in_hbm(array):
    return pltpu.with_memory_space_constraint(array, pltpu.HBM)


def spread(block, axes, count):
    wide = jnp.broadcast_to(block[None], (count,) + block.shape)
    return lax.all_to_all(wide, axes, split_axis=0, concat_axis=0, tiled=True)


def whole(shape):
    zeros = (0,) * len(shape)
    return pl.BlockSpec(shape, lambda *_: zeros)


def body(
    homolog_stack,
    entry_exists_flags,
    genuine_amino_flags,
    couplings_tensor,
    product_source_weights,
    product_target_weights,
    product_final_weights,
    coupling_logit_offset,
    horizontal_asking_weights,
    horizontal_lookup_weights,
    horizontal_content_weights,
    horizontal_sigmoid_weights,
    horizontal_final_weights,
    vertical_asking_weights,
    vertical_lookup_weights,
    vertical_content_weights,
    vertical_sigmoid_weights,
    vertical_final_weights,
):
    seq_at = lax.axis_index(SEQ)
    res_at = lax.axis_index(RES)
    xl_at = lax.axis_index("xl")
    core_at = lax.axis_index("core")
    mask = entry_exists_flags.astype(BF16)

    left, right = pl.pallas_call(
        factor_kernel,
        out_shape=[jax.ShapeDtypeStruct((48, 1152), BF16)] * 2,
        scratch_shapes=[pltpu.VMEM((1536, 128), F32)] * 2,
        compiler_params=pltpu.CompilerParams(vmem_limit_bytes=VMEM_LIMIT),
        name="factors",
    )(
        in_hbm(homolog_stack),
        in_hbm(entry_exists_flags.T),
        in_hbm(product_source_weights.T),
        in_hbm(product_target_weights.T),
    )
    swap = [
        ((a * 8 + b) * 2 + p, (b * 8 + a) * 2 + p)
        for a in range(8)
        for b in range(8)
        for p in range(2)
    ]
    pairs = [(0, 1), (1, 0)]
    right = lax.ppermute(right, ALL, swap)
    left_yh = lax.ppermute(left, "yh", pairs)
    right, left_yh = lax.optimization_barrier((right, left_yh))
    mine = spread(right, ("yl", "xh", "xl"), 8)
    left = jnp.stack([left, left_yh])
    lefts = [left] + [
        lax.ppermute(left, "z", [(z, z ^ k) for z in range(4)]) for k in range(1, 4)
    ]
    homolog_stack, mask, lefts[1] = lax.optimization_barrier((homolog_stack, mask, lefts[1]))
    tail = jnp.pad(mask.reshape(4, 12, 32), ((0, 0), (0, 4), (0, 224)))
    packed = jnp.concatenate([homolog_stack.reshape(4, 384, 256), tail], axis=1)
    team_at = lax.axis_index(TEAM)
    parts = []
    for k in range(4):
        part = lax.dynamic_index_in_dim(packed, team_at ^ k, 0, False)
        parts.append(lax.ppermute(part, TEAM, [(t, t ^ k) for t in range(4)]) if k else part)
    packed = jnp.stack(parts).reshape(2, 2, 400, 256)
    packed = jnp.where(lax.axis_index("yl") == 1, packed[::-1], packed)
    packed = jnp.where(lax.axis_index("xh") == 1, packed[:, ::-1], packed)
    packed = packed.reshape(4, 400, 256)
    final = product_final_weights.reshape(32, 8, 4, 128)
    final = jnp.transpose(final, (2, 1, 0, 3)).reshape(4, 256, 128)
    mine, final, packed, *lefts = lax.optimization_barrier((mine, final, packed, *lefts))
    other = lax.ppermute(mine, "core", pairs)
    packed_x = lax.ppermute(packed, "xl", pairs)
    packed_c = lax.ppermute(packed, "core", pairs)

    flags = genuine_amino_flags.astype(F32)
    row_flags = lax.dynamic_slice_in_dim(flags, res_at * 32, 32).reshape(1, 32)
    col_flags = lax.dynamic_slice_in_dim(flags, seq_at * 64, 64).reshape(64, 1)
    square = whole((256, 256))
    smem = pl.BlockSpec(memory_space=pltpu.SMEM)
    vmem = pl.BlockSpec(memory_space=pltpu.VMEM)
    pair_output, bias, col_mask = pl.pallas_call(
        pair_kernel,
        out_shape=(
            jax.ShapeDtypeStruct((32, 64, 128), BF16),
            jax.ShapeDtypeStruct((32, 8, 16, 128), BF16),
            jax.ShapeDtypeStruct((8, 384), F32),
        ),
        in_specs=[smem] + [vmem] * 11,
        scratch_shapes=[
            pltpu.VMEM((8, 48, 1152), BF16),
            pltpu.VMEM((2, 8, 48, 1152), BF16),
            pltpu.VMEM((8, 32, 64), F32),
        ],
        compiler_params=pltpu.CompilerParams(vmem_limit_bytes=VMEM_LIMIT),
        cost_estimate=pl.CostEstimate(
            flops=1000, transcendentals=0, bytes_accessed=1000
        ),
        name="pair",
    )(
        jnp.stack([seq_at, core_at]).astype(jnp.int32),
        *lefts,
        mine,
        other,
        couplings_tensor,
        row_flags,
        col_flags,
        final,
        coupling_logit_offset.T,
    )

    packed, packed_c, packed_x, _ = lax.optimization_barrier((packed, packed_c, packed_x, bias))
    packed_xc = lax.ppermute(packed_x, "core", pairs)
    pieces = [in_hbm(p) for p in (packed, packed_c, packed_x, packed_xc)]
    by_row = [(12, 256, 128), (12, 512, 256), (12, 256, 512), (12, 256, 128)]
    specs = [pl.BlockSpec((STEP,) + shape[1:], lambda t: (t, 0, 0)) for shape in by_row]
    rows_in = pl.pallas_call(
        ready_kernel,
        out_shape=[
            pltpu.HBM(shape, kind)
            for shape, kind in zip(by_row, (BF16, BF16, BF16, F32))
        ]
        + [pltpu.HBM((512, 128), BF16)],
        grid=(12 // STEP,),
        in_specs=[smem] + [pl.BlockSpec((4, STEP * 32, 256), lambda t: (0, t, 0))] * 4
        + [pl.BlockSpec((4, 16, 256), lambda t: (0, 24, 0))] * 4
        + [square] * 4,
        out_specs=specs + [whole((512, 128))],
        scratch_shapes=[
            pltpu.VMEM((STEP, 4, 2, 2, 32, 256), BF16),
            pltpu.VMEM((4, 2, 2, 32, 128), F32),
        ],
        compiler_params=pltpu.CompilerParams(vmem_limit_bytes=VMEM_LIMIT),
        cost_estimate=pl.CostEstimate(flops=1000, transcendentals=0, bytes_accessed=1000),
        name="ready",
    )(
        jnp.stack([xl_at, core_at]).astype(jnp.int32),
        *pieces,
        *pieces,
        in_hbm(horizontal_asking_weights),
        in_hbm(horizontal_lookup_weights),
        in_hbm(horizontal_content_weights),
        in_hbm(horizontal_sigmoid_weights),
    )
    bias = lax.all_to_all(bias, PLANE, split_axis=0, concat_axis=0, tiled=True)
    bias = bias.reshape(8, 4, 8, 16, 128)

    rows_in = [in_hbm(a) for a in rows_in]
    middle = pl.pallas_call(
        row_kernel,
        out_shape=jax.ShapeDtypeStruct((12, 128, 256), BF16),
        grid=(12 // STEP,),
        in_specs=[pl.BlockSpec((4, STEP * 32, 256), lambda t: (0, t, 0))]
        + specs
        + [whole((512, 128)), whole((8, 4, 8, 16, 128)), square],
        out_specs=pl.BlockSpec((STEP, 128, 256), lambda t: (t, 0, 0)),
        scratch_shapes=[pltpu.VMEM((8, 512, 128), F32)],
        compiler_params=pltpu.CompilerParams(vmem_limit_bytes=VMEM_LIMIT),
        cost_estimate=pl.CostEstimate(
            flops=8_000_000_000, transcendentals=6_300_000, bytes_accessed=12_000_000
        ),
        name="rows",
    )(pieces[0], *rows_in, bias, horizontal_final_weights)

    middle = jnp.transpose(middle.reshape(12, 4, 8, 4, 256), (2, 1, 0, 3, 4))
    middle = lax.all_to_all(
        middle.reshape(32, 12, 4, 256), PLANE, split_axis=0, concat_axis=0, tiled=True
    )
    middle = jnp.transpose(middle.reshape(384, 4, 256), (1, 0, 2))
    columns = pl.pallas_call(
        column_kernel,
        out_shape=jax.ShapeDtypeStruct((4, 384, 256), BF16),
        grid=(4 // PICK,),
        in_specs=[
            pl.BlockSpec((PICK, 384, 256), lambda r: (r, 0, 0)),
            whole((8, 384)),
            square,
            square,
            square,
            square,
            square,
        ],
        out_specs=pl.BlockSpec((PICK, 384, 256), lambda r: (r, 0, 0)),
        compiler_params=pltpu.CompilerParams(vmem_limit_bytes=VMEM_LIMIT),
        cost_estimate=pl.CostEstimate(
            flops=8_000_000_000, transcendentals=4_700_000, bytes_accessed=2_000_000
        ),
        name="columns",
    )(
        middle,
        col_mask,
        vertical_asking_weights,
        vertical_lookup_weights,
        vertical_content_weights,
        vertical_sigmoid_weights,
        vertical_final_weights,
    )
    columns = jnp.transpose(columns.reshape(4, 8, 48, 256), (1, 0, 2, 3))
    columns = lax.all_to_all(columns, SEQ, split_axis=0, concat_axis=0, tiled=True)
    alignment_output = jnp.transpose(columns.reshape(32, 48, 256), (1, 0, 2))
    return alignment_output, pair_output


def solution(mesh):
    parts = Mesh(mesh.devices.reshape(2, 4, 2, 2, 2, 2), ALL)
    stack = P(SEQ, RES, None)
    in_specs = (stack, P(SEQ, RES), P(), P(RES, SEQ, None)) + (P(),) * 14
    out_specs = (stack, P(RES, SEQ, None))
    return jax.shard_map(body, mesh=parts, in_specs=in_specs, out_specs=out_specs, check_vma=False)
```

time: 562 us -> 150 us (0.27); the launches traced: 552 us -> 149 us
  waiting for transfers between devices: 196 us -> 33.2 us
  local copies, waits for them, and re-layouts: 108 us -> 4.26 us
  matrix products: 88.2 us -> 0 us
  other arithmetic: 52.9 us -> 2.26 us
  Pallas kernels: 0 us -> 43 us
  blocking collectives: 70.5 us -> 35.6 us
  starting transfers between devices: 11.3 us -> 29.8 us
  between operations: 16.4 us -> 0.94 us
  loops' own time: 8.38 us -> 0 us
    reduce_scatter x1 -> x0, waiting for transfers between devices: 161 us -> none  [body(): lax.psum_scatter(partial_terms, 'seq', scatter_dimension=1, tiled=True)]
    dot_general x29 -> x0, matrix products: 86.6 us -> none  [the longest x4 25.2 us: body(): jnp.einsum('shij,sjhd->shid', expo, value_block.astype(jnp.float32))]
    slice x11 -> x0, local copies, waits for them, and re-layouts: 55.9 us -> none  [the longest x5 28 us: body(): value_piece[:, low:low + sub]]
    all_gather x2 -> x0, blocking collectives: 55.7 us -> none  [the longest x1 36.3 us: body(): lax.all_gather(bias_heads(pair_output, coupling_logit_offset), 'seq', axi...]
    pallas_call x0 -> x5, Pallas kernels: none -> 43 us  [the longest x1 14.9 us: body(): pl.pallas_call(row_kernel, out_shape=jax.ShapeDtypeStruct((12, 128, 256),...]
    reduce_sum x11 -> x0, other arithmetic: 39.2 us -> none  [the longest x2 29.5 us: body(): totals = totals * correction + jnp.sum(expo, axis=-1)]
    ppermute x0 -> x12, waiting for transfers between devices: none -> 28.4 us  [the longest x1 12.6 us: body(): right = lax.ppermute(right, ALL, swap)]
    reshape x7 -> x9, local copies, waits for them, and re-layouts: 23.8 us -> 1.84 us  [the longest x1 1.12 us: body(): alignment_output = jnp.transpose(columns.reshape(32, 48, 256), (1, 0, 2))]
  transfers between devices with their start and end apart: 7 -> 14, of which waited for: 4 -> 7; matrix products, arithmetic and copies ran while one was open for 37% -> 2% of each run, Pallas kernels for 0% -> 11%
where the time goes in v1:
time: 150 us; the launch traced here: 149 us
  Pallas kernels  43 us (29%)
  blocking collectives  35.6 us (24%)
  waiting for transfers between devices  33.2 us (22%)
  starting transfers between devices  29.8 us (20%)
  local copies, waits for them, and re-layouts  4.26 us (3%)
  other arithmetic  2.26 us (2%)
    all_to_all x1, blocking collectives, body(): lax.all_to_all(middle.reshape(32, 12, 4, 256), PLANE, split_axis=0, conca...  19.7 us
    all_to_all x1, blocking collectives, body(): lax.all_to_all(columns, SEQ, split_axis=0, concat_axis=0, tiled=True)  15.9 us
    pallas_call x1, Pallas kernels, body(): pl.pallas_call(row_kernel, out_shape=jax.ShapeDtypeStruct((12, 128, 256),...  14.9 us
    ppermute x1, waiting for transfers between devices, body(): right = lax.ppermute(right, ALL, swap)  12.6 us
    ppermute x3, waiting for transfers between devices, body(): lax.ppermute(left, 'z', [(z, z ^ k) for z in range(4)])  11.2 us
    all_to_all x1, starting transfers between devices, body(): bias = lax.all_to_all(bias, PLANE, split_axis=0, concat_axis=0, tiled=True)  8.61 us
    pallas_call x1, Pallas kernels, body(): pl.pallas_call(pair_kernel, out_shape=(jax.ShapeDtypeStruct((32, 64, 128)...  8.56 us
    pallas_call x1, Pallas kernels, body(): pl.pallas_call(ready_kernel, out_shape=[pltpu.HBM(shape, kind) for shape,...  8.4 us
  transfers between devices with their start and end apart: 14, of which 7 were waited for; matrix products, arithmetic and copies ran while one was open for 2% of the time, Pallas kernels for 11%

profile of v1, /device:TPU:8, one launch (start us, length us, event | category | flops | bytes accessed | tf_op | source)
XLA Modules:
  0.0 149.0 jit_solution(16005592082606022570)
XLA Ops:
  0.6 3.2 %factors.1 = (bf16[48,1152]{1,0:T(8,128)(2,1)S(1)}, bf16[48,1152]{1,0:T(8,128)(2,1)S(1)}) custom-call(bf16[48,32,256]{2,1,0:T(8,128)(2,1)} %x_ref.1, s32[32,48]{1,0:T(8,128)} %bitcast.68, bf16[32,256]{1,0:T(8,128)(2,1)} %bitcast.69, bf16[32,256]{1,0:T(8,128)(2,1)} %bitcast.70), custom_call_target="tpu_custom_call" | custom-call | tf_op jit(solution)/shard_map/factors/pallas_call | solution.py:312
  3.9 3.5 %collective-permute-start = (bf16[48,1152]{1,0:T(8,128)(2,1)S(1)}, bf16[48,1152]{1,0:T(8,128)(2,1)S(1)}, u32[]{:S(2)}, u32[]{:S(2)}) collective-permute-start(bf16[48,1152]{1,0:T(8,128)(2,1)S(1)} %get-tuple-element.27), channel_id=1, source_target_pairs={{0,0},{1,1},{2,16},{3,17},{4,32},{5,33},{6,48},{7,49},{8,64},{9,65... | collective-permute-start | bytes 331784 | tf_op jit(solution)/shard_map/ppermute | solution.py:331
  7.4 0.1 collective-permute-start.1
  7.5 12.6 %collective-permute-done = bf16[48,1152]{1,0:T(8,128)(2,1)S(1)} collective-permute-done((bf16[48,1152]{1,0:T(8,128)(2,1)S(1)}, bf16[48,1152]{1,0:T(8,128)(2,1)S(1)}, u32[]{:S(2)}, u32[]{:S(2)}) %collective-permute-start) | collective-permute-done | bytes 110624 | tf_op jit(solution)/shard_map/ppermute | solution.py:331
  20.1 0.1 collective-permute-start.2
  20.2 0.7 convert_element_type.8
  20.9 5.2 %collective-permute-done.2.refs_1_ = bf16[2,48,1152]{2,1,0:T(8,128)(2,1)S(1)} collective-permute-done((bf16[2,48,1152]{2,1,0:T(8,128)(2,1)S(1)}, bf16[2,48,1152]{2,1,0:T(8,128)(2,1)S(1)}, u32[]{:S(2)}, u32[]{:S(2)}) %collective-permute-start.2) | collective-permute-done | bytes 221216 | tf_op jit(solution)/shard_map/ppermute | solution.py:337
  26.1 0.1 copy.32
  26.2 0.1 fusion.1
  26.3 0.1 constant_dynamic-slice_fusion
  26.4 0.0 copy-start.10
  26.4 0.1 collective-permute-start.5
  26.5 3.4 %collective-permute-start.4 = (bf16[400,256]{1,0:T(8,128)(2,1)S(1)}, bf16[400,256]{1,0:T(8,128)(2,1)S(1)}, u32[]{:S(2)}, u32[]{:S(2)}) collective-permute-start(bf16[400,256]{1,0:T(8,128)(2,1)S(1)} %get-tuple-element.54), channel_id=1, source_target_pairs={{0,8},{4,12},{8,0},{12,4},{1,9},{5,13},{9,1},{13,5},{2,10},{6,14},... | collective-permute-start | bytes 614408 | tf_op jit(solution)/shard_map/ppermute | solution.py:346
  29.9 1.6 %collective-permute-start.3 = (bf16[400,256]{1,0:T(8,128)(2,1)S(1)}, bf16[400,256]{1,0:T(8,128)(2,1)S(1)}, u32[]{:S(2)}, u32[]{:S(2)}) collective-permute-start(bf16[400,256]{1,0:T(8,128)(2,1)S(1)} %get-tuple-element.55), channel_id=1, source_target_pairs={{0,4},{4,0},{8,12},{12,8},{1,5},{5,1},{9,13},{13,9},{2,6},{6,2},{1... | collective-permute-start | bytes 614408 | tf_op jit(solution)/shard_map/ppermute | solution.py:346
  31.4 1.0 broadcast_in_dim.2
  32.4 7.0 %all-to-all-start = ((bf16[8,48,1152]{2,1,0:T(8,128)(2,1)}), bf16[8,48,1152]{2,1,0:T(8,128)(2,1)S(1)}, u32[]{:S(2)}, u32[]{:S(2)}) async-start(bf16[8,48,1152]{2,1,0:T(8,128)(2,1)} %broadcast_in_dim.2), calls=%async_computation | async-start | bytes 1769472 | tf_op jit(solution)/shard_map/all_to_all | solution.py:278
  39.4 0.1 copy.31
  39.5 3.3 %collective-permute-start.7 = (bf16[2,48,1152]{2,1,0:T(8,128)(2,1)S(1)}, bf16[2,48,1152]{2,1,0:T(8,128)(2,1)S(1)}, u32[]{:S(2)}, u32[]{:S(2)}) collective-permute-start(bf16[2,48,1152]{2,1,0:T(8,128)(2,1)S(1)} %pad_maximum_fusion.1.refs_0_), channel_id=1, source_target_pairs={{0,48},{16,32},{32,16},{48,0},{1,49},{17,33},{33,17},{49,1},{2,50}... | collective-permute-start | bytes 663560 | tf_op jit(solution)/shard_map/ppermute | solution.py:337
  42.8 0.5 collective-permute-start.6
  43.3 0.1 pad_maximum_fusion
  43.4 0.0 copy-start.11
  43.5 0.1 reverse_select_fusion.1
  43.6 1.0 reverse_select_fusion
  44.7 6.0 %collective-permute-done.7.refs_3_ = bf16[2,48,1152]{2,1,0:T(8,128)(2,1)S(1)} collective-permute-done((bf16[2,48,1152]{2,1,0:T(8,128)(2,1)S(1)}, bf16[2,48,1152]{2,1,0:T(8,128)(2,1)S(1)}, u32[]{:S(2)}, u32[]{:S(2)}) %collective-permute-start.7) | collective-permute-done | bytes 221216 | tf_op jit(solution)/shard_map/ppermute | solution.py:337
  50.7 1.5 %collective-permute-start.9 = (bf16[4,400,256]{2,1,0:T(8,128)(2,1)}, bf16[4,400,256]{2,1,0:T(8,128)(2,1)}, u32[]{:S(2)}, u32[]{:S(2)}) collective-permute-start(bf16[4,400,256]{2,1,0:T(8,128)(2,1)} %bitcast.50), channel_id=1, source_target_pairs={{0,2},{2,0},{1,3},{3,1},{4,6},{6,4},{5,7},{7,5},{8,10},{10,8},{9,1... | collective-permute-start | bytes 2457608 | tf_op jit(solution)/shard_map/ppermute | solution.py:355
  52.2 0.2 collective-permute-start.8
  52.4 0.1 dynamic-slice_bitcast_fusion.3
  52.5 0.1 copy.33.refs_8_
  52.6 0.1 dynamic-slice_bitcast_fusion.4.refs_7_
  52.7 0.1 pad_add_fusion.at_ref
  52.7 0.4 collective-permute-done.10.refs_5_
  53.1 8.6 %pair.1 = (bf16[32,64,128]{2,1,0:T(8,128)(2,1)}, bf16[32,8,16,128]{3,2,1,0:T(8,128)(2,1)}, f32[8,384]{1,0:T(8,128)S(1)}) custom-call(s32[2]{0:T(128)S(1)} %pad_add_fusion.at_ref, bf16[2,48,1152]{2,1,0:T(8,128)(2,1)S(1)} %pad_maximum_fusion.1.refs_0_, bf16[2,48,1152]{2,1,0:T(8,128)(2,1)S(1)} %collective-permute-done.2.refs_1_, ...), custom_call_target="tpu_custom_call" | custom-call | flops 1000 | bytes 1000 | tf_op jit(solution)/shard_map/pair/pallas_call | solution.py:364
  61.7 8.6 %all-to-all-start.1 = ((bf16[32,8,16,128]{3,2,1,0:T(8,128)(2,1)}), bf16[32,8,16,128]{3,2,1,0:T(8,128)(2,1)S(1)}, u32[]{:S(2)}, u32[]{:S(2)}) async-start(bf16[32,8,16,128]{3,2,1,0:T(8,128)(2,1)} %get-tuple-element.41), calls=%async_computation.1 | async-start | bytes 2097152 | tf_op jit(solution)/shard_map/all_to_all | solution.py:427
  70.3 1.7 %collective-permute-done.9.refs_2_.refs_6_ = bf16[4,400,256]{2,1,0:T(8,128)(2,1)} collective-permute-done((bf16[4,400,256]{2,1,0:T(8,128)(2,1)}, bf16[4,400,256]{2,1,0:T(8,128)(2,1)}, u32[]{:S(2)}, u32[]{:S(2)}) %collective-permute-start.9) | collective-permute-done | bytes 819232 | tf_op jit(solution)/shard_map/ppermute | solution.py:355
  72.0 0.1 pad_add_fusion.1.at_ref
  72.1 2.5 %collective-permute-done.11.refs_3_.refs_7_ = bf16[4,400,256]{2,1,0:T(8,128)(2,1)S(1)} collective-permute-done((bf16[4,400,256]{2,1,0:T(8,128)(2,1)}, bf16[4,400,256]{2,1,0:T(8,128)(2,1)S(1)}, u32[]{:S(2)}, u32[]{:S(2)}) %collective-permute-start.11) | collective-permute-done | bytes 819232 | tf_op jit(solution)/shard_map/ppermute | solution.py:395
  74.6 0.9 copy-done.8
  75.5 8.4 %ready.1 = (bf16[12,256,128]{2,1,0:T(8,128)(2,1)}, bf16[12,512,256]{2,1,0:T(8,128)(2,1)}, bf16[12,256,512]{2,1,0:T(8,128)(2,1)}, f32[12,256,128]{2,1,0:T(8,128)}, bf16[512,128]{1,0:T(8,128)(2,1)}) custom-call(s32[2]{0:T(128)S(1)} %pad_add_fusion.1.at_ref, bf16[4,400,256]{2,1,0:T(8,128)(2,1)} %bitcast.52, ...), custom_call_target="tpu_custom_call" | custom-call | flops 1000 | bytes 1000 | tf_op jit(solution)/shard_map/ready/pallas_call | solution.py:399
  83.9 4.8 %all-to-all-done.1 = bf16[32,8,16,128]{3,2,1,0:T(8,128)(2,1)S(1)} async-done(((bf16[32,8,16,128]{3,2,1,0:T(8,128)(2,1)}), bf16[32,8,16,128]{3,2,1,0:T(8,128)(2,1)S(1)}, u32[]{:S(2)}, u32[]{:S(2)}) %all-to-all-start.1) | async-done | bytes 1048608 | tf_op jit(solution)/shard_map/all_to_all | solution.py:427
  88.7 14.9 %rows.1 = bf16[12,128,256]{2,1,0:T(8,128)(2,1)S(1)} custom-call(bf16[4,400,256]{2,1,0:T(8,128)(2,1)} %bitcast.54, bf16[12,256,128]{2,1,0:T(8,128)(2,1)} %get-tuple-element.45.query_ref, bf16[12,512,256]{2,1,0:T(8,128)(2,1)} %get-tuple-element.46.key_ref, bf16[12,256,512]{2,1,0:T(8,128)(2,1)} %get-tuple-element.47.value_ref, ...), custom_call_target="tpu_custom_call" | custom-call | flops 8000000000 | bytes 12000000 | tf_op jit(solution)/shard_map/rows/pallas_call | solution.py:431
  103.6 0.2 reshape.56
  103.8 0.3 copy.34
  104.1 19.7 %all_to_all.20 = bf16[32,12,4,256]{3,2,1,0:T(4,128)(2,1)S(1)} all-to-all(bf16[32,12,4,256]{3,2,1,0:T(4,128)(2,1)S(1)} %bitcast.58), channel_id=1, replica_groups=mesh['yh'=2,'z'=4,'yl'=2,'xh'=2,'xl'=2,'core'=2] {'yh','z','yl','xh'}, dimensions={0} | all-to-all | bytes 1572864 | tf_op jit(solution)/shard_map/all_to_all | solution.py:448
  123.8 0.1 copy.43
  124.0 7.9 %columns.1 = bf16[4,384,256]{2,1,0:T(8,128)(2,1)S(1)} custom-call(bf16[4,384,256]{2,1,0:T(8,128)(2,1)S(1)} %bitcast.46, f32[8,384]{1,0:T(8,128)S(1)} %get-tuple-element.50.mask_ref, bf16[256,256]{1,0:T(8,128)(2,1)S(1)} %copy-done.3, bf16[256,256]{1,0:T(8,128)(2,1)S(1)} %copy-done.4, bf16[256,256]{1,0:T(8,128)(2,1)S(1)} %copy-done.5, ...), custom_call_target="tpu_custom_call" | custom-call | flops 8000000000 | bytes 2000000 | tf_op jit(solution)/shard_map/columns/pallas_call | solution.py:452
  131.9 0.1 copy.42
  132.0 15.9 %all_to_all.21 = bf16[8,4,48,256]{3,2,1,0:T(8,128)(2,1)S(1)} all-to-all(bf16[8,4,48,256]{3,2,1,0:T(8,128)(2,1)S(1)} %bitcast.60), channel_id=1, replica_groups=mesh['yh'=2,'z'=4,'yl'=2,'xh'=2,'xl'=2,'core'=2] {'yh','z'}, dimensions={0} | all-to-all | bytes 1572864 | tf_op jit(solution)/shard_map/all_to_all | solution.py:481
  147.9 1.1 copy.41
  (33 shorter events, 0.1 us)
Async XLA Ops:
  0.6 25.6 %copy-start.9 = (bf16[48,32,256]{2,1,0:T(8,128)(2,1)S(1)}, bf16[48,32,256]{2,1,0:T(8,128)(2,1)}, u32[]{:S(2)}) copy-start(bf16[48,32,256]{2,1,0:T(8,128)(2,1)} %x_ref.1) | copy-start | bytes 2359300
  3.9 16.2 %collective-permute-start = (bf16[48,1152]{1,0:T(8,128)(2,1)S(1)}, bf16[48,1152]{1,0:T(8,128)(2,1)S(1)}, u32[]{:S(2)}, u32[]{:S(2)}) collective-permute-start(bf16[48,1152]{1,0:T(8,128)(2,1)S(1)} %get-tuple-element.27), channel_id=1, source_target_pairs={{0,0},{1,1},{2,16},{3,17},{4,32},{5,33},{6,48},{7,49},{8,64},{9,65... | collective-permute-start | bytes 331784 | tf_op jit(solution)/shard_map/ppermute | solution.py:331
  7.4 12.7 %collective-permute-start.1 = (bf16[48,1152]{1,0:T(8,128)(2,1)S(1)}, bf16[48,1152]{1,0:T(8,128)(2,1)S(1)}, u32[]{:S(2)}, u32[]{:S(2)}) collective-permute-start(bf16[48,1152]{1,0:T(8,128)(2,1)S(1)} %get-tuple-element.28), channel_id=1, source_target_pairs={{0,64},{64,0},{1,65},{65,1},{2,66},{66,2},{3,67},{67,3},{4,68},{68... | collective-permute-start | bytes 331784 | tf_op jit(solution)/shard_map/ppermute | solution.py:332
  20.1 6.0 %collective-permute-start.2 = (bf16[2,48,1152]{2,1,0:T(8,128)(2,1)S(1)}, bf16[2,48,1152]{2,1,0:T(8,128)(2,1)S(1)}, u32[]{:S(2)}, u32[]{:S(2)}) collective-permute-start(bf16[2,48,1152]{2,1,0:T(8,128)(2,1)S(1)} %pad_maximum_fusion.1.refs_0_), channel_id=1, source_target_pairs={{0,16},{16,0},{32,48},{48,32},{1,17},{17,1},{33,49},{49,33},{2,18}... | collective-permute-start | bytes 663560 | tf_op jit(solution)/shard_map/ppermute | solution.py:337
  26.4 13.0 %copy-start.10 = (bf16[1024,128]{1,0:T(8,128)(2,1)S(1)}, bf16[1024,128]{1,0:T(8,128)(2,1)}, u32[]{:S(2)}) copy-start(bf16[1024,128]{1,0:T(8,128)(2,1)} %param.24) | copy-start | bytes 786436
  26.4 16.9 %collective-permute-start.5 = (bf16[400,256]{1,0:T(8,128)(2,1)S(1)}, bf16[400,256]{1,0:T(8,128)(2,1)S(1)}, u32[]{:S(2)}, u32[]{:S(2)}) collective-permute-start(bf16[400,256]{1,0:T(8,128)(2,1)S(1)} %get-tuple-element.53), channel_id=1, source_target_pairs={{0,12},{4,8},{8,4},{12,0},{1,13},{5,9},{9,5},{13,1},{2,14},{6,10},... | collective-permute-start | bytes 614408 | tf_op jit(solution)/shard_map/ppermute | solution.py:346
  26.5 16.8 %collective-permute-start.4 = (bf16[400,256]{1,0:T(8,128)(2,1)S(1)}, bf16[400,256]{1,0:T(8,128)(2,1)S(1)}, u32[]{:S(2)}, u32[]{:S(2)}) collective-permute-start(bf16[400,256]{1,0:T(8,128)(2,1)S(1)} %get-tuple-element.54), channel_id=1, source_target_pairs={{0,8},{4,12},{8,0},{12,4},{1,9},{5,13},{9,1},{13,5},{2,10},{6,14},... | collective-permute-start | bytes 614408 | tf_op jit(solution)/shard_map/ppermute | solution.py:346
  29.9 13.4 %collective-permute-start.3 = (bf16[400,256]{1,0:T(8,128)(2,1)S(1)}, bf16[400,256]{1,0:T(8,128)(2,1)S(1)}, u32[]{:S(2)}, u32[]{:S(2)}) collective-permute-start(bf16[400,256]{1,0:T(8,128)(2,1)S(1)} %get-tuple-element.55), channel_id=1, source_target_pairs={{0,4},{4,0},{8,12},{12,8},{1,5},{5,1},{9,13},{13,9},{2,6},{6,2},{1... | collective-permute-start | bytes 614408 | tf_op jit(solution)/shard_map/ppermute | solution.py:346
  32.4 18.3 %all-to-all-start = ((bf16[8,48,1152]{2,1,0:T(8,128)(2,1)}), bf16[8,48,1152]{2,1,0:T(8,128)(2,1)S(1)}, u32[]{:S(2)}, u32[]{:S(2)}) async-start(bf16[8,48,1152]{2,1,0:T(8,128)(2,1)} %broadcast_in_dim.2), calls=%async_computation | async-start | bytes 1769472 | tf_op jit(solution)/shard_map/all_to_all | solution.py:278
  39.5 11.2 %collective-permute-start.7 = (bf16[2,48,1152]{2,1,0:T(8,128)(2,1)S(1)}, bf16[2,48,1152]{2,1,0:T(8,128)(2,1)S(1)}, u32[]{:S(2)}, u32[]{:S(2)}) collective-permute-start(bf16[2,48,1152]{2,1,0:T(8,128)(2,1)S(1)} %pad_maximum_fusion.1.refs_0_), channel_id=1, source_target_pairs={{0,48},{16,32},{32,16},{48,0},{1,49},{17,33},{33,17},{49,1},{2,50}... | collective-permute-start | bytes 663560 | tf_op jit(solution)/shard_map/ppermute | solution.py:337
  42.8 7.9 %collective-permute-start.6 = (bf16[2,48,1152]{2,1,0:T(8,128)(2,1)S(1)}, bf16[2,48,1152]{2,1,0:T(8,128)(2,1)S(1)}, u32[]{:S(2)}, u32[]{:S(2)}) collective-permute-start(bf16[2,48,1152]{2,1,0:T(8,128)(2,1)S(1)} %pad_maximum_fusion.1.refs_0_), channel_id=1, source_target_pairs={{0,32},{16,48},{32,0},{48,16},{1,33},{17,49},{33,1},{49,17},{2,34}... | collective-permute-start | bytes 663560 | tf_op jit(solution)/shard_map/ppermute | solution.py:337
  43.4 9.0 %copy-start.11 = (s32[512]{0:T(512)S(1)}, s32[512]{0:T(512)}, u32[]{:S(2)}) copy-start(s32[512]{0:T(512)} %param.20) | copy-start | bytes 6148
  43.4 9.7 %copy-start = (bf16[32,64,128]{2,1,0:T(8,128)(2,1)S(1)}, bf16[32,64,128]{2,1,0:T(8,128)(2,1)}, u32[]{:S(2)}) copy-start(bf16[32,64,128]{2,1,0:T(8,128)(2,1)} %refs_6_.1) | copy-start | bytes 1572868
  43.5 9.7 %copy-start.1 = (bf16[128,8]{0,1:T(8,128)(2,1)S(1)}, bf16[128,8]{0,1:T(8,128)(2,1)}, u32[]{:S(2)}) copy-start(bf16[128,8]{0,1:T(8,128)(2,1)} %param.25) | copy-start | bytes 6148
  50.7 2.4 %collective-permute-start.10 = (bf16[8,48,1152]{2,1,0:T(8,128)(2,1)S(1)}, bf16[8,48,1152]{2,1,0:T(8,128)(2,1)S(1)}, u32[]{:S(2)}, u32[]{:S(2)}) collective-permute-start(bf16[8,48,1152]{2,1,0:T(8,128)(2,1)S(1)} %all-to-all-done.refs_4_), channel_id=1, source_target_pairs={{0,1},{1,0},{2,3},{3,2},{4,5},{5,4},{6,7},{7,6},{8,9},{9,8},{10,11... | collective-permute-start | bytes 2654216 | tf_op jit(solution)/shard_map/ppermute | solution.py:354
  50.7 21.3 %collective-permute-start.9 = (bf16[4,400,256]{2,1,0:T(8,128)(2,1)}, bf16[4,400,256]{2,1,0:T(8,128)(2,1)}, u32[]{:S(2)}, u32[]{:S(2)}) collective-permute-start(bf16[4,400,256]{2,1,0:T(8,128)(2,1)} %bitcast.50), channel_id=1, source_target_pairs={{0,2},{2,0},{1,3},{3,1},{4,6},{6,4},{5,7},{7,5},{8,10},{10,8},{9,1... | collective-permute-start | bytes 2457608 | tf_op jit(solution)/shard_map/ppermute | solution.py:355
  52.2 19.8 %collective-permute-start.8 = (bf16[4,400,256]{2,1,0:T(8,128)(2,1)}, bf16[4,400,256]{2,1,0:T(8,128)(2,1)}, u32[]{:S(2)}, u32[]{:S(2)}) collective-permute-start(bf16[4,400,256]{2,1,0:T(8,128)(2,1)} %bitcast.51), channel_id=1, source_target_pairs={{0,1},{1,0},{2,3},{3,2},{4,5},{5,4},{6,7},{7,6},{8,9},{9,8},{10,11... | collective-permute-start | bytes 2457608 | tf_op jit(solution)/shard_map/ppermute | solution.py:356
  61.7 27.0 %all-to-all-start.1 = ((bf16[32,8,16,128]{3,2,1,0:T(8,128)(2,1)}), bf16[32,8,16,128]{3,2,1,0:T(8,128)(2,1)S(1)}, u32[]{:S(2)}, u32[]{:S(2)}) async-start(bf16[32,8,16,128]{3,2,1,0:T(8,128)(2,1)} %get-tuple-element.41), calls=%async_computation.1 | async-start | bytes 2097152 | tf_op jit(solution)/shard_map/all_to_all | solution.py:427
  72.0 2.5 %collective-permute-start.11 = (bf16[4,400,256]{2,1,0:T(8,128)(2,1)}, bf16[4,400,256]{2,1,0:T(8,128)(2,1)S(1)}, u32[]{:S(2)}, u32[]{:S(2)}) collective-permute-start(bf16[4,400,256]{2,1,0:T(8,128)(2,1)} %collective-permute-done.9.refs_2_.refs_6_), channel_id=1, source_target_pairs={{0,1},{1,0},{2,3},{3,2},{4,5},{5,4},{6,7},{7,6},{8,9},{9,8},{10,11... | collective-permute-start | bytes 2457608 | tf_op jit(solution)/shard_map/ppermute | solution.py:395
  72.1 16.6 %copy-start.2 = (bf16[256,256]{1,0:T(8,128)(2,1)S(1)}, bf16[256,256]{1,0:T(8,128)(2,1)}, u32[]{:S(2)}) copy-start(bf16[256,256]{1,0:T(8,128)(2,1)} %wo_ref.2) | copy-start | bytes 393220
  74.6 0.9 copy-start.8
  104.1 19.9 %copy-start.3 = (bf16[256,256]{1,0:T(8,128)(2,1)S(1)}, bf16[256,256]{1,0:T(8,128)(2,1)}, u32[]{:S(2)}) copy-start(bf16[256,256]{1,0:T(8,128)(2,1)} %wq_ref.1) | copy-start | bytes 393220
  104.1 19.9 %copy-start.4 = (bf16[256,256]{1,0:T(8,128)(2,1)S(1)}, bf16[256,256]{1,0:T(8,128)(2,1)}, u32[]{:S(2)}) copy-start(bf16[256,256]{1,0:T(8,128)(2,1)} %wk_ref.1) | copy-start | bytes 393220
  104.1 19.9 %copy-start.5 = (bf16[256,256]{1,0:T(8,128)(2,1)S(1)}, bf16[256,256]{1,0:T(8,128)(2,1)}, u32[]{:S(2)}) copy-start(bf16[256,256]{1,0:T(8,128)(2,1)} %wv_ref.1) | copy-start | bytes 393220
  104.1 19.9 %copy-start.6 = (bf16[256,256]{1,0:T(8,128)(2,1)S(1)}, bf16[256,256]{1,0:T(8,128)(2,1)}, u32[]{:S(2)}) copy-start(bf16[256,256]{1,0:T(8,128)(2,1)} %wg_ref.1) | copy-start | bytes 393220
  104.1 19.9 %copy-start.7 = (bf16[256,256]{1,0:T(8,128)(2,1)S(1)}, bf16[256,256]{1,0:T(8,128)(2,1)}, u32[]{:S(2)}) copy-start(bf16[256,256]{1,0:T(8,128)(2,1)} %wo_ref.3) | copy-start | bytes 393220

commit v2 on v1

--- a/solution.py
+++ b/solution.py
@@ -38,28 +38,31 @@
 
 
 class Attention:
-    def __init__(self, query_t, key, value_t, bias_of, mask_lanes, lane):
+    def __init__(self, query_t, key, value_t, bias_of, mask_lanes, lane, heads):
         self.query_t, self.key, self.value_t = query_t, key, value_t
         self.bias_of, self.mask_lanes, self.lane = bias_of, mask_lanes, lane
+        self.heads = heads
+        self.units = HEADS // heads
         self.count = query_t.shape[1]
         self.found = []
 
-    def score(self, pair):
-        part = slice(pair // 2 * 128, pair // 2 * 128 + 128)
+    def score(self, unit):
+        first = unit * self.heads
+        part = slice(first // 4 * 128, first // 4 * 128 + 128)
         own = self.query_t[part]
         row = lax.broadcasted_iota(jnp.int32, own.shape, 0)
         one = jnp.where(row == self.lane, 1.0, 0.0).astype(BF16)
         stacked = []
-        for h in range(2):
-            mine = row // HEAD == pair % 2 * 2 + h
+        for h in range(self.heads):
+            mine = row // HEAD == first % 4 + h
             stacked.append(jnp.concatenate([jnp.where(mine, own, jnp.zeros_like(own)), one], axis=0))
         keys = jnp.concatenate([self.key[:, part], self.mask_lanes], axis=1)
         return project(keys, jnp.concatenate(stacked, axis=1))
 
-    def weigh(self, pair, scores):
+    def weigh(self, unit, scores):
         weights = []
-        for h in range(2):
-            extra = self.bias_of(pair * 2 + h)
+        for h in range(self.heads):
+            extra = self.bias_of(unit * self.heads + h)
             for low in range(0, self.count, 128):
                 tile = scores[:, h * self.count + low : h * self.count + low + 128]
                 if extra is not None:
@@ -67,27 +70,28 @@
                 weights.append(jnp.exp2(tile - jnp.max(tile, axis=0, keepdims=True)).astype(BF16))
         return jnp.concatenate(weights, axis=1)
 
-    def mix(self, pair, weights):
+    def mix(self, unit, weights):
+        size = self.heads * HEAD
         ones = jnp.ones((16, self.value_t.shape[1]), BF16)
-        values = jnp.concatenate([self.value_t[pair * 64 : pair * 64 + 64], ones], axis=0)
+        values = jnp.concatenate([self.value_t[unit * size : (unit + 1) * size], ones], axis=0)
         mixed = project(values, weights)
-        for h in range(2):
+        for h in range(self.heads):
             cols = slice(h * self.count, (h + 1) * self.count)
-            self.found.append(mixed[h * HEAD : (h + 1) * HEAD, cols] / mixed[64:65, cols])
+            self.found.append(mixed[h * HEAD : (h + 1) * HEAD, cols] / mixed[size : size + 1, cols])
 
     def result(self):
         return jnp.concatenate(self.found, axis=0)
 
 
 def run_pipelined(attentions, finish):
-    units = [(a, pair) for a in attentions for pair in range(4)]
+    units = [(a, unit) for a in attentions for unit in range(a.units)]
     ahead = units[0][0].score(0)
-    for place, (attention, pair) in enumerate(units):
+    for place, (attention, unit) in enumerate(units):
         scores = ahead
         if place + 1 < len(units):
             ahead = units[place + 1][0].score(units[place + 1][1])
-        attention.mix(pair, attention.weigh(pair, scores))
-        if pair == 3:
+        attention.mix(unit, attention.weigh(unit, scores))
+        if unit == attention.units - 1:
             finish(attentions.index(attention), attention.result())
 
 
@@ -97,7 +101,9 @@
     return jnp.where(top, jnp.broadcast_to(mask_row, shape), 0.0).astype(BF16).T
 
 
-def factor_kernel(x_ref, mask_ref, source_ref, target_ref, left_ref, right_ref, lefts, rights):
+def factor_kernel(
+    x_ref, mask_ref, source_ref, target_ref, left_ref, right_ref, packed_ref, lefts, rights
+):
     ln = normalize(x_ref[...].reshape(1536, 256))
     mask = mask_ref[...].astype(F32).T
     lefts[:, :32] = lax.dot_general(ln, source_ref[...], NT, preferred_element_type=F32)
@@ -116,6 +122,11 @@
     tail = jnp.concatenate([mask, jnp.zeros((48, 96), F32)], axis=1).astype(BF16)
     left_ref[:, 1024:] = tail
     right_ref[:, 1024:] = tail
+    for u in range(4):
+        packed_ref[u, :384] = x_ref[u * 12 : (u + 1) * 12].reshape(384, 256)
+        flags = jnp.concatenate([mask[u * 12 : (u + 1) * 12], jnp.zeros((4, 32), F32)], axis=0)
+        flags = jnp.concatenate([flags, jnp.zeros((16, 224), F32)], axis=1)
+        packed_ref[u, 384:] = flags.astype(BF16)
 
 
 def pair_kernel(at_ref, *refs):
@@ -123,8 +134,10 @@
     mine_ref, other_ref, pair_ref, rows_ref, cols_ref, final_ref, offset_ref = refs[4:11]
     out_ref, bias_ref, column_ref, left_hold, right_hold, hold = refs[11:]
     seq_at, core = at_ref[0], at_ref[1]
-    right_hold[core] = mine_ref[...]
-    right_hold[1 - core] = other_ref[...]
+    for k in range(8):
+        place = k // 4 * 4 + (k + 8 - seq_at) % 4
+        right_hold[core, place] = mine_ref[k]
+        right_hold[1 - core, place] = other_ref[k]
     for k in range(8):
         left_hold[seq_at ^ k] = left_pieces[k % 4][k // 4]
     left_all = left_hold[...].reshape(384, 1152)
@@ -144,19 +157,19 @@
     factor = cols_ref[...] * rows_ref[...] / (count + 0.001)
     offset = offset_ref[...]
     def outer_of(block):
-        left = left_all[:, block * 256 : (block + 1) * 256]
+        left = left_all[:, block * 512 : (block + 1) * 512]
         return [
             lax.dot_general(left, r[:, :1024], TN, preferred_element_type=F32).astype(BF16)
             for r in right
         ]
 
     ahead = outer_of(0)
-    for block in range(4):
+    for block in range(2):
         outer = ahead
-        if block < 3:
+        if block < 1:
             ahead = outer_of(block + 1)
         turned = []
-        for i in range(8):
+        for i in range(16):
             for p in range(2):
                 rows = outer[p][i * 32 : (i + 1) * 32]
                 tiles = [rows[:, t * 128 : (t + 1) * 128] for t in range(8)]
@@ -166,8 +179,8 @@
             lhs = jnp.concatenate([t[e * 32 : (e + 1) * 32] for t in turned], axis=0)
             part = project(lhs, final_ref[e])
             terms = part if terms is None else terms + part
-        for i in range(8):
-            at = block * 8 + i
+        for i in range(16):
+            at = block * 16 + i
             sums = terms[i * 64 : (i + 1) * 64]
             fresh = pair_ref[at].astype(F32) + factor[:, at : at + 1] * sums
             fresh = fresh.astype(BF16)
@@ -239,6 +252,7 @@
             lambda h: held[h],
             mask_ref[...],
             pl.program_id(0) * STEP + t,
+            4,
         )
         for t in range(STEP)
     ]
@@ -259,7 +273,7 @@
         value_t = turned(wv_ref).astype(BF16)
         gates.append(jax.nn.sigmoid(turned(wg_ref)))
         mask = mask_columns(mask_ref[pl.ds(pl.program_id(0) * PICK + r, 1), :])
-        attentions.append(Attention(query_t, key, value_t, lambda h: None, mask, 0))
+        attentions.append(Attention(query_t, key, value_t, lambda h: None, mask, 0, 2))
 
     def finish(r, found):
         gated = (gates[r] * found).astype(BF16)
@@ -307,11 +321,11 @@
     res_at = lax.axis_index(RES)
     xl_at = lax.axis_index("xl")
     core_at = lax.axis_index("core")
-    mask = entry_exists_flags.astype(BF16)
-
-    left, right = pl.pallas_call(
+
+    left, right, packed = pl.pallas_call(
         factor_kernel,
-        out_shape=[jax.ShapeDtypeStruct((48, 1152), BF16)] * 2,
+        out_shape=[jax.ShapeDtypeStruct((48, 1152), BF16)] * 2
+        + [jax.ShapeDtypeStruct((4, 400, 256), BF16)],
         scratch_shapes=[pltpu.VMEM((1536, 128), F32)] * 2,
         compiler_params=pltpu.CompilerParams(vmem_limit_bytes=VMEM_LIMIT),
         name="factors",
@@ -322,7 +336,7 @@
         in_hbm(product_target_weights.T),
     )
     swap = [
-        ((a * 8 + b) * 2 + p, (b * 8 + a) * 2 + p)
+        ((a * 8 + b) * 2 + p, (b * 8 + a // 4 * 4 + (a + b) % 4) * 2 + p)
         for a in range(8)
         for b in range(8)
         for p in range(2)
@@ -330,27 +344,24 @@
     pairs = [(0, 1), (1, 0)]
     right = lax.ppermute(right, ALL, swap)
     left_yh = lax.ppermute(left, "yh", pairs)
-    right, left_yh = lax.optimization_barrier((right, left_yh))
+    team_at = lax.axis_index(TEAM)
+    parts = []
+    for k in range(4):
+        part = lax.dynamic_index_in_dim(packed, team_at ^ k, 0, False)
+        parts.append(lax.ppermute(part, TEAM, [(t, t ^ k) for t in range(4)]) if k else part)
+    right, left_yh, parts[2] = lax.optimization_barrier((right, left_yh, parts[2]))
+    packed = jnp.stack(parts).reshape(2, 2, 400, 256)
+    packed = jnp.where(lax.axis_index("yl") == 1, packed[::-1], packed)
+    packed = jnp.where(lax.axis_index("xh") == 1, packed[:, ::-1], packed)
+    packed = packed.reshape(4, 400, 256)
     mine = spread(right, ("yl", "xh", "xl"), 8)
     left = jnp.stack([left, left_yh])
     lefts = [left] + [
         lax.ppermute(left, "z", [(z, z ^ k) for z in range(4)]) for k in range(1, 4)
     ]
-    homolog_stack, mask, lefts[1] = lax.optimization_barrier((homolog_stack, mask, lefts[1]))
-    tail = jnp.pad(mask.reshape(4, 12, 32), ((0, 0), (0, 4), (0, 224)))
-    packed = jnp.concatenate([homolog_stack.reshape(4, 384, 256), tail], axis=1)
-    team_at = lax.axis_index(TEAM)
-    parts = []
-    for k in range(4):
-        part = lax.dynamic_index_in_dim(packed, team_at ^ k, 0, False)
-        parts.append(lax.ppermute(part, TEAM, [(t, t ^ k) for t in range(4)]) if k else part)
-    packed = jnp.stack(parts).reshape(2, 2, 400, 256)
-    packed = jnp.where(lax.axis_index("yl") == 1, packed[::-1], packed)
-    packed = jnp.where(lax.axis_index("xh") == 1, packed[:, ::-1], packed)
-    packed = packed.reshape(4, 400, 256)
     final = product_final_weights.reshape(32, 8, 4, 128)
     final = jnp.transpose(final, (2, 1, 0, 3)).reshape(4, 256, 128)
-    mine, final, packed, *lefts = lax.optimization_barrier((mine, final, packed, *lefts))
+    mine, final, *lefts = lax.optimization_barrier((mine, final, *lefts))
     other = lax.ppermute(mine, "core", pairs)
     packed_x = lax.ppermute(packed, "xl", pairs)
     packed_c = lax.ppermute(packed, "core", pairs)

time: 150 us -> 145 us (0.967)
  waiting for transfers between devices: 33.2 us -> 28.7 us
  Pallas kernels: 43 us -> 40 us
  other arithmetic: 2.26 us -> 4.95 us
    ppermute x3, waiting for transfers between devices: 0.01 us -> 12.5 us  [body(): lax.ppermute(part, TEAM, [(t, t ^ k) for t in range(4)])]
    ppermute x3, waiting for transfers between devices: 11.2 us -> 0.01 us  [body(): lax.ppermute(left, 'z', [(z, z ^ k) for z in range(4)])]
    ppermute x1, waiting for transfers between devices: 12.6 us -> 4.52 us  [body(): right = lax.ppermute(right, ALL, swap)]
    ppermute x1, waiting for transfers between devices: 1.74 us -> 5.76 us  [body(): packed_x = lax.ppermute(packed, 'xl', pairs)]
    all_to_all x1, waiting for transfers between devices: 4.81 us -> 1.7 us  [body(): bias = lax.all_to_all(bias, PLANE, split_axis=0, concat_axis=0, tiled=True)]
    all_to_all x1, starting transfers between devices: 6.98 us -> 9.07 us  [spread(): return lax.all_to_all(wide, axes, split_axis=0, concat_axis=0, tiled=True)]
    pallas_call x1, Pallas kernels: 14.9 us -> 12.9 us  [body(): pl.pallas_call(row_kernel, out_shape=jax.ShapeDtypeStruct((12, 128, 256),...]
    ppermute x1, waiting for transfers between devices: 0.01 us -> 1.72 us  [body(): left_yh = lax.ppermute(left, 'yh', pairs)]
  transfers between devices with their start and end apart: 14 -> 14, of which waited for: 7 -> 7; matrix products, arithmetic and copies ran while one was open for 2% -> 4% of each run, Pallas kernels for 11% -> 11%
where the time goes in v2:
time: 145 us; the launch traced here: 143 us
  Pallas kernels  40 us (28%)
  blocking collectives  34.9 us (24%)
  starting transfers between devices  29.1 us (20%)
  waiting for transfers between devices  28.7 us (20%)
  other arithmetic  4.95 us (3%)
  local copies, waits for them, and re-layouts  4.16 us (3%)
    all_to_all x1, blocking collectives, body(): lax.all_to_all(middle.reshape(32, 12, 4, 256), PLANE, split_axis=0, conca...  20 us
    all_to_all x1, blocking collectives, body(): lax.all_to_all(columns, SEQ, split_axis=0, concat_axis=0, tiled=True)  14.9 us
    pallas_call x1, Pallas kernels, body(): pl.pallas_call(row_kernel, out_shape=jax.ShapeDtypeStruct((12, 128, 256),...  12.9 us
    ppermute x3, waiting for transfers between devices, body(): lax.ppermute(part, TEAM, [(t, t ^ k) for t in range(4)])  12.5 us
    all_to_all x1, starting transfers between devices, spread(): return lax.all_to_all(wide, axes, split_axis=0, concat_axis=0, tiled=True)  9.07 us
    pallas_call x1, Pallas kernels, body(): pl.pallas_call(ready_kernel, out_shape=[pltpu.HBM(shape, kind) for shape,...  8.4 us
    pallas_call x1, Pallas kernels, body(): pl.pallas_call(column_kernel, out_shape=jax.ShapeDtypeStruct((4, 384, 256...  7.89 us
    pallas_call x1, Pallas kernels, body(): pl.pallas_call(pair_kernel, out_shape=(jax.ShapeDtypeStruct((32, 64, 128)...  7.55 us
  transfers between devices with their start and end apart: 14, of which 7 were waited for; matrix products, arithmetic and copies ran while one was open for 4% of the time, Pallas kernels for 11%

profile of v2, /device:TPU:8, one launch (start us, length us, event | category | flops | bytes accessed | tf_op | source)
XLA Modules:
  0.0 142.7 jit_solution(17246869475341797449)
XLA Ops:
  0.7 3.2 %factors.1 = (bf16[48,1152]{1,0:T(8,128)(2,1)S(1)}, bf16[48,1152]{1,0:T(8,128)(2,1)S(1)}, bf16[4,400,256]{2,1,0:T(8,128)(2,1)S(1)}) custom-call(bf16[48,32,256]{2,1,0:T(8,128)(2,1)} %x_ref.1, s32[32,48]{1,0:T(8,128)} %bitcast.59, bf16[32,256]{1,0:T(8,128)(2,1)} %bitcast.60, bf16[32,256]{1,0:T(8,128)(2,1)} %bitcast.61), custom_call_target="tpu_custom_call" | custom-call | tf_op jit(solution)/shard_map/factors/pallas_call | solution.py:325
  3.9 0.1 constant_dynamic-slice_fusion
  4.0 0.4 collective-permute-start.3
  4.4 4.4 %collective-permute-start.1 = (bf16[48,1152]{1,0:T(8,128)(2,1)S(1)}, bf16[48,1152]{1,0:T(8,128)(2,1)S(1)}, u32[]{:S(2)}, u32[]{:S(2)}) collective-permute-start(bf16[48,1152]{1,0:T(8,128)(2,1)S(1)} %get-tuple-element.26), channel_id=1, source_target_pairs={{0,0},{1,1},{2,18},{3,19},{4,36},{5,37},{6,54},{7,55},{8,64},{9,65... | collective-permute-start | bytes 331784 | tf_op jit(solution)/shard_map/ppermute | solution.py:345
  8.8 0.1 collective-permute-start.2
  8.9 4.5 %collective-permute-done.1 = bf16[48,1152]{1,0:T(8,128)(2,1)S(1)} collective-permute-done((bf16[48,1152]{1,0:T(8,128)(2,1)S(1)}, bf16[48,1152]{1,0:T(8,128)(2,1)S(1)}, u32[]{:S(2)}, u32[]{:S(2)}) %collective-permute-start.1) | collective-permute-done | bytes 110624 | tf_op jit(solution)/shard_map/ppermute | solution.py:345
  13.4 1.7 %collective-permute-done.2 = bf16[48,1152]{1,0:T(8,128)(2,1)S(1)} collective-permute-done((bf16[48,1152]{1,0:T(8,128)(2,1)S(1)}, bf16[48,1152]{1,0:T(8,128)(2,1)S(1)}, u32[]{:S(2)}, u32[]{:S(2)}) %collective-permute-start.2) | collective-permute-done | bytes 110624 | tf_op jit(solution)/shard_map/ppermute | solution.py:346
  15.2 1.0 broadcast_in_dim.2
  16.2 9.1 %all-to-all-start = ((bf16[8,48,1152]{2,1,0:T(8,128)(2,1)}), bf16[8,48,1152]{2,1,0:T(8,128)(2,1)S(1)}, u32[]{:S(2)}, u32[]{:S(2)}) async-start(bf16[8,48,1152]{2,1,0:T(8,128)(2,1)} %broadcast_in_dim.2), calls=%async_computation | async-start | bytes 1769472 | tf_op jit(solution)/shard_map/all_to_all | solution.py:292
  25.2 3.0 %collective-permute-start.4 = (bf16[400,256]{1,0:T(8,128)(2,1)S(1)}, bf16[400,256]{1,0:T(8,128)(2,1)}, u32[]{:S(2)}, u32[]{:S(2)}) collective-permute-start(bf16[400,256]{1,0:T(8,128)(2,1)S(1)} %get-tuple-element.49), channel_id=1, source_target_pairs={{0,12},{4,8},{8,4},{12,0},{1,13},{5,9},{9,5},{13,1},{2,14},{6,10},... | collective-permute-start | bytes 614408 | tf_op jit(solution)/shard_map/ppermute | solution.py:351
  28.3 0.1 collective-permute-start
  28.4 0.1 copy.29
  28.5 0.8 collective-permute-start.9
  29.3 2.0 %collective-permute-start.8 = (bf16[2,48,1152]{2,1,0:T(8,128)(2,1)S(1)}, bf16[2,48,1152]{2,1,0:T(8,128)(2,1)S(1)}, u32[]{:S(2)}, u32[]{:S(2)}) collective-permute-start(bf16[2,48,1152]{2,1,0:T(8,128)(2,1)S(1)} %pad_maximum_fusion.1.refs_0_), channel_id=1, source_target_pairs={{0,32},{16,48},{32,0},{48,16},{1,33},{17,49},{33,1},{49,17},{2,34}... | collective-permute-start | bytes 663560 | tf_op jit(solution)/shard_map/ppermute | solution.py:360
  31.3 1.4 collective-permute-start.7
  32.7 10.3 %collective-permute-done.4 = bf16[400,256]{1,0:T(8,128)(2,1)} collective-permute-done((bf16[400,256]{1,0:T(8,128)(2,1)S(1)}, bf16[400,256]{1,0:T(8,128)(2,1)}, u32[]{:S(2)}, u32[]{:S(2)}) %collective-permute-start.4) | collective-permute-done | bytes 204832 | tf_op jit(solution)/shard_map/ppermute | solution.py:351
  43.0 2.2 %collective-permute-done = bf16[400,256]{1,0:T(8,128)(2,1)} collective-permute-done((bf16[400,256]{1,0:T(8,128)(2,1)S(1)}, bf16[400,256]{1,0:T(8,128)(2,1)}, u32[]{:S(2)}, u32[]{:S(2)}) %collective-permute-start) | collective-permute-done | bytes 204832 | tf_op jit(solution)/shard_map/ppermute | solution.py:351
  45.2 1.1 pad_maximum_fusion
  46.4 1.1 reverse_select_fusion.1
  47.5 0.1 collective-permute-start.10
  47.6 2.6 %reverse_select_fusion = bf16[2,2,400,256]{3,2,1,0:T(8,128)(2,1)} fusion(bf16[2,2,400,256]{3,2,1,0:T(8,128)(2,1)} %reverse_select_fusion.1, pred[]{:T(512)S(6)} %eq.6), kind=kLoop, calls=%fused_computation | loop fusion | flops 409600 | bytes 1638401 | tf_op jit(solution)/shard_map/jit(_where)/select_n | solution.py:355
  50.1 0.5 collective-permute-start.6
  50.6 0.2 collective-permute-start.5
  50.9 0.1 dynamic-slice_bitcast_fusion.3
  50.9 0.1 copy.30.refs_8_
  51.0 0.1 dynamic-slice_bitcast_fusion.4.refs_7_
  51.1 0.1 pad_add_fusion.at_ref
  51.2 7.6 %pair.1 = (bf16[32,64,128]{2,1,0:T(8,128)(2,1)}, bf16[32,8,16,128]{3,2,1,0:T(8,128)(2,1)}, f32[8,384]{1,0:T(8,128)S(1)}) custom-call(s32[2]{0:T(128)S(1)} %pad_add_fusion.at_ref, bf16[2,48,1152]{2,1,0:T(8,128)(2,1)S(1)} %pad_maximum_fusion.1.refs_0_, bf16[2,48,1152]{2,1,0:T(8,128)(2,1)S(1)} %collective-permute-done.7.refs_1_, ...), custom_call_target="tpu_custom_call" | custom-call | flops 1000 | bytes 1000 | tf_op jit(solution)/shard_map/pair/pallas_call | solution.py:375
  58.7 7.0 %all-to-all-start.1 = ((bf16[32,8,16,128]{3,2,1,0:T(8,128)(2,1)}), bf16[32,8,16,128]{3,2,1,0:T(8,128)(2,1)S(1)}, u32[]{:S(2)}, u32[]{:S(2)}) async-start(bf16[32,8,16,128]{3,2,1,0:T(8,128)(2,1)} %get-tuple-element.37), calls=%async_computation.1 | async-start | bytes 2097152 | tf_op jit(solution)/shard_map/all_to_all | solution.py:438
  65.7 5.8 %collective-permute-done.6.refs_2_.refs_6_ = bf16[4,400,256]{2,1,0:T(8,128)(2,1)} collective-permute-done((bf16[4,400,256]{2,1,0:T(8,128)(2,1)}, bf16[4,400,256]{2,1,0:T(8,128)(2,1)}, u32[]{:S(2)}, u32[]{:S(2)}) %collective-permute-start.6) | collective-permute-done | bytes 819232 | tf_op jit(solution)/shard_map/ppermute | solution.py:366
  71.5 0.1 pad_add_fusion.1.at_ref
  71.6 2.5 %collective-permute-done.11.refs_3_.refs_7_ = bf16[4,400,256]{2,1,0:T(8,128)(2,1)S(1)} collective-permute-done((bf16[4,400,256]{2,1,0:T(8,128)(2,1)}, bf16[4,400,256]{2,1,0:T(8,128)(2,1)S(1)}, u32[]{:S(2)}, u32[]{:S(2)}) %collective-permute-start.11) | collective-permute-done | bytes 819232 | tf_op jit(solution)/shard_map/ppermute | solution.py:406
  74.0 0.9 copy-done.8
  75.0 8.4 %ready.1 = (bf16[12,256,128]{2,1,0:T(8,128)(2,1)}, bf16[12,512,256]{2,1,0:T(8,128)(2,1)}, bf16[12,256,512]{2,1,0:T(8,128)(2,1)}, f32[12,256,128]{2,1,0:T(8,128)}, bf16[512,128]{1,0:T(8,128)(2,1)}) custom-call(s32[2]{0:T(128)S(1)} %pad_add_fusion.1.at_ref, bf16[4,400,256]{2,1,0:T(8,128)(2,1)} %bitcast.10.refs_0_.refs_4_.x_ref, ...), custom_call_target="tpu_custom_call" | custom-call | flops 1000 | bytes 1000 | tf_op jit(solution)/shard_map/ready/pallas_call | solution.py:410
  83.4 1.7 %all-to-all-done.1 = bf16[32,8,16,128]{3,2,1,0:T(8,128)(2,1)S(1)} async-done(((bf16[32,8,16,128]{3,2,1,0:T(8,128)(2,1)}), bf16[32,8,16,128]{3,2,1,0:T(8,128)(2,1)S(1)}, u32[]{:S(2)}, u32[]{:S(2)}) %all-to-all-start.1) | async-done | bytes 1048608 | tf_op jit(solution)/shard_map/all_to_all | solution.py:438
  85.1 12.9 %rows.1 = bf16[12,128,256]{2,1,0:T(8,128)(2,1)S(1)} custom-call(bf16[4,400,256]{2,1,0:T(8,128)(2,1)} %bitcast.10.refs_0_.refs_4_.x_ref, bf16[12,256,128]{2,1,0:T(8,128)(2,1)} %get-tuple-element.41.query_ref, bf16[12,512,256]{2,1,0:T(8,128)(2,1)} %get-tuple-element.42.key_ref, bf16[12,256,512]{2,1,0:T(8,128)(2,1)} %get-tuple-element.43.value_ref, ...), custom_call_target="tpu_custom_call" | custom-call | flops 8000000000 | bytes 12000000 | tf_op jit(solution)/shard_map/rows/pallas_call | solution.py:442
  98.0 0.0 copy-start.3
  98.0 0.0 copy-start.4
  98.0 0.0 copy-start.5
  98.0 0.0 copy-start.6
  98.0 0.2 reshape.48
  98.2 0.3 copy.31
  98.5 20.0 %all_to_all.20 = bf16[32,12,4,256]{3,2,1,0:T(4,128)(2,1)S(1)} all-to-all(bf16[32,12,4,256]{3,2,1,0:T(4,128)(2,1)S(1)} %bitcast.51), channel_id=1, replica_groups=mesh['yh'=2,'z'=4,'yl'=2,'xh'=2,'xl'=2,'core'=2] {'yh','z','yl','xh'}, dimensions={0} | all-to-all | bytes 1572864 | tf_op jit(solution)/shard_map/all_to_all | solution.py:459
  118.5 0.1 copy.40
  118.7 7.9 %columns.1 = bf16[4,384,256]{2,1,0:T(8,128)(2,1)S(1)} custom-call(bf16[4,384,256]{2,1,0:T(8,128)(2,1)S(1)} %bitcast.45, f32[8,384]{1,0:T(8,128)S(1)} %get-tuple-element.46.mask_ref, bf16[256,256]{1,0:T(8,128)(2,1)S(1)} %copy-done.3, bf16[256,256]{1,0:T(8,128)(2,1)S(1)} %copy-done.4, bf16[256,256]{1,0:T(8,128)(2,1)S(1)} %copy-done.5, ...), custom_call_target="tpu_custom_call" | custom-call | flops 8000000000 | bytes 2000000 | tf_op jit(solution)/shard_map/columns/pallas_call | solution.py:463
  126.6 0.1 copy.39
  126.6 14.9 %all_to_all.21 = bf16[8,4,48,256]{3,2,1,0:T(8,128)(2,1)S(1)} all-to-all(bf16[8,4,48,256]{3,2,1,0:T(8,128)(2,1)S(1)} %bitcast.53), channel_id=1, replica_groups=mesh['yh'=2,'z'=4,'yl'=2,'xh'=2,'xl'=2,'core'=2] {'yh','z'}, dimensions={0} | all-to-all | bytes 1572864 | tf_op jit(solution)/shard_map/all_to_all | solution.py:492
  141.5 1.1 copy.38
  (27 shorter events, 0.1 us)
Async XLA Ops:
  0.6 27.8 %copy-start.9 = (bf16[1024,128]{1,0:T(8,128)(2,1)S(1)}, bf16[1024,128]{1,0:T(8,128)(2,1)}, u32[]{:S(2)}) copy-start(bf16[1024,128]{1,0:T(8,128)(2,1)} %param.24) | copy-start | bytes 786436
  4.0 11.2 %collective-permute-start.3 = (bf16[400,256]{1,0:T(8,128)(2,1)S(1)}, bf16[400,256]{1,0:T(8,128)(2,1)S(1)}, u32[]{:S(2)}, u32[]{:S(2)}) collective-permute-start(bf16[400,256]{1,0:T(8,128)(2,1)S(1)} %get-tuple-element.50), channel_id=1, source_target_pairs={{0,8},{4,12},{8,0},{12,4},{1,9},{5,13},{9,1},{13,5},{2,10},{6,14},... | collective-permute-start | bytes 614408 | tf_op jit(solution)/shard_map/ppermute | solution.py:351
  4.4 9.0 %collective-permute-start.1 = (bf16[48,1152]{1,0:T(8,128)(2,1)S(1)}, bf16[48,1152]{1,0:T(8,128)(2,1)S(1)}, u32[]{:S(2)}, u32[]{:S(2)}) collective-permute-start(bf16[48,1152]{1,0:T(8,128)(2,1)S(1)} %get-tuple-element.26), channel_id=1, source_target_pairs={{0,0},{1,1},{2,18},{3,19},{4,36},{5,37},{6,54},{7,55},{8,64},{9,65... | collective-permute-start | bytes 331784 | tf_op jit(solution)/shard_map/ppermute | solution.py:345
  8.8 6.3 %collective-permute-start.2 = (bf16[48,1152]{1,0:T(8,128)(2,1)S(1)}, bf16[48,1152]{1,0:T(8,128)(2,1)S(1)}, u32[]{:S(2)}, u32[]{:S(2)}) collective-permute-start(bf16[48,1152]{1,0:T(8,128)(2,1)S(1)} %get-tuple-element.27), channel_id=1, source_target_pairs={{0,64},{64,0},{1,65},{65,1},{2,66},{66,2},{3,67},{67,3},{4,68},{68... | collective-permute-start | bytes 331784 | tf_op jit(solution)/shard_map/ppermute | solution.py:346
  16.2 31.3 %all-to-all-start = ((bf16[8,48,1152]{2,1,0:T(8,128)(2,1)}), bf16[8,48,1152]{2,1,0:T(8,128)(2,1)S(1)}, u32[]{:S(2)}, u32[]{:S(2)}) async-start(bf16[8,48,1152]{2,1,0:T(8,128)(2,1)} %broadcast_in_dim.2), calls=%async_computation | async-start | bytes 1769472 | tf_op jit(solution)/shard_map/all_to_all | solution.py:292
  25.2 25.6 %copy-start.10 = (s32[512]{0:T(512)S(1)}, s32[512]{0:T(512)}, u32[]{:S(2)}) copy-start(s32[512]{0:T(512)} %param.20) | copy-start | bytes 6148
  25.2 26.0 %copy-start = (bf16[32,64,128]{2,1,0:T(8,128)(2,1)S(1)}, bf16[32,64,128]{2,1,0:T(8,128)(2,1)}, u32[]{:S(2)}) copy-start(bf16[32,64,128]{2,1,0:T(8,128)(2,1)} %refs_6_.1) | copy-start | bytes 1572868
  25.2 26.0 %copy-start.1 = (bf16[128,8]{0,1:T(8,128)(2,1)S(1)}, bf16[128,8]{0,1:T(8,128)(2,1)}, u32[]{:S(2)}) copy-start(bf16[128,8]{0,1:T(8,128)(2,1)} %param.25) | copy-start | bytes 6148
  25.2 17.8 %collective-permute-start.4 = (bf16[400,256]{1,0:T(8,128)(2,1)S(1)}, bf16[400,256]{1,0:T(8,128)(2,1)}, u32[]{:S(2)}, u32[]{:S(2)}) collective-permute-start(bf16[400,256]{1,0:T(8,128)(2,1)S(1)} %get-tuple-element.49), channel_id=1, source_target_pairs={{0,12},{4,8},{8,4},{12,0},{1,13},{5,9},{9,5},{13,1},{2,14},{6,10},... | collective-permute-start | bytes 614408 | tf_op jit(solution)/shard_map/ppermute | solution.py:351
  28.3 16.9 %collective-permute-start = (bf16[400,256]{1,0:T(8,128)(2,1)S(1)}, bf16[400,256]{1,0:T(8,128)(2,1)}, u32[]{:S(2)}, u32[]{:S(2)}) collective-permute-start(bf16[400,256]{1,0:T(8,128)(2,1)S(1)} %get-tuple-element.51), channel_id=1, source_target_pairs={{0,4},{4,0},{8,12},{12,8},{1,5},{5,1},{9,13},{13,9},{2,6},{6,2},{1... | collective-permute-start | bytes 614408 | tf_op jit(solution)/shard_map/ppermute | solution.py:351
  28.5 18.9 %collective-permute-start.9 = (bf16[2,48,1152]{2,1,0:T(8,128)(2,1)S(1)}, bf16[2,48,1152]{2,1,0:T(8,128)(2,1)S(1)}, u32[]{:S(2)}, u32[]{:S(2)}) collective-permute-start(bf16[2,48,1152]{2,1,0:T(8,128)(2,1)S(1)} %pad_maximum_fusion.1.refs_0_), channel_id=1, source_target_pairs={{0,48},{16,32},{32,16},{48,0},{1,49},{17,33},{33,17},{49,1},{2,50}... | collective-permute-start | bytes 663560 | tf_op jit(solution)/shard_map/ppermute | solution.py:360
  29.3 18.1 %collective-permute-start.8 = (bf16[2,48,1152]{2,1,0:T(8,128)(2,1)S(1)}, bf16[2,48,1152]{2,1,0:T(8,128)(2,1)S(1)}, u32[]{:S(2)}, u32[]{:S(2)}) collective-permute-start(bf16[2,48,1152]{2,1,0:T(8,128)(2,1)S(1)} %pad_maximum_fusion.1.refs_0_), channel_id=1, source_target_pairs={{0,32},{16,48},{32,0},{48,16},{1,33},{17,49},{33,1},{49,17},{2,34}... | collective-permute-start | bytes 663560 | tf_op jit(solution)/shard_map/ppermute | solution.py:360
  31.3 16.1 %collective-permute-start.7 = (bf16[2,48,1152]{2,1,0:T(8,128)(2,1)S(1)}, bf16[2,48,1152]{2,1,0:T(8,128)(2,1)S(1)}, u32[]{:S(2)}, u32[]{:S(2)}) collective-permute-start(bf16[2,48,1152]{2,1,0:T(8,128)(2,1)S(1)} %pad_maximum_fusion.1.refs_0_), channel_id=1, source_target_pairs={{0,16},{16,0},{32,48},{48,32},{1,17},{17,1},{33,49},{49,33},{2,18}... | collective-permute-start | bytes 663560 | tf_op jit(solution)/shard_map/ppermute | solution.py:360
  47.5 3.7 %collective-permute-start.10 = (bf16[8,48,1152]{2,1,0:T(8,128)(2,1)S(1)}, bf16[8,48,1152]{2,1,0:T(8,128)(2,1)S(1)}, u32[]{:S(2)}, u32[]{:S(2)}) collective-permute-start(bf16[8,48,1152]{2,1,0:T(8,128)(2,1)S(1)} %all-to-all-done.refs_4_), channel_id=1, source_target_pairs={{0,1},{1,0},{2,3},{3,2},{4,5},{5,4},{6,7},{7,6},{8,9},{9,8},{10,11... | collective-permute-start | bytes 2654216 | tf_op jit(solution)/shard_map/ppermute | solution.py:365
  50.1 21.4 %collective-permute-start.6 = (bf16[4,400,256]{2,1,0:T(8,128)(2,1)}, bf16[4,400,256]{2,1,0:T(8,128)(2,1)}, u32[]{:S(2)}, u32[]{:S(2)}) collective-permute-start(bf16[4,400,256]{2,1,0:T(8,128)(2,1)} %bitcast.10.refs_0_.refs_4_.x_ref), channel_id=1, source_target_pairs={{0,2},{2,0},{1,3},{3,1},{4,6},{6,4},{5,7},{7,5},{8,10},{10,8},{9,1... | collective-permute-start | bytes 2457608 | tf_op jit(solution)/shard_map/ppermute | solution.py:366
  50.6 20.8 %collective-permute-start.5 = (bf16[4,400,256]{2,1,0:T(8,128)(2,1)}, bf16[4,400,256]{2,1,0:T(8,128)(2,1)}, u32[]{:S(2)}, u32[]{:S(2)}) collective-permute-start(bf16[4,400,256]{2,1,0:T(8,128)(2,1)} %bitcast.10.refs_0_.refs_4_.x_ref), channel_id=1, source_target_pairs={{0,1},{1,0},{2,3},{3,2},{4,5},{5,4},{6,7},{7,6},{8,9},{9,8},{10,11... | collective-permute-start | bytes 2457608 | tf_op jit(solution)/shard_map/ppermute | solution.py:367
  58.7 26.3 %all-to-all-start.1 = ((bf16[32,8,16,128]{3,2,1,0:T(8,128)(2,1)}), bf16[32,8,16,128]{3,2,1,0:T(8,128)(2,1)S(1)}, u32[]{:S(2)}, u32[]{:S(2)}) async-start(bf16[32,8,16,128]{3,2,1,0:T(8,128)(2,1)} %get-tuple-element.37), calls=%async_computation.1 | async-start | bytes 2097152 | tf_op jit(solution)/shard_map/all_to_all | solution.py:438
  71.5 2.5 %collective-permute-start.11 = (bf16[4,400,256]{2,1,0:T(8,128)(2,1)}, bf16[4,400,256]{2,1,0:T(8,128)(2,1)S(1)}, u32[]{:S(2)}, u32[]{:S(2)}) collective-permute-start(bf16[4,400,256]{2,1,0:T(8,128)(2,1)} %collective-permute-done.6.refs_2_.refs_6_), channel_id=1, source_target_pairs={{0,1},{1,0},{2,3},{3,2},{4,5},{5,4},{6,7},{7,6},{8,9},{9,8},{10,11... | collective-permute-start | bytes 2457608 | tf_op jit(solution)/shard_map/ppermute | solution.py:406
  71.6 13.5 %copy-start.2 = (bf16[256,256]{1,0:T(8,128)(2,1)S(1)}, bf16[256,256]{1,0:T(8,128)(2,1)}, u32[]{:S(2)}) copy-start(bf16[256,256]{1,0:T(8,128)(2,1)} %wo_ref.2) | copy-start | bytes 393220
  74.0 0.9 copy-start.8
  98.0 20.6 %copy-start.3 = (bf16[256,256]{1,0:T(8,128)(2,1)S(1)}, bf16[256,256]{1,0:T(8,128)(2,1)}, u32[]{:S(2)}) copy-start(bf16[256,256]{1,0:T(8,128)(2,1)} %wq_ref.1) | copy-start | bytes 393220
  98.0 20.6 %copy-start.4 = (bf16[256,256]{1,0:T(8,128)(2,1)S(1)}, bf16[256,256]{1,0:T(8,128)(2,1)}, u32[]{:S(2)}) copy-start(bf16[256,256]{1,0:T(8,128)(2,1)} %wk_ref.1) | copy-start | bytes 393220
  98.0 20.6 %copy-start.5 = (bf16[256,256]{1,0:T(8,128)(2,1)S(1)}, bf16[256,256]{1,0:T(8,128)(2,1)}, u32[]{:S(2)}) copy-start(bf16[256,256]{1,0:T(8,128)(2,1)} %wv_ref.1) | copy-start | bytes 393220
  98.0 20.6 %copy-start.6 = (bf16[256,256]{1,0:T(8,128)(2,1)S(1)}, bf16[256,256]{1,0:T(8,128)(2,1)}, u32[]{:S(2)}) copy-start(bf16[256,256]{1,0:T(8,128)(2,1)} %wg_ref.1) | copy-start | bytes 393220
  98.0 20.6 %copy-start.7 = (bf16[256,256]{1,0:T(8,128)(2,1)S(1)}, bf16[256,256]{1,0:T(8,128)(2,1)}, u32[]{:S(2)}) copy-start(bf16[256,256]{1,0:T(8,128)(2,1)} %wo_ref.3) | copy-start | bytes 393220

commit v3 on v2

--- a/solution.py
+++ b/solution.py
@@ -212,18 +212,25 @@
                 columns[u, a, b, :, :16] = absent[:32]
         mask_ref[...] = columns[...].reshape(512, 128).astype(BF16)
 
+    asked = []
     for t in range(STEP):
         rows = slice(t * 32, (t + 1) * 32)
-        asked = normalize(x_ref[:, rows].reshape(128, 256))
-        ordered[t, :, xl, core] = asked.reshape(4, 32, 256)
+        asked.append(normalize(x_ref[:, rows].reshape(128, 256)))
+        ordered[t, :, xl, core] = asked[t].reshape(4, 32, 256)
         ordered[t, :, xl, 1 - core] = normalize(xc_ref[:, rows])
         ordered[t, :, 1 - xl, core] = normalize(xx_ref[:, rows])
         ordered[t, :, 1 - xl, 1 - core] = normalize(xxc_ref[:, rows])
-        keys = ordered[t].reshape(512, 256)
-        query_ref[t] = (project(asked, wq_ref[...]) * (HEAD**-0.5 * LOG2E)).T.astype(BF16)
-        key_ref[t] = project(keys, wk_ref[...]).astype(BF16)
-        value_ref[t] = project(keys, wv_ref[...]).astype(BF16).T
-        gate_ref[t] = jax.nn.sigmoid(project(asked, wg_ref[...])).T
+    keys = ordered[...].reshape(STEP * 512, 256)
+    both = project(keys, jnp.concatenate([wk_ref[...], wv_ref[...]], axis=1))
+    asking = jnp.concatenate([wq_ref[...], wg_ref[...]], axis=1)
+    asks = project(jnp.concatenate(asked, axis=0), asking)
+    for t in range(STEP):
+        own = asks[t * 128 : (t + 1) * 128]
+        query_ref[t] = (own[:, :256] * (HEAD**-0.5 * LOG2E)).T.astype(BF16)
+        gate_ref[t] = jax.nn.sigmoid(own[:, 256:]).T
+        rows = slice(t * 512, (t + 1) * 512)
+        key_ref[t] = both[rows, :256].astype(BF16)
+        value_ref[t] = both[rows, 256:].astype(BF16).T
 
 
 def row_kernel(
@@ -260,20 +267,21 @@
 
 
 def column_kernel(x_ref, mask_ref, wq_ref, wk_ref, wv_ref, wg_ref, wo_ref, out_ref):
+    keys = normalize(x_ref[...].reshape(PICK * 384, 256))
+    key = project(keys, wk_ref[...]).astype(BF16)
+    weights = jnp.concatenate([wq_ref[...], wv_ref[...], wg_ref[...]], axis=1)
+    turned = lax.dot_general(weights, keys.T, TN, preferred_element_type=F32)
+    query_t = (turned[:256] * (HEAD**-0.5 * LOG2E)).astype(BF16)
+    value_t = turned[256:512].astype(BF16)
+    gate = jax.nn.sigmoid(turned[512:])
     gates, attentions = [], []
     for r in range(PICK):
-        keys = normalize(x_ref[r])
-        keys_t = keys.T
-
-        def turned(weight_ref):
-            return lax.dot_general(weight_ref[...], keys_t, TN, preferred_element_type=F32)
-
-        query_t = (turned(wq_ref) * (HEAD**-0.5 * LOG2E)).astype(BF16)
-        key = project(keys, wk_ref[...]).astype(BF16)
-        value_t = turned(wv_ref).astype(BF16)
-        gates.append(jax.nn.sigmoid(turned(wg_ref)))
+        rows = slice(r * 384, (r + 1) * 384)
+        gates.append(gate[:, rows])
         mask = mask_columns(mask_ref[pl.ds(pl.program_id(0) * PICK + r, 1), :])
-        attentions.append(Attention(query_t, key, value_t, lambda h: None, mask, 0, 2))
+        attentions.append(
+            Attention(query_t[:, rows], key[rows], value_t[:, rows], lambda h: None, mask, 0, 2)
+        )
 
     def finish(r, found):
         gated = (gates[r] * found).astype(BF16)
@@ -349,11 +357,11 @@
     for k in range(4):
         part = lax.dynamic_index_in_dim(packed, team_at ^ k, 0, False)
         parts.append(lax.ppermute(part, TEAM, [(t, t ^ k) for t in range(4)]) if k else part)
-    right, left_yh, parts[2] = lax.optimization_barrier((right, left_yh, parts[2]))
     packed = jnp.stack(parts).reshape(2, 2, 400, 256)
     packed = jnp.where(lax.axis_index("yl") == 1, packed[::-1], packed)
     packed = jnp.where(lax.axis_index("xh") == 1, packed[:, ::-1], packed)
     packed = packed.reshape(4, 400, 256)
+    right, left_yh, packed = lax.optimization_barrier((right, left_yh, packed))
     mine = spread(right, ("yl", "xh", "xl"), 8)
     left = jnp.stack([left, left_yh])
     lefts = [left] + [

time: 145 us -> 139 us (0.959)
  waiting for transfers between devices: 28.7 us -> 25 us
  other arithmetic: 4.95 us -> 1.48 us
  starting transfers between devices: 29.1 us -> 30.7 us
    ppermute x3, waiting for transfers between devices: 0.01 us -> 8.86 us  [body(): lax.ppermute(left, 'z', [(z, z ^ k) for z in range(4)])]
    ppermute x3, waiting for transfers between devices: 12.5 us -> 5.14 us  [body(): lax.ppermute(part, TEAM, [(t, t ^ k) for t in range(4)])]
    ppermute x1, waiting for transfers between devices: 4.52 us -> 0.01 us  [body(): right = lax.ppermute(right, ALL, swap)]
    select_n x1, other arithmetic: 2.55 us -> 1.05 us  [body(): packed = jnp.where(lax.axis_index('xh') == 1, packed[:, ::-1], packed)]
    ppermute x3, starting transfers between devices: 3.59 us -> 5.07 us  [body(): lax.ppermute(part, TEAM, [(t, t ^ k) for t in range(4)])]
  transfers between devices with their start and end apart: 14 -> 14, of which waited for: 7 -> 9; matrix products, arithmetic and copies ran while one was open for 4% -> 1% of each run, Pallas kernels for 11% -> 12%
where the time goes in v3:
time: 139 us; the launch traced here: 138 us
  Pallas kernels  39.9 us (29%)
  blocking collectives  35.8 us (26%)
  starting transfers between devices  30.7 us (22%)
  waiting for transfers between devices  25 us (18%)
  local copies, waits for them, and re-layouts  4.17 us (3%)
  other arithmetic  1.48 us (1%)
    all_to_all x1, blocking collectives, body(): lax.all_to_all(middle.reshape(32, 12, 4, 256), PLANE, split_axis=0, conca...  21 us
    all_to_all x1, blocking collectives, body(): lax.all_to_all(columns, SEQ, split_axis=0, concat_axis=0, tiled=True)  14.8 us
    pallas_call x1, Pallas kernels, body(): pl.pallas_call(row_kernel, out_shape=jax.ShapeDtypeStruct((12, 128, 256),...  12.9 us
    all_to_all x1, starting transfers between devices, spread(): return lax.all_to_all(wide, axes, split_axis=0, concat_axis=0, tiled=True)  10 us
    ppermute x3, waiting for transfers between devices, body(): lax.ppermute(left, 'z', [(z, z ^ k) for z in range(4)])  8.86 us
    pallas_call x1, Pallas kernels, body(): pl.pallas_call(ready_kernel, out_shape=[pltpu.HBM(shape, kind) for shape,...  8.77 us
    pallas_call x1, Pallas kernels, body(): pl.pallas_call(pair_kernel, out_shape=(jax.ShapeDtypeStruct((32, 64, 128)...  7.54 us
    pallas_call x1, Pallas kernels, body(): pl.pallas_call(column_kernel, out_shape=jax.ShapeDtypeStruct((4, 384, 256...  7.44 us
  transfers between devices with their start and end apart: 14, of which 9 were waited for; matrix products, arithmetic and copies ran while one was open for 1% of the time, Pallas kernels for 12%

profile of v3, /device:TPU:8, one launch (start us, length us, event | category | flops | bytes accessed | tf_op | source)
XLA Modules:
  0.0 137.9 jit_solution(5870880564944283213)
XLA Ops:
  0.7 3.2 %factors.1 = (bf16[48,1152]{1,0:T(8,128)(2,1)S(1)}, bf16[48,1152]{1,0:T(8,128)(2,1)S(1)}, bf16[4,400,256]{2,1,0:T(8,128)(2,1)S(1)}) custom-call(bf16[48,32,256]{2,1,0:T(8,128)(2,1)} %x_ref.1, s32[32,48]{1,0:T(8,128)} %bitcast.66, bf16[32,256]{1,0:T(8,128)(2,1)} %bitcast.67, bf16[32,256]{1,0:T(8,128)(2,1)} %bitcast.68), custom_call_target="tpu_custom_call" | custom-call | tf_op jit(solution)/shard_map/factors/pallas_call | solution.py:333
  3.9 0.1 constant_dynamic-slice_fusion
  3.9 3.0 %collective-permute-start.4 = (bf16[400,256]{1,0:T(8,128)(2,1)S(1)}, bf16[400,256]{1,0:T(8,128)(2,1)S(1)}, u32[]{:S(2)}, u32[]{:S(2)}) collective-permute-start(bf16[400,256]{1,0:T(8,128)(2,1)S(1)} %get-tuple-element.49), channel_id=1, source_target_pairs={{0,12},{4,8},{8,4},{12,0},{1,13},{5,9},{9,5},{13,1},{2,14},{6,10},... | collective-permute-start | bytes 614408 | tf_op jit(solution)/shard_map/ppermute | solution.py:359
  6.9 1.6 %collective-permute-start.3 = (bf16[400,256]{1,0:T(8,128)(2,1)S(1)}, bf16[400,256]{1,0:T(8,128)(2,1)S(1)}, u32[]{:S(2)}, u32[]{:S(2)}) collective-permute-start(bf16[400,256]{1,0:T(8,128)(2,1)S(1)} %get-tuple-element.50), channel_id=1, source_target_pairs={{0,8},{4,12},{8,0},{12,4},{1,9},{5,13},{9,1},{13,5},{2,10},{6,14},... | collective-permute-start | bytes 614408 | tf_op jit(solution)/shard_map/ppermute | solution.py:359
  8.5 0.5 collective-permute-start.2
  9.0 3.5 %collective-permute-start = (bf16[48,1152]{1,0:T(8,128)(2,1)S(1)}, bf16[48,1152]{1,0:T(8,128)(2,1)S(1)}, u32[]{:S(2)}, u32[]{:S(2)}) collective-permute-start(bf16[48,1152]{1,0:T(8,128)(2,1)S(1)} %get-tuple-element.25), channel_id=1, source_target_pairs={{0,0},{1,1},{2,18},{3,19},{4,36},{5,37},{6,54},{7,55},{8,64},{9,65... | collective-permute-start | bytes 331784 | tf_op jit(solution)/shard_map/ppermute | solution.py:353
  12.5 0.1 collective-permute-start.1
  12.6 1.8 %collective-permute-done.4 = bf16[400,256]{1,0:T(8,128)(2,1)S(1)} collective-permute-done((bf16[400,256]{1,0:T(8,128)(2,1)S(1)}, bf16[400,256]{1,0:T(8,128)(2,1)S(1)}, u32[]{:S(2)}, u32[]{:S(2)}) %collective-permute-start.4) | collective-permute-done | bytes 204832 | tf_op jit(solution)/shard_map/ppermute | solution.py:359
  14.4 3.3 %collective-permute-done.3 = bf16[400,256]{1,0:T(8,128)(2,1)S(1)} collective-permute-done((bf16[400,256]{1,0:T(8,128)(2,1)S(1)}, bf16[400,256]{1,0:T(8,128)(2,1)S(1)}, u32[]{:S(2)}, u32[]{:S(2)}) %collective-permute-start.3) | collective-permute-done | bytes 204832 | tf_op jit(solution)/shard_map/ppermute | solution.py:359
  17.7 0.1 pad_maximum_fusion
  17.8 0.0 copy-start.10
  17.9 0.1 reverse_select_fusion.1
  18.0 0.0 copy-start
  18.0 1.1 reverse_select_fusion
  19.1 1.9 %collective-permute-done.1 = bf16[48,1152]{1,0:T(8,128)(2,1)S(1)} collective-permute-done((bf16[48,1152]{1,0:T(8,128)(2,1)S(1)}, bf16[48,1152]{1,0:T(8,128)(2,1)S(1)}, u32[]{:S(2)}, u32[]{:S(2)}) %collective-permute-start.1) | collective-permute-done | bytes 110624 | tf_op jit(solution)/shard_map/ppermute | solution.py:354
  21.0 1.0 broadcast_in_dim.2
  22.0 10.0 %all-to-all-start = ((bf16[8,48,1152]{2,1,0:T(8,128)(2,1)}), bf16[8,48,1152]{2,1,0:T(8,128)(2,1)S(1)}, u32[]{:S(2)}, u32[]{:S(2)}) async-start(bf16[8,48,1152]{2,1,0:T(8,128)(2,1)} %broadcast_in_dim.2), calls=%async_computation | async-start | bytes 1769472 | tf_op jit(solution)/shard_map/all_to_all | solution.py:300
  32.1 0.5 collective-permute-start.9
  32.6 1.4 %collective-permute-start.8 = (bf16[2,48,1152]{2,1,0:T(8,128)(2,1)S(1)}, bf16[2,48,1152]{2,1,0:T(8,128)(2,1)S(1)}, u32[]{:S(2)}, u32[]{:S(2)}) collective-permute-start(bf16[2,48,1152]{2,1,0:T(8,128)(2,1)S(1)} %pad_maximum_fusion.1.refs_0_), channel_id=1, source_target_pairs={{0,32},{16,48},{32,0},{48,16},{1,33},{17,49},{33,1},{49,17},{2,34}... | collective-permute-start | bytes 663560 | tf_op jit(solution)/shard_map/ppermute | solution.py:368
  34.0 2.3 %collective-permute-start.7 = (bf16[2,48,1152]{2,1,0:T(8,128)(2,1)S(1)}, bf16[2,48,1152]{2,1,0:T(8,128)(2,1)S(1)}, u32[]{:S(2)}, u32[]{:S(2)}) collective-permute-start(bf16[2,48,1152]{2,1,0:T(8,128)(2,1)S(1)} %pad_maximum_fusion.1.refs_0_), channel_id=1, source_target_pairs={{0,16},{16,0},{32,48},{48,32},{1,17},{17,1},{33,49},{49,33},{2,18}... | collective-permute-start | bytes 663560 | tf_op jit(solution)/shard_map/ppermute | solution.py:368
  36.3 0.1 copy.29
  36.4 8.2 %collective-permute-done.9.refs_3_ = bf16[2,48,1152]{2,1,0:T(8,128)(2,1)S(1)} collective-permute-done((bf16[2,48,1152]{2,1,0:T(8,128)(2,1)S(1)}, bf16[2,48,1152]{2,1,0:T(8,128)(2,1)S(1)}, u32[]{:S(2)}, u32[]{:S(2)}) %collective-permute-start.9) | collective-permute-done | bytes 221216 | tf_op jit(solution)/shard_map/ppermute | solution.py:368
  44.6 0.6 collective-permute-done.7.refs_1_
  45.2 1.5 %collective-permute-start.6 = (bf16[4,400,256]{2,1,0:T(8,128)(2,1)}, bf16[4,400,256]{2,1,0:T(8,128)(2,1)}, u32[]{:S(2)}, u32[]{:S(2)}) collective-permute-start(bf16[4,400,256]{2,1,0:T(8,128)(2,1)} %bitcast.49), channel_id=1, source_target_pairs={{0,2},{2,0},{1,3},{3,1},{4,6},{6,4},{5,7},{7,5},{8,10},{10,8},{9,1... | collective-permute-start | bytes 2457608 | tf_op jit(solution)/shard_map/ppermute | solution.py:374
  46.7 0.2 collective-permute-start.5
  46.9 0.1 dynamic-slice_bitcast_fusion.3
  47.0 0.1 copy.30.refs_8_
  47.1 0.1 dynamic-slice_bitcast_fusion.4.refs_7_
  47.2 0.1 pad_add_fusion.at_ref
  47.3 0.4 collective-permute-done.10.refs_5_
  47.7 7.5 %pair.1 = (bf16[32,64,128]{2,1,0:T(8,128)(2,1)}, bf16[32,8,16,128]{3,2,1,0:T(8,128)(2,1)}, f32[8,384]{1,0:T(8,128)S(1)}) custom-call(s32[2]{0:T(128)S(1)} %pad_add_fusion.at_ref, bf16[2,48,1152]{2,1,0:T(8,128)(2,1)S(1)} %pad_maximum_fusion.1.refs_0_, bf16[2,48,1152]{2,1,0:T(8,128)(2,1)S(1)} %collective-permute-done.7.refs_1_, ...), custom_call_target="tpu_custom_call" | custom-call | flops 1000 | bytes 1000 | tf_op jit(solution)/shard_map/pair/pallas_call | solution.py:383
  55.2 6.2 %all-to-all-start.1 = ((bf16[32,8,16,128]{3,2,1,0:T(8,128)(2,1)}), bf16[32,8,16,128]{3,2,1,0:T(8,128)(2,1)S(1)}, u32[]{:S(2)}, u32[]{:S(2)}) async-start(bf16[32,8,16,128]{3,2,1,0:T(8,128)(2,1)} %get-tuple-element.37), calls=%async_computation.1 | async-start | bytes 2097152 | tf_op jit(solution)/shard_map/all_to_all | solution.py:446
  61.4 5.2 %collective-permute-done.6.refs_2_.refs_6_ = bf16[4,400,256]{2,1,0:T(8,128)(2,1)} collective-permute-done((bf16[4,400,256]{2,1,0:T(8,128)(2,1)}, bf16[4,400,256]{2,1,0:T(8,128)(2,1)}, u32[]{:S(2)}, u32[]{:S(2)}) %collective-permute-start.6) | collective-permute-done | bytes 819232 | tf_op jit(solution)/shard_map/ppermute | solution.py:374
  66.6 0.1 pad_add_fusion.1.at_ref
  66.7 2.5 %collective-permute-done.11.refs_3_.refs_7_ = bf16[4,400,256]{2,1,0:T(8,128)(2,1)S(1)} collective-permute-done((bf16[4,400,256]{2,1,0:T(8,128)(2,1)}, bf16[4,400,256]{2,1,0:T(8,128)(2,1)S(1)}, u32[]{:S(2)}, u32[]{:S(2)}) %collective-permute-start.11) | collective-permute-done | bytes 819232 | tf_op jit(solution)/shard_map/ppermute | solution.py:414
  69.1 0.9 copy-done.8
  70.1 8.8 %ready.1 = (bf16[12,256,128]{2,1,0:T(8,128)(2,1)}, bf16[12,512,256]{2,1,0:T(8,128)(2,1)}, bf16[12,256,512]{2,1,0:T(8,128)(2,1)}, f32[12,256,128]{2,1,0:T(8,128)}, bf16[512,128]{1,0:T(8,128)(2,1)}) custom-call(s32[2]{0:T(128)S(1)} %pad_add_fusion.1.at_ref, bf16[4,400,256]{2,1,0:T(8,128)(2,1)} %bitcast.51, ...), custom_call_target="tpu_custom_call" | custom-call | flops 1000 | bytes 1000 | tf_op jit(solution)/shard_map/ready/pallas_call | solution.py:418
  78.8 1.0 all-to-all-done.1
  79.8 12.9 %rows.1 = bf16[12,128,256]{2,1,0:T(8,128)(2,1)S(1)} custom-call(bf16[4,400,256]{2,1,0:T(8,128)(2,1)} %bitcast.53, bf16[12,256,128]{2,1,0:T(8,128)(2,1)} %get-tuple-element.41.query_ref, bf16[12,512,256]{2,1,0:T(8,128)(2,1)} %get-tuple-element.42.key_ref, bf16[12,256,512]{2,1,0:T(8,128)(2,1)} %get-tuple-element.43.value_ref, ...), custom_call_target="tpu_custom_call" | custom-call | flops 8000000000 | bytes 12000000 | tf_op jit(solution)/shard_map/rows/pallas_call | solution.py:450
  92.7 0.0 copy-start.3
  92.8 0.2 reshape.48
  93.0 0.3 copy.31
  93.3 21.0 %all_to_all.20 = bf16[32,12,4,256]{3,2,1,0:T(4,128)(2,1)S(1)} all-to-all(bf16[32,12,4,256]{3,2,1,0:T(4,128)(2,1)S(1)} %bitcast.56), channel_id=1, replica_groups=mesh['yh'=2,'z'=4,'yl'=2,'xh'=2,'xl'=2,'core'=2] {'yh','z','yl','xh'}, dimensions={0} | all-to-all | bytes 1572864 | tf_op jit(solution)/shard_map/all_to_all | solution.py:467
  114.3 0.1 copy.40
  114.4 7.4 %columns.1 = bf16[4,384,256]{2,1,0:T(8,128)(2,1)S(1)} custom-call(bf16[4,384,256]{2,1,0:T(8,128)(2,1)S(1)} %bitcast.45, f32[8,384]{1,0:T(8,128)S(1)} %get-tuple-element.46.mask_ref, bf16[256,256]{1,0:T(8,128)(2,1)S(1)} %copy-done.3, bf16[256,256]{1,0:T(8,128)(2,1)S(1)} %copy-done.4, bf16[256,256]{1,0:T(8,128)(2,1)S(1)} %copy-done.5, ...), custom_call_target="tpu_custom_call" | custom-call | flops 8000000000 | bytes 2000000 | tf_op jit(solution)/shard_map/columns/pallas_call | solution.py:471
  121.9 0.1 copy.39
  122.0 14.8 %all_to_all.21 = bf16[8,4,48,256]{3,2,1,0:T(8,128)(2,1)S(1)} all-to-all(bf16[8,4,48,256]{3,2,1,0:T(8,128)(2,1)S(1)} %bitcast.58), channel_id=1, replica_groups=mesh['yh'=2,'z'=4,'yl'=2,'xh'=2,'xl'=2,'core'=2] {'yh','z'}, dimensions={0} | all-to-all | bytes 1572864 | tf_op jit(solution)/shard_map/all_to_all | solution.py:500
  136.7 1.1 copy.38
  (27 shorter events, 0.1 us)
Async XLA Ops:
  3.9 10.5 %collective-permute-start.4 = (bf16[400,256]{1,0:T(8,128)(2,1)S(1)}, bf16[400,256]{1,0:T(8,128)(2,1)S(1)}, u32[]{:S(2)}, u32[]{:S(2)}) collective-permute-start(bf16[400,256]{1,0:T(8,128)(2,1)S(1)} %get-tuple-element.49), channel_id=1, source_target_pairs={{0,12},{4,8},{8,4},{12,0},{1,13},{5,9},{9,5},{13,1},{2,14},{6,10},... | collective-permute-start | bytes 614408 | tf_op jit(solution)/shard_map/ppermute | solution.py:359
  6.9 10.8 %collective-permute-start.3 = (bf16[400,256]{1,0:T(8,128)(2,1)S(1)}, bf16[400,256]{1,0:T(8,128)(2,1)S(1)}, u32[]{:S(2)}, u32[]{:S(2)}) collective-permute-start(bf16[400,256]{1,0:T(8,128)(2,1)S(1)} %get-tuple-element.50), channel_id=1, source_target_pairs={{0,8},{4,12},{8,0},{12,4},{1,9},{5,13},{9,1},{13,5},{2,10},{6,14},... | collective-permute-start | bytes 614408 | tf_op jit(solution)/shard_map/ppermute | solution.py:359
  8.5 9.2 %collective-permute-start.2 = (bf16[400,256]{1,0:T(8,128)(2,1)S(1)}, bf16[400,256]{1,0:T(8,128)(2,1)S(1)}, u32[]{:S(2)}, u32[]{:S(2)}) collective-permute-start(bf16[400,256]{1,0:T(8,128)(2,1)S(1)} %get-tuple-element.51), channel_id=1, source_target_pairs={{0,4},{4,0},{8,12},{12,8},{1,5},{5,1},{9,13},{13,9},{2,6},{6,2},{1... | collective-permute-start | bytes 614408 | tf_op jit(solution)/shard_map/ppermute | solution.py:359
  9.0 10.1 %collective-permute-start = (bf16[48,1152]{1,0:T(8,128)(2,1)S(1)}, bf16[48,1152]{1,0:T(8,128)(2,1)S(1)}, u32[]{:S(2)}, u32[]{:S(2)}) collective-permute-start(bf16[48,1152]{1,0:T(8,128)(2,1)S(1)} %get-tuple-element.25), channel_id=1, source_target_pairs={{0,0},{1,1},{2,18},{3,19},{4,36},{5,37},{6,54},{7,55},{8,64},{9,65... | collective-permute-start | bytes 331784 | tf_op jit(solution)/shard_map/ppermute | solution.py:353
  12.5 8.5 %collective-permute-start.1 = (bf16[48,1152]{1,0:T(8,128)(2,1)S(1)}, bf16[48,1152]{1,0:T(8,128)(2,1)S(1)}, u32[]{:S(2)}, u32[]{:S(2)}) collective-permute-start(bf16[48,1152]{1,0:T(8,128)(2,1)S(1)} %get-tuple-element.26), channel_id=1, source_target_pairs={{0,64},{64,0},{1,65},{65,1},{2,66},{66,2},{3,67},{67,3},{4,68},{68... | collective-permute-start | bytes 331784 | tf_op jit(solution)/shard_map/ppermute | solution.py:354
  17.8 18.4 %copy-start.9 = (bf16[1024,128]{1,0:T(8,128)(2,1)S(1)}, bf16[1024,128]{1,0:T(8,128)(2,1)}, u32[]{:S(2)}) copy-start(bf16[1024,128]{1,0:T(8,128)(2,1)} %param.24) | copy-start | bytes 786436
  17.8 29.1 %copy-start.10 = (s32[512]{0:T(512)S(1)}, s32[512]{0:T(512)}, u32[]{:S(2)}) copy-start(s32[512]{0:T(512)} %param.20) | copy-start | bytes 6148
  18.0 29.7 %copy-start = (bf16[32,64,128]{2,1,0:T(8,128)(2,1)S(1)}, bf16[32,64,128]{2,1,0:T(8,128)(2,1)}, u32[]{:S(2)}) copy-start(bf16[32,64,128]{2,1,0:T(8,128)(2,1)} %refs_6_.1) | copy-start | bytes 1572868
  18.0 29.6 %copy-start.1 = (bf16[128,8]{0,1:T(8,128)(2,1)S(1)}, bf16[128,8]{0,1:T(8,128)(2,1)}, u32[]{:S(2)}) copy-start(bf16[128,8]{0,1:T(8,128)(2,1)} %param.25) | copy-start | bytes 6148
  22.0 23.2 %all-to-all-start = ((bf16[8,48,1152]{2,1,0:T(8,128)(2,1)}), bf16[8,48,1152]{2,1,0:T(8,128)(2,1)S(1)}, u32[]{:S(2)}, u32[]{:S(2)}) async-start(bf16[8,48,1152]{2,1,0:T(8,128)(2,1)} %broadcast_in_dim.2), calls=%async_computation | async-start | bytes 1769472 | tf_op jit(solution)/shard_map/all_to_all | solution.py:300
  32.1 12.5 %collective-permute-start.9 = (bf16[2,48,1152]{2,1,0:T(8,128)(2,1)S(1)}, bf16[2,48,1152]{2,1,0:T(8,128)(2,1)S(1)}, u32[]{:S(2)}, u32[]{:S(2)}) collective-permute-start(bf16[2,48,1152]{2,1,0:T(8,128)(2,1)S(1)} %pad_maximum_fusion.1.refs_0_), channel_id=1, source_target_pairs={{0,48},{16,32},{32,16},{48,0},{1,49},{17,33},{33,17},{49,1},{2,50}... | collective-permute-start | bytes 663560 | tf_op jit(solution)/shard_map/ppermute | solution.py:368
  32.6 12.0 %collective-permute-start.8 = (bf16[2,48,1152]{2,1,0:T(8,128)(2,1)S(1)}, bf16[2,48,1152]{2,1,0:T(8,128)(2,1)S(1)}, u32[]{:S(2)}, u32[]{:S(2)}) collective-permute-start(bf16[2,48,1152]{2,1,0:T(8,128)(2,1)S(1)} %pad_maximum_fusion.1.refs_0_), channel_id=1, source_target_pairs={{0,32},{16,48},{32,0},{48,16},{1,33},{17,49},{33,1},{49,17},{2,34}... | collective-permute-start | bytes 663560 | tf_op jit(solution)/shard_map/ppermute | solution.py:368
  34.0 11.2 %collective-permute-start.7 = (bf16[2,48,1152]{2,1,0:T(8,128)(2,1)S(1)}, bf16[2,48,1152]{2,1,0:T(8,128)(2,1)S(1)}, u32[]{:S(2)}, u32[]{:S(2)}) collective-permute-start(bf16[2,48,1152]{2,1,0:T(8,128)(2,1)S(1)} %pad_maximum_fusion.1.refs_0_), channel_id=1, source_target_pairs={{0,16},{16,0},{32,48},{48,32},{1,17},{17,1},{33,49},{49,33},{2,18}... | collective-permute-start | bytes 663560 | tf_op jit(solution)/shard_map/ppermute | solution.py:368
  45.2 2.4 %collective-permute-start.10 = (bf16[8,48,1152]{2,1,0:T(8,128)(2,1)S(1)}, bf16[8,48,1152]{2,1,0:T(8,128)(2,1)S(1)}, u32[]{:S(2)}, u32[]{:S(2)}) collective-permute-start(bf16[8,48,1152]{2,1,0:T(8,128)(2,1)S(1)} %all-to-all-done.refs_4_), channel_id=1, source_target_pairs={{0,1},{1,0},{2,3},{3,2},{4,5},{5,4},{6,7},{7,6},{8,9},{9,8},{10,11... | collective-permute-start | bytes 2654216 | tf_op jit(solution)/shard_map/ppermute | solution.py:373
  45.2 21.4 %collective-permute-start.6 = (bf16[4,400,256]{2,1,0:T(8,128)(2,1)}, bf16[4,400,256]{2,1,0:T(8,128)(2,1)}, u32[]{:S(2)}, u32[]{:S(2)}) collective-permute-start(bf16[4,400,256]{2,1,0:T(8,128)(2,1)} %bitcast.49), channel_id=1, source_target_pairs={{0,2},{2,0},{1,3},{3,1},{4,6},{6,4},{5,7},{7,5},{8,10},{10,8},{9,1... | collective-permute-start | bytes 2457608 | tf_op jit(solution)/shard_map/ppermute | solution.py:374
  46.7 19.9 %collective-permute-start.5 = (bf16[4,400,256]{2,1,0:T(8,128)(2,1)}, bf16[4,400,256]{2,1,0:T(8,128)(2,1)}, u32[]{:S(2)}, u32[]{:S(2)}) collective-permute-start(bf16[4,400,256]{2,1,0:T(8,128)(2,1)} %bitcast.50), channel_id=1, source_target_pairs={{0,1},{1,0},{2,3},{3,2},{4,5},{5,4},{6,7},{7,6},{8,9},{9,8},{10,11... | collective-permute-start | bytes 2457608 | tf_op jit(solution)/shard_map/ppermute | solution.py:375
  55.2 24.6 %all-to-all-start.1 = ((bf16[32,8,16,128]{3,2,1,0:T(8,128)(2,1)}), bf16[32,8,16,128]{3,2,1,0:T(8,128)(2,1)S(1)}, u32[]{:S(2)}, u32[]{:S(2)}) async-start(bf16[32,8,16,128]{3,2,1,0:T(8,128)(2,1)} %get-tuple-element.37), calls=%async_computation.1 | async-start | bytes 2097152 | tf_op jit(solution)/shard_map/all_to_all | solution.py:446
  66.6 2.5 %collective-permute-start.11 = (bf16[4,400,256]{2,1,0:T(8,128)(2,1)}, bf16[4,400,256]{2,1,0:T(8,128)(2,1)S(1)}, u32[]{:S(2)}, u32[]{:S(2)}) collective-permute-start(bf16[4,400,256]{2,1,0:T(8,128)(2,1)} %collective-permute-done.6.refs_2_.refs_6_), channel_id=1, source_target_pairs={{0,1},{1,0},{2,3},{3,2},{4,5},{5,4},{6,7},{7,6},{8,9},{9,8},{10,11... | collective-permute-start | bytes 2457608 | tf_op jit(solution)/shard_map/ppermute | solution.py:414
  66.7 13.2 %copy-start.2 = (bf16[256,256]{1,0:T(8,128)(2,1)S(1)}, bf16[256,256]{1,0:T(8,128)(2,1)}, u32[]{:S(2)}) copy-start(bf16[256,256]{1,0:T(8,128)(2,1)} %wo_ref.2) | copy-start | bytes 393220
  69.1 0.9 copy-start.8
  92.7 21.7 %copy-start.3 = (bf16[256,256]{1,0:T(8,128)(2,1)S(1)}, bf16[256,256]{1,0:T(8,128)(2,1)}, u32[]{:S(2)}) copy-start(bf16[256,256]{1,0:T(8,128)(2,1)} %wq_ref.1) | copy-start | bytes 393220
  92.8 21.6 %copy-start.4 = (bf16[256,256]{1,0:T(8,128)(2,1)S(1)}, bf16[256,256]{1,0:T(8,128)(2,1)}, u32[]{:S(2)}) copy-start(bf16[256,256]{1,0:T(8,128)(2,1)} %wk_ref.1) | copy-start | bytes 393220
  92.8 21.6 %copy-start.5 = (bf16[256,256]{1,0:T(8,128)(2,1)S(1)}, bf16[256,256]{1,0:T(8,128)(2,1)}, u32[]{:S(2)}) copy-start(bf16[256,256]{1,0:T(8,128)(2,1)} %wv_ref.1) | copy-start | bytes 393220
  92.8 21.6 %copy-start.6 = (bf16[256,256]{1,0:T(8,128)(2,1)S(1)}, bf16[256,256]{1,0:T(8,128)(2,1)}, u32[]{:S(2)}) copy-start(bf16[256,256]{1,0:T(8,128)(2,1)} %wg_ref.1) | copy-start | bytes 393220
  92.8 21.6 %copy-start.7 = (bf16[256,256]{1,0:T(8,128)(2,1)S(1)}, bf16[256,256]{1,0:T(8,128)(2,1)}, u32[]{:S(2)}) copy-start(bf16[256,256]{1,0:T(8,128)(2,1)} %wo_ref.3) | copy-start | bytes 393220

commit v4 on v3

--- a/solution.py
+++ b/solution.py
@@ -101,9 +101,7 @@
     return jnp.where(top, jnp.broadcast_to(mask_row, shape), 0.0).astype(BF16).T
 
 
-def factor_kernel(
-    x_ref, mask_ref, source_ref, target_ref, left_ref, right_ref, packed_ref, lefts, rights
-):
+def factor_kernel(x_ref, mask_ref, source_ref, target_ref, left_ref, right_ref, lefts, rights):
     ln = normalize(x_ref[...].reshape(1536, 256))
     mask = mask_ref[...].astype(F32).T
     lefts[:, :32] = lax.dot_general(ln, source_ref[...], NT, preferred_element_type=F32)
@@ -122,11 +120,6 @@
     tail = jnp.concatenate([mask, jnp.zeros((48, 96), F32)], axis=1).astype(BF16)
     left_ref[:, 1024:] = tail
     right_ref[:, 1024:] = tail
-    for u in range(4):
-        packed_ref[u, :384] = x_ref[u * 12 : (u + 1) * 12].reshape(384, 256)
-        flags = jnp.concatenate([mask[u * 12 : (u + 1) * 12], jnp.zeros((4, 32), F32)], axis=0)
-        flags = jnp.concatenate([flags, jnp.zeros((16, 224), F32)], axis=1)
-        packed_ref[u, 384:] = flags.astype(BF16)
 
 
 def pair_kernel(at_ref, *refs):
@@ -157,19 +150,16 @@
     factor = cols_ref[...] * rows_ref[...] / (count + 0.001)
     offset = offset_ref[...]
     def outer_of(block):
-        left = left_all[:, block * 512 : (block + 1) * 512]
+        left = left_all[:, block * 1024 : (block + 1) * 1024]
         return [
             lax.dot_general(left, r[:, :1024], TN, preferred_element_type=F32).astype(BF16)
             for r in right
         ]
 
-    ahead = outer_of(0)
-    for block in range(2):
-        outer = ahead
-        if block < 1:
-            ahead = outer_of(block + 1)
+    for block in range(1):
+        outer = outer_of(block)
         turned = []
-        for i in range(16):
+        for i in range(32):
             for p in range(2):
                 rows = outer[p][i * 32 : (i + 1) * 32]
                 tiles = [rows[:, t * 128 : (t + 1) * 128] for t in range(8)]
@@ -179,8 +169,8 @@
             lhs = jnp.concatenate([t[e * 32 : (e + 1) * 32] for t in turned], axis=0)
             part = project(lhs, final_ref[e])
             terms = part if terms is None else terms + part
-        for i in range(16):
-            at = block * 16 + i
+        for i in range(32):
+            at = block * 32 + i
             sums = terms[i * 64 : (i + 1) * 64]
             fresh = pair_ref[at].astype(F32) + factor[:, at : at + 1] * sums
             fresh = fresh.astype(BF16)
@@ -212,25 +202,18 @@
                 columns[u, a, b, :, :16] = absent[:32]
         mask_ref[...] = columns[...].reshape(512, 128).astype(BF16)
 
-    asked = []
     for t in range(STEP):
         rows = slice(t * 32, (t + 1) * 32)
-        asked.append(normalize(x_ref[:, rows].reshape(128, 256)))
-        ordered[t, :, xl, core] = asked[t].reshape(4, 32, 256)
+        asked = normalize(x_ref[:, rows].reshape(128, 256))
+        ordered[t, :, xl, core] = asked.reshape(4, 32, 256)
         ordered[t, :, xl, 1 - core] = normalize(xc_ref[:, rows])
         ordered[t, :, 1 - xl, core] = normalize(xx_ref[:, rows])
         ordered[t, :, 1 - xl, 1 - core] = normalize(xxc_ref[:, rows])
-    keys = ordered[...].reshape(STEP * 512, 256)
-    both = project(keys, jnp.concatenate([wk_ref[...], wv_ref[...]], axis=1))
-    asking = jnp.concatenate([wq_ref[...], wg_ref[...]], axis=1)
-    asks = project(jnp.concatenate(asked, axis=0), asking)
-    for t in range(STEP):
-        own = asks[t * 128 : (t + 1) * 128]
-        query_ref[t] = (own[:, :256] * (HEAD**-0.5 * LOG2E)).T.astype(BF16)
-        gate_ref[t] = jax.nn.sigmoid(own[:, 256:]).T
-        rows = slice(t * 512, (t + 1) * 512)
-        key_ref[t] = both[rows, :256].astype(BF16)
-        value_ref[t] = both[rows, 256:].astype(BF16).T
+        keys = ordered[t].reshape(512, 256)
+        query_ref[t] = (project(asked, wq_ref[...]) * (HEAD**-0.5 * LOG2E)).T.astype(BF16)
+        key_ref[t] = project(keys, wk_ref[...]).astype(BF16)
+        value_ref[t] = project(keys, wv_ref[...]).astype(BF16).T
+        gate_ref[t] = jax.nn.sigmoid(project(asked, wg_ref[...])).T
 
 
 def row_kernel(
@@ -329,11 +312,23 @@
     res_at = lax.axis_index(RES)
     xl_at = lax.axis_index("xl")
     core_at = lax.axis_index("core")
-
-    left, right, packed = pl.pallas_call(
+    mask = entry_exists_flags.astype(BF16)
+
+    tail = jnp.pad(mask.reshape(4, 12, 32), ((0, 0), (0, 4), (0, 224)))
+    packed = jnp.concatenate([homolog_stack.reshape(4, 384, 256), tail], axis=1)
+    team_at = lax.axis_index(TEAM)
+    parts = []
+    for k in range(4):
+        part = lax.dynamic_index_in_dim(packed, team_at ^ k, 0, False)
+        parts.append(lax.ppermute(part, TEAM, [(t, t ^ k) for t in range(4)]) if k else part)
+    packed = jnp.stack(parts).reshape(2, 2, 400, 256)
+    packed = jnp.where(lax.axis_index("yl") == 1, packed[::-1], packed)
+    packed = jnp.where(lax.axis_index("xh") == 1, packed[:, ::-1], packed)
+    packed = packed.reshape(4, 400, 256)
+
+    left, right = pl.pallas_call(
         factor_kernel,
-        out_shape=[jax.ShapeDtypeStruct((48, 1152), BF16)] * 2
-        + [jax.ShapeDtypeStruct((4, 400, 256), BF16)],
+        out_shape=[jax.ShapeDtypeStruct((48, 1152), BF16)] * 2,
         scratch_shapes=[pltpu.VMEM((1536, 128), F32)] * 2,
         compiler_params=pltpu.CompilerParams(vmem_limit_bytes=VMEM_LIMIT),
         name="factors",
@@ -352,15 +347,6 @@
     pairs = [(0, 1), (1, 0)]
     right = lax.ppermute(right, ALL, swap)
     left_yh = lax.ppermute(left, "yh", pairs)
-    team_at = lax.axis_index(TEAM)
-    parts = []
-    for k in range(4):
-        part = lax.dynamic_index_in_dim(packed, team_at ^ k, 0, False)
-        parts.append(lax.ppermute(part, TEAM, [(t, t ^ k) for t in range(4)]) if k else part)
-    packed = jnp.stack(parts).reshape(2, 2, 400, 256)
-    packed = jnp.where(lax.axis_index("yl") == 1, packed[::-1], packed)
-    packed = jnp.where(lax.axis_index("xh") == 1, packed[:, ::-1], packed)
-    packed = packed.reshape(4, 400, 256)
     right, left_yh, packed = lax.optimization_barrier((right, left_yh, packed))
     mine = spread(right, ("yl", "xh", "xl"), 8)
     left = jnp.stack([left, left_yh])
@@ -412,7 +398,7 @@
 
     packed, packed_c, packed_x, _ = lax.optimization_barrier((packed, packed_c, packed_x, bias))
     packed_xc = lax.ppermute(packed_x, "core", pairs)
-    pieces = [in_hbm(p) for p in (packed, packed_c, packed_x, packed_xc)]
+    pieces = [in_hbm(p) for p in (packed, packed_c, packed_x)] + [packed_xc]
     by_row = [(12, 256, 128), (12, 512, 256), (12, 256, 512), (12, 256, 128)]
     specs = [pl.BlockSpec((STEP,) + shape[1:], lambda t: (t, 0, 0)) for shape in by_row]
     rows_in = pl.pallas_call(

time: 139 us -> 138 us (level)
  other arithmetic: 1.48 us -> 3.41 us
  blocking collectives: 35.8 us -> 34.2 us
    ppermute x3, waiting for transfers between devices: 5.14 us -> 1.85 us  [body(): lax.ppermute(part, TEAM, [(t, t ^ k) for t in range(4)])]
    all_to_all x1, waiting for transfers between devices: 0.98 us -> 4.12 us  [body(): bias = lax.all_to_all(bias, PLANE, split_axis=0, concat_axis=0, tiled=True)]
    all_to_all x1, blocking collectives: 21 us -> 19.4 us  [body(): lax.all_to_all(middle.reshape(32, 12, 4, 256), PLANE, split_axis=0, conca...]
    all_to_all x1, starting transfers between devices: 6.18 us -> 7.66 us  [body(): bias = lax.all_to_all(bias, PLANE, split_axis=0, concat_axis=0, tiled=True)]
  transfers between devices with their start and end apart: 14 -> 14, of which waited for: 9 -> 9; matrix products, arithmetic and copies ran while one was open for 1% -> 1% of each run, Pallas kernels for 12% -> 13%
where the time goes in v4:
time: 138 us; the launch traced here: 136 us
  Pallas kernels  38.6 us (28%)
  blocking collectives  34.2 us (25%)
  starting transfers between devices  31.4 us (23%)
  waiting for transfers between devices  24.3 us (18%)
  other arithmetic  3.41 us (2%)
  local copies, waits for them, and re-layouts  3.33 us (2%)
    all_to_all x1, blocking collectives, body(): lax.all_to_all(middle.reshape(32, 12, 4, 256), PLANE, split_axis=0, conca...  19.4 us
    all_to_all x1, blocking collectives, body(): lax.all_to_all(columns, SEQ, split_axis=0, concat_axis=0, tiled=True)  14.8 us
    pallas_call x1, Pallas kernels, body(): pl.pallas_call(row_kernel, out_shape=jax.ShapeDtypeStruct((12, 128, 256),...  12.9 us
    all_to_all x1, starting transfers between devices, spread(): return lax.all_to_all(wide, axes, split_axis=0, concat_axis=0, tiled=True)  9.2 us
    pallas_call x1, Pallas kernels, body(): pl.pallas_call(ready_kernel, out_shape=[pltpu.HBM(shape, kind) for shape,...  8.29 us
    ppermute x3, waiting for transfers between devices, body(): lax.ppermute(left, 'z', [(z, z ^ k) for z in range(4)])  7.93 us
    all_to_all x1, starting transfers between devices, body(): bias = lax.all_to_all(bias, PLANE, split_axis=0, concat_axis=0, tiled=True)  7.66 us
    pallas_call x1, Pallas kernels, body(): pl.pallas_call(column_kernel, out_shape=jax.ShapeDtypeStruct((4, 384, 256...  7.44 us
  transfers between devices with their start and end apart: 14, of which 9 were waited for; matrix products, arithmetic and copies ran while one was open for 1% of the time, Pallas kernels for 13%

profile of v4, /device:TPU:8, one launch (start us, length us, event | category | flops | bytes accessed | tf_op | source)
XLA Modules:
  0.0 136.1 jit_solution(11008916346064164967)
XLA Ops:
  0.7 0.7 convert_element_type.8
  1.4 0.1 copy.31
  1.5 1.2 fusion.1
  2.7 0.1 constant_dynamic-slice_fusion
  2.8 3.0 %collective-permute-start.4 = (bf16[400,256]{1,0:T(8,128)(2,1)S(1)}, bf16[400,256]{1,0:T(8,128)(2,1)S(1)}, u32[]{:S(2)}, u32[]{:S(2)}) collective-permute-start(bf16[400,256]{1,0:T(8,128)(2,1)S(1)} %get-tuple-element.47), channel_id=1, source_target_pairs={{0,12},{4,8},{8,4},{12,0},{1,13},{5,9},{9,5},{13,1},{2,14},{6,10},... | collective-permute-start | bytes 614408 | tf_op jit(solution)/shard_map/ppermute | solution.py:323
  5.8 1.6 %collective-permute-start.3 = (bf16[400,256]{1,0:T(8,128)(2,1)S(1)}, bf16[400,256]{1,0:T(8,128)(2,1)S(1)}, u32[]{:S(2)}, u32[]{:S(2)}) collective-permute-start(bf16[400,256]{1,0:T(8,128)(2,1)S(1)} %get-tuple-element.48), channel_id=1, source_target_pairs={{0,8},{4,12},{8,0},{12,4},{1,9},{5,13},{9,1},{13,5},{2,10},{6,14},... | collective-permute-start | bytes 614408 | tf_op jit(solution)/shard_map/ppermute | solution.py:323
  7.3 0.5 collective-permute-start.2
  7.9 3.2 %factors.1 = (bf16[48,1152]{1,0:T(8,128)(2,1)S(1)}, bf16[48,1152]{1,0:T(8,128)(2,1)S(1)}) custom-call(bf16[48,32,256]{2,1,0:T(8,128)(2,1)} %x_ref.1, s32[32,48]{1,0:T(8,128)} %bitcast.68, bf16[32,256]{1,0:T(8,128)(2,1)} %bitcast.69, bf16[32,256]{1,0:T(8,128)(2,1)} %bitcast.70), custom_call_target="tpu_custom_call" | custom-call | tf_op jit(solution)/shard_map/factors/pallas_call | solution.py:329
  11.0 3.5 %collective-permute-start = (bf16[48,1152]{1,0:T(8,128)(2,1)S(1)}, bf16[48,1152]{1,0:T(8,128)(2,1)S(1)}, u32[]{:S(2)}, u32[]{:S(2)}) collective-permute-start(bf16[48,1152]{1,0:T(8,128)(2,1)S(1)} %get-tuple-element.24), channel_id=1, source_target_pairs={{0,0},{1,1},{2,18},{3,19},{4,36},{5,37},{6,54},{7,55},{8,64},{9,65... | collective-permute-start | bytes 331784 | tf_op jit(solution)/shard_map/ppermute | solution.py:348
  14.5 0.1 collective-permute-start.1
  14.6 1.8 %collective-permute-done.3 = bf16[400,256]{1,0:T(8,128)(2,1)S(1)} collective-permute-done((bf16[400,256]{1,0:T(8,128)(2,1)S(1)}, bf16[400,256]{1,0:T(8,128)(2,1)S(1)}, u32[]{:S(2)}, u32[]{:S(2)}) %collective-permute-start.3) | collective-permute-done | bytes 204832 | tf_op jit(solution)/shard_map/ppermute | solution.py:323
  16.5 0.1 pad_maximum_fusion
  16.6 0.2 reverse_select_fusion.1
  16.8 1.0 reverse_select_fusion
  17.8 1.1 collective-permute-done
  18.9 2.0 %collective-permute-done.1 = bf16[48,1152]{1,0:T(8,128)(2,1)S(1)} collective-permute-done((bf16[48,1152]{1,0:T(8,128)(2,1)S(1)}, bf16[48,1152]{1,0:T(8,128)(2,1)S(1)}, u32[]{:S(2)}, u32[]{:S(2)}) %collective-permute-start.1) | collective-permute-done | bytes 110624 | tf_op jit(solution)/shard_map/ppermute | solution.py:349
  20.9 1.0 broadcast_in_dim.2
  21.9 9.2 %all-to-all-start = ((bf16[8,48,1152]{2,1,0:T(8,128)(2,1)}), bf16[8,48,1152]{2,1,0:T(8,128)(2,1)S(1)}, u32[]{:S(2)}, u32[]{:S(2)}) async-start(bf16[8,48,1152]{2,1,0:T(8,128)(2,1)} %broadcast_in_dim.2), calls=%async_computation | async-start | bytes 1769472 | tf_op jit(solution)/shard_map/all_to_all | solution.py:283
  31.1 1.4 %collective-permute-start.9 = (bf16[2,48,1152]{2,1,0:T(8,128)(2,1)S(1)}, bf16[2,48,1152]{2,1,0:T(8,128)(2,1)S(1)}, u32[]{:S(2)}, u32[]{:S(2)}) collective-permute-start(bf16[2,48,1152]{2,1,0:T(8,128)(2,1)S(1)} %pad_maximum_fusion.1.refs_0_), channel_id=1, source_target_pairs={{0,48},{16,32},{32,16},{48,0},{1,49},{17,33},{33,17},{49,1},{2,50}... | collective-permute-start | bytes 663560 | tf_op jit(solution)/shard_map/ppermute | solution.py:354
  32.5 1.4 %collective-permute-start.8 = (bf16[2,48,1152]{2,1,0:T(8,128)(2,1)S(1)}, bf16[2,48,1152]{2,1,0:T(8,128)(2,1)S(1)}, u32[]{:S(2)}, u32[]{:S(2)}) collective-permute-start(bf16[2,48,1152]{2,1,0:T(8,128)(2,1)S(1)} %pad_maximum_fusion.1.refs_0_), channel_id=1, source_target_pairs={{0,32},{16,48},{32,0},{48,16},{1,33},{17,49},{33,1},{49,17},{2,34}... | collective-permute-start | bytes 663560 | tf_op jit(solution)/shard_map/ppermute | solution.py:354
  33.9 1.4 collective-permute-start.7
  35.3 0.1 copy.32
  35.4 7.3 %collective-permute-done.9.refs_3_ = bf16[2,48,1152]{2,1,0:T(8,128)(2,1)S(1)} collective-permute-done((bf16[2,48,1152]{2,1,0:T(8,128)(2,1)S(1)}, bf16[2,48,1152]{2,1,0:T(8,128)(2,1)S(1)}, u32[]{:S(2)}, u32[]{:S(2)}) %collective-permute-start.9) | collective-permute-done | bytes 221216 | tf_op jit(solution)/shard_map/ppermute | solution.py:354
  42.7 0.6 collective-permute-done.7.refs_1_
  43.3 1.5 %collective-permute-start.6 = (bf16[4,400,256]{2,1,0:T(8,128)(2,1)}, bf16[4,400,256]{2,1,0:T(8,128)(2,1)}, u32[]{:S(2)}, u32[]{:S(2)}) collective-permute-start(bf16[4,400,256]{2,1,0:T(8,128)(2,1)} %bitcast.50), channel_id=1, source_target_pairs={{0,2},{2,0},{1,3},{3,1},{4,6},{6,4},{5,7},{7,5},{8,10},{10,8},{9,1... | collective-permute-start | bytes 2457608 | tf_op jit(solution)/shard_map/ppermute | solution.py:360
  44.8 0.2 collective-permute-start.5
  45.0 0.1 dynamic-slice_bitcast_fusion.3
  45.1 0.1 copy.33.refs_8_
  45.2 0.1 dynamic-slice_bitcast_fusion.4.refs_7_
  45.3 0.1 pad_add_fusion.at_ref
  45.3 0.4 collective-permute-done.10.refs_5_
  45.7 6.8 %pair.1 = (bf16[32,64,128]{2,1,0:T(8,128)(2,1)}, bf16[32,8,16,128]{3,2,1,0:T(8,128)(2,1)}, f32[8,384]{1,0:T(8,128)S(1)}) custom-call(s32[2]{0:T(128)S(1)} %pad_add_fusion.at_ref, bf16[2,48,1152]{2,1,0:T(8,128)(2,1)S(1)} %pad_maximum_fusion.1.refs_0_, bf16[2,48,1152]{2,1,0:T(8,128)(2,1)S(1)} %collective-permute-done.7.refs_1_, ...), custom_call_target="tpu_custom_call" | custom-call | flops 1000 | bytes 1000 | tf_op jit(solution)/shard_map/pair/pallas_call | solution.py:369
  52.5 7.7 %all-to-all-start.1 = ((bf16[32,8,16,128]{3,2,1,0:T(8,128)(2,1)}), bf16[32,8,16,128]{3,2,1,0:T(8,128)(2,1)S(1)}, u32[]{:S(2)}, u32[]{:S(2)}) async-start(bf16[32,8,16,128]{3,2,1,0:T(8,128)(2,1)} %get-tuple-element.35), calls=%async_computation.1 | async-start | bytes 2097152 | tf_op jit(solution)/shard_map/all_to_all | solution.py:432
  60.2 4.5 %collective-permute-done.6.refs_2_.refs_6_ = bf16[4,400,256]{2,1,0:T(8,128)(2,1)} collective-permute-done((bf16[4,400,256]{2,1,0:T(8,128)(2,1)}, bf16[4,400,256]{2,1,0:T(8,128)(2,1)}, u32[]{:S(2)}, u32[]{:S(2)}) %collective-permute-start.6) | collective-permute-done | bytes 819232 | tf_op jit(solution)/shard_map/ppermute | solution.py:360
  64.7 0.1 pad_add_fusion.1.at_ref
  64.8 2.5 %collective-permute-done.11.refs_3_.refs_7_ = bf16[4,400,256]{2,1,0:T(8,128)(2,1)S(1)} collective-permute-done((bf16[4,400,256]{2,1,0:T(8,128)(2,1)}, bf16[4,400,256]{2,1,0:T(8,128)(2,1)S(1)}, u32[]{:S(2)}, u32[]{:S(2)}) %collective-permute-start.11) | collective-permute-done | bytes 819232 | tf_op jit(solution)/shard_map/ppermute | solution.py:400
  67.2 8.3 %ready.1 = (bf16[12,256,128]{2,1,0:T(8,128)(2,1)}, bf16[12,512,256]{2,1,0:T(8,128)(2,1)}, bf16[12,256,512]{2,1,0:T(8,128)(2,1)}, f32[12,256,128]{2,1,0:T(8,128)}, bf16[512,128]{1,0:T(8,128)(2,1)}) custom-call(s32[2]{0:T(128)S(1)} %pad_add_fusion.1.at_ref, bf16[4,400,256]{2,1,0:T(8,128)(2,1)} %bitcast.52, ...), custom_call_target="tpu_custom_call" | custom-call | flops 1000 | bytes 1000 | tf_op jit(solution)/shard_map/ready/pallas_call | solution.py:404
  75.5 4.1 %all-to-all-done.1 = bf16[32,8,16,128]{3,2,1,0:T(8,128)(2,1)S(1)} async-done(((bf16[32,8,16,128]{3,2,1,0:T(8,128)(2,1)}), bf16[32,8,16,128]{3,2,1,0:T(8,128)(2,1)S(1)}, u32[]{:S(2)}, u32[]{:S(2)}) %all-to-all-start.1) | async-done | bytes 1048608 | tf_op jit(solution)/shard_map/all_to_all | solution.py:432
  79.6 12.9 %rows.1 = bf16[12,128,256]{2,1,0:T(8,128)(2,1)S(1)} custom-call(bf16[4,400,256]{2,1,0:T(8,128)(2,1)} %bitcast.54, bf16[12,256,128]{2,1,0:T(8,128)(2,1)} %get-tuple-element.39.query_ref, bf16[12,512,256]{2,1,0:T(8,128)(2,1)} %get-tuple-element.40.key_ref, bf16[12,256,512]{2,1,0:T(8,128)(2,1)} %get-tuple-element.41.value_ref, ...), custom_call_target="tpu_custom_call" | custom-call | flops 8000000000 | bytes 12000000 | tf_op jit(solution)/shard_map/rows/pallas_call | solution.py:436
  92.5 0.2 reshape.56
  92.7 0.3 copy.34
  93.0 0.0 copy-start.3
  93.1 19.4 %all_to_all.20 = bf16[32,12,4,256]{3,2,1,0:T(4,128)(2,1)S(1)} all-to-all(bf16[32,12,4,256]{3,2,1,0:T(4,128)(2,1)S(1)} %bitcast.58), channel_id=1, replica_groups=mesh['yh'=2,'z'=4,'yl'=2,'xh'=2,'xl'=2,'core'=2] {'yh','z','yl','xh'}, dimensions={0} | all-to-all | bytes 1572864 | tf_op jit(solution)/shard_map/all_to_all | solution.py:453
  112.5 0.1 copy.43
  112.7 7.4 %columns.1 = bf16[4,384,256]{2,1,0:T(8,128)(2,1)S(1)} custom-call(bf16[4,384,256]{2,1,0:T(8,128)(2,1)S(1)} %bitcast.46, f32[8,384]{1,0:T(8,128)S(1)} %get-tuple-element.44.mask_ref, bf16[256,256]{1,0:T(8,128)(2,1)S(1)} %copy-done.3, bf16[256,256]{1,0:T(8,128)(2,1)S(1)} %copy-done.4, bf16[256,256]{1,0:T(8,128)(2,1)S(1)} %copy-done.5, ...), custom_call_target="tpu_custom_call" | custom-call | flops 8000000000 | bytes 2000000 | tf_op jit(solution)/shard_map/columns/pallas_call | solution.py:457
  120.1 0.1 copy.42
  120.2 14.8 %all_to_all.21 = bf16[8,4,48,256]{3,2,1,0:T(8,128)(2,1)S(1)} all-to-all(bf16[8,4,48,256]{3,2,1,0:T(8,128)(2,1)S(1)} %bitcast.60), channel_id=1, replica_groups=mesh['yh'=2,'z'=4,'yl'=2,'xh'=2,'xl'=2,'core'=2] {'yh','z'}, dimensions={0} | all-to-all | bytes 1572864 | tf_op jit(solution)/shard_map/all_to_all | solution.py:486
  135.0 1.1 copy.41
  (29 shorter events, 0.1 us)
Async XLA Ops:
  2.8 11.8 %collective-permute-start.4 = (bf16[400,256]{1,0:T(8,128)(2,1)S(1)}, bf16[400,256]{1,0:T(8,128)(2,1)S(1)}, u32[]{:S(2)}, u32[]{:S(2)}) collective-permute-start(bf16[400,256]{1,0:T(8,128)(2,1)S(1)} %get-tuple-element.47), channel_id=1, source_target_pairs={{0,12},{4,8},{8,4},{12,0},{1,13},{5,9},{9,5},{13,1},{2,14},{6,10},... | collective-permute-start | bytes 614408 | tf_op jit(solution)/shard_map/ppermute | solution.py:323
  5.8 10.7 %collective-permute-start.3 = (bf16[400,256]{1,0:T(8,128)(2,1)S(1)}, bf16[400,256]{1,0:T(8,128)(2,1)S(1)}, u32[]{:S(2)}, u32[]{:S(2)}) collective-permute-start(bf16[400,256]{1,0:T(8,128)(2,1)S(1)} %get-tuple-element.48), channel_id=1, source_target_pairs={{0,8},{4,12},{8,0},{12,4},{1,9},{5,13},{9,1},{13,5},{2,10},{6,14},... | collective-permute-start | bytes 614408 | tf_op jit(solution)/shard_map/ppermute | solution.py:323
  7.3 9.1 %collective-permute-start.2 = (bf16[400,256]{1,0:T(8,128)(2,1)S(1)}, bf16[400,256]{1,0:T(8,128)(2,1)S(1)}, u32[]{:S(2)}, u32[]{:S(2)}) collective-permute-start(bf16[400,256]{1,0:T(8,128)(2,1)S(1)} %get-tuple-element.49), channel_id=1, source_target_pairs={{0,4},{4,0},{8,12},{12,8},{1,5},{5,1},{9,13},{13,9},{2,6},{6,2},{1... | collective-permute-start | bytes 614408 | tf_op jit(solution)/shard_map/ppermute | solution.py:323
  11.0 7.8 %collective-permute-start = (bf16[48,1152]{1,0:T(8,128)(2,1)S(1)}, bf16[48,1152]{1,0:T(8,128)(2,1)S(1)}, u32[]{:S(2)}, u32[]{:S(2)}) collective-permute-start(bf16[48,1152]{1,0:T(8,128)(2,1)S(1)} %get-tuple-element.24), channel_id=1, source_target_pairs={{0,0},{1,1},{2,18},{3,19},{4,36},{5,37},{6,54},{7,55},{8,64},{9,65... | collective-permute-start | bytes 331784 | tf_op jit(solution)/shard_map/ppermute | solution.py:348
  14.5 6.3 %collective-permute-start.1 = (bf16[48,1152]{1,0:T(8,128)(2,1)S(1)}, bf16[48,1152]{1,0:T(8,128)(2,1)S(1)}, u32[]{:S(2)}, u32[]{:S(2)}) collective-permute-start(bf16[48,1152]{1,0:T(8,128)(2,1)S(1)} %get-tuple-element.25), channel_id=1, source_target_pairs={{0,64},{64,0},{1,65},{65,1},{2,66},{66,2},{3,67},{67,3},{4,68},{68... | collective-permute-start | bytes 331784 | tf_op jit(solution)/shard_map/ppermute | solution.py:349
  17.8 17.5 %copy-start.8 = (bf16[1024,128]{1,0:T(8,128)(2,1)S(1)}, bf16[1024,128]{1,0:T(8,128)(2,1)}, u32[]{:S(2)}) copy-start(bf16[1024,128]{1,0:T(8,128)(2,1)} %param.24) | copy-start | bytes 786436
  21.8 23.2 %copy-start.9 = (s32[512]{0:T(512)S(1)}, s32[512]{0:T(512)}, u32[]{:S(2)}) copy-start(s32[512]{0:T(512)} %param.20) | copy-start | bytes 6148
  21.8 23.9 %copy-start = (bf16[32,64,128]{2,1,0:T(8,128)(2,1)S(1)}, bf16[32,64,128]{2,1,0:T(8,128)(2,1)}, u32[]{:S(2)}) copy-start(bf16[32,64,128]{2,1,0:T(8,128)(2,1)} %refs_6_.1) | copy-start | bytes 1572868
  21.9 23.9 %copy-start.1 = (bf16[128,8]{0,1:T(8,128)(2,1)S(1)}, bf16[128,8]{0,1:T(8,128)(2,1)}, u32[]{:S(2)}) copy-start(bf16[128,8]{0,1:T(8,128)(2,1)} %param.25) | copy-start | bytes 6148
  21.9 21.5 %all-to-all-start = ((bf16[8,48,1152]{2,1,0:T(8,128)(2,1)}), bf16[8,48,1152]{2,1,0:T(8,128)(2,1)S(1)}, u32[]{:S(2)}, u32[]{:S(2)}) async-start(bf16[8,48,1152]{2,1,0:T(8,128)(2,1)} %broadcast_in_dim.2), calls=%async_computation | async-start | bytes 1769472 | tf_op jit(solution)/shard_map/all_to_all | solution.py:283
  31.1 11.6 %collective-permute-start.9 = (bf16[2,48,1152]{2,1,0:T(8,128)(2,1)S(1)}, bf16[2,48,1152]{2,1,0:T(8,128)(2,1)S(1)}, u32[]{:S(2)}, u32[]{:S(2)}) collective-permute-start(bf16[2,48,1152]{2,1,0:T(8,128)(2,1)S(1)} %pad_maximum_fusion.1.refs_0_), channel_id=1, source_target_pairs={{0,48},{16,32},{32,16},{48,0},{1,49},{17,33},{33,17},{49,1},{2,50}... | collective-permute-start | bytes 663560 | tf_op jit(solution)/shard_map/ppermute | solution.py:354
  32.5 10.2 %collective-permute-start.8 = (bf16[2,48,1152]{2,1,0:T(8,128)(2,1)S(1)}, bf16[2,48,1152]{2,1,0:T(8,128)(2,1)S(1)}, u32[]{:S(2)}, u32[]{:S(2)}) collective-permute-start(bf16[2,48,1152]{2,1,0:T(8,128)(2,1)S(1)} %pad_maximum_fusion.1.refs_0_), channel_id=1, source_target_pairs={{0,32},{16,48},{32,0},{48,16},{1,33},{17,49},{33,1},{49,17},{2,34}... | collective-permute-start | bytes 663560 | tf_op jit(solution)/shard_map/ppermute | solution.py:354
  33.9 9.4 %collective-permute-start.7 = (bf16[2,48,1152]{2,1,0:T(8,128)(2,1)S(1)}, bf16[2,48,1152]{2,1,0:T(8,128)(2,1)S(1)}, u32[]{:S(2)}, u32[]{:S(2)}) collective-permute-start(bf16[2,48,1152]{2,1,0:T(8,128)(2,1)S(1)} %pad_maximum_fusion.1.refs_0_), channel_id=1, source_target_pairs={{0,16},{16,0},{32,48},{48,32},{1,17},{17,1},{33,49},{49,33},{2,18}... | collective-permute-start | bytes 663560 | tf_op jit(solution)/shard_map/ppermute | solution.py:354
  43.3 2.4 %collective-permute-start.10 = (bf16[8,48,1152]{2,1,0:T(8,128)(2,1)S(1)}, bf16[8,48,1152]{2,1,0:T(8,128)(2,1)S(1)}, u32[]{:S(2)}, u32[]{:S(2)}) collective-permute-start(bf16[8,48,1152]{2,1,0:T(8,128)(2,1)S(1)} %all-to-all-done.refs_4_), channel_id=1, source_target_pairs={{0,1},{1,0},{2,3},{3,2},{4,5},{5,4},{6,7},{7,6},{8,9},{9,8},{10,11... | collective-permute-start | bytes 2654216 | tf_op jit(solution)/shard_map/ppermute | solution.py:359
  43.3 21.4 %collective-permute-start.6 = (bf16[4,400,256]{2,1,0:T(8,128)(2,1)}, bf16[4,400,256]{2,1,0:T(8,128)(2,1)}, u32[]{:S(2)}, u32[]{:S(2)}) collective-permute-start(bf16[4,400,256]{2,1,0:T(8,128)(2,1)} %bitcast.50), channel_id=1, source_target_pairs={{0,2},{2,0},{1,3},{3,1},{4,6},{6,4},{5,7},{7,5},{8,10},{10,8},{9,1... | collective-permute-start | bytes 2457608 | tf_op jit(solution)/shard_map/ppermute | solution.py:360
  44.8 19.9 %collective-permute-start.5 = (bf16[4,400,256]{2,1,0:T(8,128)(2,1)}, bf16[4,400,256]{2,1,0:T(8,128)(2,1)}, u32[]{:S(2)}, u32[]{:S(2)}) collective-permute-start(bf16[4,400,256]{2,1,0:T(8,128)(2,1)} %bitcast.51), channel_id=1, source_target_pairs={{0,1},{1,0},{2,3},{3,2},{4,5},{5,4},{6,7},{7,6},{8,9},{9,8},{10,11... | collective-permute-start | bytes 2457608 | tf_op jit(solution)/shard_map/ppermute | solution.py:361
  52.5 27.1 %all-to-all-start.1 = ((bf16[32,8,16,128]{3,2,1,0:T(8,128)(2,1)}), bf16[32,8,16,128]{3,2,1,0:T(8,128)(2,1)S(1)}, u32[]{:S(2)}, u32[]{:S(2)}) async-start(bf16[32,8,16,128]{3,2,1,0:T(8,128)(2,1)} %get-tuple-element.35), calls=%async_computation.1 | async-start | bytes 2097152 | tf_op jit(solution)/shard_map/all_to_all | solution.py:432
  64.7 2.5 %collective-permute-start.11 = (bf16[4,400,256]{2,1,0:T(8,128)(2,1)}, bf16[4,400,256]{2,1,0:T(8,128)(2,1)S(1)}, u32[]{:S(2)}, u32[]{:S(2)}) collective-permute-start(bf16[4,400,256]{2,1,0:T(8,128)(2,1)} %collective-permute-done.6.refs_2_.refs_6_), channel_id=1, source_target_pairs={{0,1},{1,0},{2,3},{3,2},{4,5},{5,4},{6,7},{7,6},{8,9},{9,8},{10,11... | collective-permute-start | bytes 2457608 | tf_op jit(solution)/shard_map/ppermute | solution.py:400
  64.7 14.9 %copy-start.2 = (bf16[256,256]{1,0:T(8,128)(2,1)S(1)}, bf16[256,256]{1,0:T(8,128)(2,1)}, u32[]{:S(2)}) copy-start(bf16[256,256]{1,0:T(8,128)(2,1)} %wo_ref.2) | copy-start | bytes 393220
  93.0 19.6 %copy-start.3 = (bf16[256,256]{1,0:T(8,128)(2,1)S(1)}, bf16[256,256]{1,0:T(8,128)(2,1)}, u32[]{:S(2)}) copy-start(bf16[256,256]{1,0:T(8,128)(2,1)} %wq_ref.1) | copy-start | bytes 393220
  93.0 19.6 %copy-start.4 = (bf16[256,256]{1,0:T(8,128)(2,1)S(1)}, bf16[256,256]{1,0:T(8,128)(2,1)}, u32[]{:S(2)}) copy-start(bf16[256,256]{1,0:T(8,128)(2,1)} %wk_ref.1) | copy-start | bytes 393220
  93.1 19.6 %copy-start.5 = (bf16[256,256]{1,0:T(8,128)(2,1)S(1)}, bf16[256,256]{1,0:T(8,128)(2,1)}, u32[]{:S(2)}) copy-start(bf16[256,256]{1,0:T(8,128)(2,1)} %wv_ref.1) | copy-start | bytes 393220
  93.1 19.6 %copy-start.6 = (bf16[256,256]{1,0:T(8,128)(2,1)S(1)}, bf16[256,256]{1,0:T(8,128)(2,1)}, u32[]{:S(2)}) copy-start(bf16[256,256]{1,0:T(8,128)(2,1)} %wg_ref.1) | copy-start | bytes 393220
  93.1 19.6 %copy-start.7 = (bf16[256,256]{1,0:T(8,128)(2,1)S(1)}, bf16[256,256]{1,0:T(8,128)(2,1)}, u32[]{:S(2)}) copy-start(bf16[256,256]{1,0:T(8,128)(2,1)} %wo_ref.3) | copy-start | bytes 393220

commit v5 on v4

--- a/solution.py
+++ b/solution.py
@@ -14,6 +14,7 @@
 BF16 = jnp.bfloat16
 NEG = -1e9
 STEP = 3
+TURN = 4
 PICK = 2
 SEQ = ("yh", "z")
 RES = ("yl", "xh", "xl", "core")
@@ -194,12 +195,9 @@
 
     @pl.when(pl.program_id(0) == 0)
     def _():
-        columns[...] = jnp.zeros_like(columns)
         places = [(xl, core), (xl, 1 - core), (1 - xl, core), (1 - xl, 1 - core)]
         for tail_ref, (a, b) in zip(tails, places):
-            for u in range(4):
-                absent = ((tail_ref[u, :, :128].astype(F32) - 1.0) * -NEG).T
-                columns[u, a, b, :, :16] = absent[:32]
+            columns[:, a, b] = (tail_ref[:, :, :128].astype(F32) - 1.0) * -NEG
         mask_ref[...] = columns[...].reshape(512, 128).astype(BF16)
 
     for t in range(STEP):
@@ -217,7 +215,7 @@
 
 
 def row_kernel(
-    x_ref, query_ref, key_ref, value_ref, gate_ref, mask_ref, bias_ref, wo_ref, out_ref, held
+    at_ref, x_ref, query_ref, key_ref, value_ref, gate_ref, mask_ref, bias_ref, wo_ref, out_ref, held
 ):
     @pl.when(pl.program_id(0) == 0)
     def _():
@@ -241,10 +239,10 @@
             value_ref[t],
             lambda h: held[h],
             mask_ref[...],
-            pl.program_id(0) * STEP + t,
+            at_ref[0] * 12 + pl.program_id(0) * TURN + t,
             4,
         )
-        for t in range(STEP)
+        for t in range(TURN)
     ]
     run_pipelined(attentions, finish)
 
@@ -312,19 +310,19 @@
     res_at = lax.axis_index(RES)
     xl_at = lax.axis_index("xl")
     core_at = lax.axis_index("core")
-    mask = entry_exists_flags.astype(BF16)
-
-    tail = jnp.pad(mask.reshape(4, 12, 32), ((0, 0), (0, 4), (0, 224)))
+
+    tail = jnp.pad(entry_exists_flags.T.astype(BF16), ((0, 0), (0, 208)))
+    tail = jnp.broadcast_to(tail[None], (4, 32, 256))
     packed = jnp.concatenate([homolog_stack.reshape(4, 384, 256), tail], axis=1)
     team_at = lax.axis_index(TEAM)
     parts = []
     for k in range(4):
         part = lax.dynamic_index_in_dim(packed, team_at ^ k, 0, False)
         parts.append(lax.ppermute(part, TEAM, [(t, t ^ k) for t in range(4)]) if k else part)
-    packed = jnp.stack(parts).reshape(2, 2, 400, 256)
+    packed = jnp.stack(parts).reshape(2, 2, 416, 256)
     packed = jnp.where(lax.axis_index("yl") == 1, packed[::-1], packed)
     packed = jnp.where(lax.axis_index("xh") == 1, packed[:, ::-1], packed)
-    packed = packed.reshape(4, 400, 256)
+    packed = packed.reshape(4, 416, 256)
 
     left, right = pl.pallas_call(
         factor_kernel,
@@ -410,7 +408,7 @@
         + [pltpu.HBM((512, 128), BF16)],
         grid=(12 // STEP,),
         in_specs=[smem] + [pl.BlockSpec((4, STEP * 32, 256), lambda t: (0, t, 0))] * 4
-        + [pl.BlockSpec((4, 16, 256), lambda t: (0, 24, 0))] * 4
+        + [pl.BlockSpec((4, 32, 256), lambda t: (0, 12, 0))] * 4
         + [square] * 4,
         out_specs=specs + [whole((512, 128))],
         scratch_shapes=[
@@ -436,18 +434,18 @@
     middle = pl.pallas_call(
         row_kernel,
         out_shape=jax.ShapeDtypeStruct((12, 128, 256), BF16),
-        grid=(12 // STEP,),
-        in_specs=[pl.BlockSpec((4, STEP * 32, 256), lambda t: (0, t, 0))]
-        + specs
+        grid=(12 // TURN,),
+        in_specs=[smem, pl.BlockSpec((4, TURN * 32, 256), lambda t: (0, t, 0))]
+        + [pl.BlockSpec((TURN,) + shape[1:], lambda t: (t, 0, 0)) for shape in by_row]
         + [whole((512, 128)), whole((8, 4, 8, 16, 128)), square],
-        out_specs=pl.BlockSpec((STEP, 128, 256), lambda t: (t, 0, 0)),
+        out_specs=pl.BlockSpec((TURN, 128, 256), lambda t: (t, 0, 0)),
         scratch_shapes=[pltpu.VMEM((8, 512, 128), F32)],
         compiler_params=pltpu.CompilerParams(vmem_limit_bytes=VMEM_LIMIT),
         cost_estimate=pl.CostEstimate(
             flops=8_000_000_000, transcendentals=6_300_000, bytes_accessed=12_000_000
         ),
         name="rows",
-    )(pieces[0], *rows_in, bias, horizontal_final_weights)
+    )(team_at.astype(jnp.int32).reshape(1), pieces[0], *rows_in, bias, horizontal_final_weights)
 
     middle = jnp.transpose(middle.reshape(12, 4, 8, 4, 256), (2, 1, 0, 3, 4))
     middle = lax.all_to_all(

time: 138 us -> 138 us (level)
    ppermute x3, waiting for transfers between devices: 1.85 us -> 3.23 us  [body(): lax.ppermute(part, TEAM, [(t, t ^ k) for t in range(4)])]
  transfers between devices with their start and end apart: 14 -> 14, of which waited for: 9 -> 8; matrix products, arithmetic and copies ran while one was open for 1% -> 1% of each run, Pallas kernels for 13% -> 13%
where the time goes in v5:
time: 138 us; the launch traced here: 137 us
  Pallas kernels  38.1 us (28%)
  blocking collectives  35 us (25%)
  starting transfers between devices  32.1 us (23%)
  waiting for transfers between devices  24.2 us (18%)
  other arithmetic  3.52 us (3%)
  local copies, waits for them, and re-layouts  3.18 us (2%)
    all_to_all x1, blocking collectives, body(): lax.all_to_all(middle.reshape(32, 12, 4, 256), PLANE, split_axis=0, conca...  19.1 us
    all_to_all x1, blocking collectives, body(): lax.all_to_all(columns, SEQ, split_axis=0, concat_axis=0, tiled=True)  15.9 us
    pallas_call x1, Pallas kernels, body(): pl.pallas_call(row_kernel, out_shape=jax.ShapeDtypeStruct((12, 128, 256),...  12.5 us
    all_to_all x1, starting transfers between devices, spread(): return lax.all_to_all(wide, axes, split_axis=0, concat_axis=0, tiled=True)  9.07 us
    all_to_all x1, starting transfers between devices, body(): bias = lax.all_to_all(bias, PLANE, split_axis=0, concat_axis=0, tiled=True)  8.5 us
    pallas_call x1, Pallas kernels, body(): pl.pallas_call(ready_kernel, out_shape=[pltpu.HBM(shape, kind) for shape,...  8.2 us
    pallas_call x1, Pallas kernels, body(): pl.pallas_call(column_kernel, out_shape=jax.ShapeDtypeStruct((4, 384, 256...  7.44 us
    ppermute x3, waiting for transfers between devices, body(): lax.ppermute(left, 'z', [(z, z ^ k) for z in range(4)])  7.09 us
  transfers between devices with their start and end apart: 14, of which 8 were waited for; matrix products, arithmetic and copies ran while one was open for 1% of the time, Pallas kernels for 13%

profile of v5, /device:TPU:8, one launch (start us, length us, event | category | flops | bytes accessed | tf_op | source)
XLA Modules:
  0.0 136.9 jit_solution(8709418640204535690)
XLA Ops:
  0.7 0.7 bitcast_convert_fusion
  1.4 1.3 fusion.1
  2.7 3.1 %collective-permute-start.2 = (bf16[416,256]{1,0:T(8,128)(2,1)S(1)}, bf16[416,256]{1,0:T(8,128)(2,1)S(1)}, u32[]{:S(2)}, u32[]{:S(2)}) collective-permute-start(bf16[416,256]{1,0:T(8,128)(2,1)S(1)} %get-tuple-element.47), channel_id=1, source_target_pairs={{0,4},{4,0},{8,12},{12,8},{1,5},{5,1},{9,13},{13,9},{2,6},{6,2},{1... | collective-permute-start | bytes 638984 | tf_op jit(solution)/shard_map/ppermute | solution.py:321
  5.8 0.4 collective-permute-start.3
  6.2 1.5 %collective-permute-start.4 = (bf16[416,256]{1,0:T(8,128)(2,1)S(1)}, bf16[416,256]{1,0:T(8,128)(2,1)S(1)}, u32[]{:S(2)}, u32[]{:S(2)}) collective-permute-start(bf16[416,256]{1,0:T(8,128)(2,1)S(1)} %get-tuple-element.49), channel_id=1, source_target_pairs={{0,12},{4,8},{8,4},{12,0},{1,13},{5,9},{9,5},{13,1},{2,14},{6,10},... | collective-permute-start | bytes 638984 | tf_op jit(solution)/shard_map/ppermute | solution.py:321
  7.8 3.2 %factors.1 = (bf16[48,1152]{1,0:T(8,128)(2,1)S(1)}, bf16[48,1152]{1,0:T(8,128)(2,1)S(1)}) custom-call(bf16[48,32,256]{2,1,0:T(8,128)(2,1)} %x_ref.1, s32[32,48]{1,0:T(8,128)} %bitcast.70, bf16[32,256]{1,0:T(8,128)(2,1)} %bitcast.71, bf16[32,256]{1,0:T(8,128)(2,1)} %bitcast.72), custom_call_target="tpu_custom_call" | custom-call | tf_op jit(solution)/shard_map/factors/pallas_call | solution.py:327
  10.9 3.5 %collective-permute-start = (bf16[48,1152]{1,0:T(8,128)(2,1)S(1)}, bf16[48,1152]{1,0:T(8,128)(2,1)S(1)}, u32[]{:S(2)}, u32[]{:S(2)}) collective-permute-start(bf16[48,1152]{1,0:T(8,128)(2,1)S(1)} %get-tuple-element.24), channel_id=1, source_target_pairs={{0,0},{1,1},{2,18},{3,19},{4,36},{5,37},{6,54},{7,55},{8,64},{9,65... | collective-permute-start | bytes 331784 | tf_op jit(solution)/shard_map/ppermute | solution.py:346
  14.4 0.1 collective-permute-start.1
  14.5 3.2 %collective-permute-done.3 = bf16[416,256]{1,0:T(8,128)(2,1)S(1)} collective-permute-done((bf16[416,256]{1,0:T(8,128)(2,1)S(1)}, bf16[416,256]{1,0:T(8,128)(2,1)S(1)}, u32[]{:S(2)}, u32[]{:S(2)}) %collective-permute-start.3) | collective-permute-done | bytes 213024 | tf_op jit(solution)/shard_map/ppermute | solution.py:321
  17.8 0.1 pad_maximum_fusion
  17.9 0.0 copy-start.8
  17.9 0.2 reverse_select_fusion.1
  18.1 0.0 copy-start.9
  18.1 1.1 reverse_select_fusion
  19.2 1.6 %collective-permute-done.1 = bf16[48,1152]{1,0:T(8,128)(2,1)S(1)} collective-permute-done((bf16[48,1152]{1,0:T(8,128)(2,1)S(1)}, bf16[48,1152]{1,0:T(8,128)(2,1)S(1)}, u32[]{:S(2)}, u32[]{:S(2)}) %collective-permute-start.1) | collective-permute-done | bytes 110624 | tf_op jit(solution)/shard_map/ppermute | solution.py:347
  20.8 1.0 broadcast_in_dim.5
  21.8 9.1 %all-to-all-start = ((bf16[8,48,1152]{2,1,0:T(8,128)(2,1)}), bf16[8,48,1152]{2,1,0:T(8,128)(2,1)S(1)}, u32[]{:S(2)}, u32[]{:S(2)}) async-start(bf16[8,48,1152]{2,1,0:T(8,128)(2,1)} %broadcast_in_dim.5), calls=%async_computation | async-start | bytes 1769472 | tf_op jit(solution)/shard_map/all_to_all | solution.py:281
  30.9 1.2 collective-permute-start.9
  32.0 1.7 %collective-permute-start.8 = (bf16[2,48,1152]{2,1,0:T(8,128)(2,1)S(1)}, bf16[2,48,1152]{2,1,0:T(8,128)(2,1)S(1)}, u32[]{:S(2)}, u32[]{:S(2)}) collective-permute-start(bf16[2,48,1152]{2,1,0:T(8,128)(2,1)S(1)} %pad_maximum_fusion.1.refs_0_), channel_id=1, source_target_pairs={{0,32},{16,48},{32,0},{48,16},{1,33},{17,49},{33,1},{49,17},{2,34}... | collective-permute-start | bytes 663560 | tf_op jit(solution)/shard_map/ppermute | solution.py:352
  33.7 1.4 collective-permute-start.7
  35.0 0.1 copy.29
  35.1 6.4 %collective-permute-done.9.refs_3_ = bf16[2,48,1152]{2,1,0:T(8,128)(2,1)S(1)} collective-permute-done((bf16[2,48,1152]{2,1,0:T(8,128)(2,1)S(1)}, bf16[2,48,1152]{2,1,0:T(8,128)(2,1)S(1)}, u32[]{:S(2)}, u32[]{:S(2)}) %collective-permute-start.9) | collective-permute-done | bytes 221216 | tf_op jit(solution)/shard_map/ppermute | solution.py:352
  41.6 0.7 collective-permute-done.7.refs_1_
  42.2 1.5 %collective-permute-start.6 = (bf16[4,416,256]{2,1,0:T(8,128)(2,1)}, bf16[4,416,256]{2,1,0:T(8,128)(2,1)}, u32[]{:S(2)}, u32[]{:S(2)}) collective-permute-start(bf16[4,416,256]{2,1,0:T(8,128)(2,1)} %bitcast.52), channel_id=1, source_target_pairs={{0,2},{2,0},{1,3},{3,1},{4,6},{6,4},{5,7},{7,5},{8,10},{10,8},{9,1... | collective-permute-start | bytes 2555912 | tf_op jit(solution)/shard_map/ppermute | solution.py:358
  43.7 0.2 collective-permute-start.5
  43.9 0.1 dynamic-slice_bitcast_fusion
  44.0 0.1 copy.30.refs_8_
  44.1 0.1 dynamic-slice_bitcast_fusion.1.refs_7_
  44.2 0.1 pad_add_fusion.at_ref
  44.3 0.4 collective-permute-done.10.refs_5_
  44.7 6.8 %pair.1 = (bf16[32,64,128]{2,1,0:T(8,128)(2,1)}, bf16[32,8,16,128]{3,2,1,0:T(8,128)(2,1)}, f32[8,384]{1,0:T(8,128)S(1)}) custom-call(s32[2]{0:T(128)S(1)} %pad_add_fusion.at_ref, bf16[2,48,1152]{2,1,0:T(8,128)(2,1)S(1)} %pad_maximum_fusion.1.refs_0_, bf16[2,48,1152]{2,1,0:T(8,128)(2,1)S(1)} %collective-permute-done.7.refs_1_, ...), custom_call_target="tpu_custom_call" | custom-call | flops 1000 | bytes 1000 | tf_op jit(solution)/shard_map/pair/pallas_call | solution.py:367
  51.4 8.5 %all-to-all-start.1 = ((bf16[32,8,16,128]{3,2,1,0:T(8,128)(2,1)}), bf16[32,8,16,128]{3,2,1,0:T(8,128)(2,1)S(1)}, u32[]{:S(2)}, u32[]{:S(2)}) async-start(bf16[32,8,16,128]{3,2,1,0:T(8,128)(2,1)} %get-tuple-element.35), calls=%async_computation.1 | async-start | bytes 2097152 | tf_op jit(solution)/shard_map/all_to_all | solution.py:430
  59.9 4.4 %collective-permute-done.6.refs_2_.refs_6_ = bf16[4,416,256]{2,1,0:T(8,128)(2,1)} collective-permute-done((bf16[4,416,256]{2,1,0:T(8,128)(2,1)}, bf16[4,416,256]{2,1,0:T(8,128)(2,1)}, u32[]{:S(2)}, u32[]{:S(2)}) %collective-permute-start.6) | collective-permute-done | bytes 852000 | tf_op jit(solution)/shard_map/ppermute | solution.py:358
  64.3 0.1 pad_add_fusion.1.at_ref
  64.4 2.5 %collective-permute-done.11.refs_3_.refs_7_ = bf16[4,416,256]{2,1,0:T(8,128)(2,1)S(1)} collective-permute-done((bf16[4,416,256]{2,1,0:T(8,128)(2,1)}, bf16[4,416,256]{2,1,0:T(8,128)(2,1)S(1)}, u32[]{:S(2)}, u32[]{:S(2)}) %collective-permute-start.11) | collective-permute-done | bytes 852000 | tf_op jit(solution)/shard_map/ppermute | solution.py:398
  66.9 8.2 %ready.1 = (bf16[12,256,128]{2,1,0:T(8,128)(2,1)}, bf16[12,512,256]{2,1,0:T(8,128)(2,1)}, bf16[12,256,512]{2,1,0:T(8,128)(2,1)}, f32[12,256,128]{2,1,0:T(8,128)}, bf16[512,128]{1,0:T(8,128)(2,1)}) custom-call(s32[2]{0:T(128)S(1)} %pad_add_fusion.1.at_ref, bf16[4,416,256]{2,1,0:T(8,128)(2,1)} %bitcast.54, ...), custom_call_target="tpu_custom_call" | custom-call | flops 1000 | bytes 1000 | tf_op jit(solution)/shard_map/ready/pallas_call | solution.py:402
  75.1 5.0 %all-to-all-done.1 = bf16[32,8,16,128]{3,2,1,0:T(8,128)(2,1)S(1)} async-done(((bf16[32,8,16,128]{3,2,1,0:T(8,128)(2,1)}), bf16[32,8,16,128]{3,2,1,0:T(8,128)(2,1)S(1)}, u32[]{:S(2)}, u32[]{:S(2)}) %all-to-all-start.1) | async-done | bytes 1048608 | tf_op jit(solution)/shard_map/all_to_all | solution.py:430
  80.1 12.5 %rows.1 = bf16[12,128,256]{2,1,0:T(8,128)(2,1)S(1)} custom-call(s32[1]{0:T(128)} %bitcast.at_ref, bf16[4,416,256]{2,1,0:T(8,128)(2,1)} %bitcast.56, bf16[12,256,128]{2,1,0:T(8,128)(2,1)} %get-tuple-element.39.query_ref, bf16[12,512,256]{2,1,0:T(8,128)(2,1)} %get-tuple-element.40.key_ref, bf16[12,256,512]{2,1,0:T(8,128)(2,1)} %get-tuple-element.41.value_ref, ...), custom_call_target="tpu_custom_call" | custom-call | flops 8000000000 | bytes 12000000 | tf_op jit(solution)/shard_map/rows/pallas_call | solution.py:434
  92.6 0.0 copy-start.4
  92.6 0.0 copy-start.5
  92.7 0.2 reshape.57
  92.9 0.3 copy.31
  93.2 19.1 %all_to_all.20 = bf16[32,12,4,256]{3,2,1,0:T(4,128)(2,1)S(1)} all-to-all(bf16[32,12,4,256]{3,2,1,0:T(4,128)(2,1)S(1)} %bitcast.59), channel_id=1, replica_groups=mesh['yh'=2,'z'=4,'yl'=2,'xh'=2,'xl'=2,'core'=2] {'yh','z','yl','xh'}, dimensions={0} | all-to-all | bytes 1572864 | tf_op jit(solution)/shard_map/all_to_all | solution.py:451
  112.3 0.1 copy.40
  112.4 7.4 %columns.1 = bf16[4,384,256]{2,1,0:T(8,128)(2,1)S(1)} custom-call(bf16[4,384,256]{2,1,0:T(8,128)(2,1)S(1)} %bitcast.48, f32[8,384]{1,0:T(8,128)S(1)} %get-tuple-element.44.mask_ref, bf16[256,256]{1,0:T(8,128)(2,1)S(1)} %copy-done.3, bf16[256,256]{1,0:T(8,128)(2,1)S(1)} %copy-done.4, bf16[256,256]{1,0:T(8,128)(2,1)S(1)} %copy-done.5, ...), custom_call_target="tpu_custom_call" | custom-call | flops 8000000000 | bytes 2000000 | tf_op jit(solution)/shard_map/columns/pallas_call | solution.py:455
  119.9 0.1 copy.39
  119.9 15.9 %all_to_all.21 = bf16[8,4,48,256]{3,2,1,0:T(8,128)(2,1)S(1)} all-to-all(bf16[8,4,48,256]{3,2,1,0:T(8,128)(2,1)S(1)} %bitcast.61), channel_id=1, replica_groups=mesh['yh'=2,'z'=4,'yl'=2,'xh'=2,'xl'=2,'core'=2] {'yh','z'}, dimensions={0} | all-to-all | bytes 1572864 | tf_op jit(solution)/shard_map/all_to_all | solution.py:484
  135.8 1.1 copy.38
  (28 shorter events, 0.1 us)
Async XLA Ops:
  2.7 11.8 %collective-permute-start.2 = (bf16[416,256]{1,0:T(8,128)(2,1)S(1)}, bf16[416,256]{1,0:T(8,128)(2,1)S(1)}, u32[]{:S(2)}, u32[]{:S(2)}) collective-permute-start(bf16[416,256]{1,0:T(8,128)(2,1)S(1)} %get-tuple-element.47), channel_id=1, source_target_pairs={{0,4},{4,0},{8,12},{12,8},{1,5},{5,1},{9,13},{13,9},{2,6},{6,2},{1... | collective-permute-start | bytes 638984 | tf_op jit(solution)/shard_map/ppermute | solution.py:321
  5.8 12.0 %collective-permute-start.3 = (bf16[416,256]{1,0:T(8,128)(2,1)S(1)}, bf16[416,256]{1,0:T(8,128)(2,1)S(1)}, u32[]{:S(2)}, u32[]{:S(2)}) collective-permute-start(bf16[416,256]{1,0:T(8,128)(2,1)S(1)} %get-tuple-element.48), channel_id=1, source_target_pairs={{0,8},{4,12},{8,0},{12,4},{1,9},{5,13},{9,1},{13,5},{2,10},{6,14},... | collective-permute-start | bytes 638984 | tf_op jit(solution)/shard_map/ppermute | solution.py:321
  6.2 11.5 %collective-permute-start.4 = (bf16[416,256]{1,0:T(8,128)(2,1)S(1)}, bf16[416,256]{1,0:T(8,128)(2,1)S(1)}, u32[]{:S(2)}, u32[]{:S(2)}) collective-permute-start(bf16[416,256]{1,0:T(8,128)(2,1)S(1)} %get-tuple-element.49), channel_id=1, source_target_pairs={{0,12},{4,8},{8,4},{12,0},{1,13},{5,9},{9,5},{13,1},{2,14},{6,10},... | collective-permute-start | bytes 638984 | tf_op jit(solution)/shard_map/ppermute | solution.py:321
  10.9 8.2 %collective-permute-start = (bf16[48,1152]{1,0:T(8,128)(2,1)S(1)}, bf16[48,1152]{1,0:T(8,128)(2,1)S(1)}, u32[]{:S(2)}, u32[]{:S(2)}) collective-permute-start(bf16[48,1152]{1,0:T(8,128)(2,1)S(1)} %get-tuple-element.24), channel_id=1, source_target_pairs={{0,0},{1,1},{2,18},{3,19},{4,36},{5,37},{6,54},{7,55},{8,64},{9,65... | collective-permute-start | bytes 331784 | tf_op jit(solution)/shard_map/ppermute | solution.py:346
  14.4 6.3 %collective-permute-start.1 = (bf16[48,1152]{1,0:T(8,128)(2,1)S(1)}, bf16[48,1152]{1,0:T(8,128)(2,1)S(1)}, u32[]{:S(2)}, u32[]{:S(2)}) collective-permute-start(bf16[48,1152]{1,0:T(8,128)(2,1)S(1)} %get-tuple-element.25), channel_id=1, source_target_pairs={{0,64},{64,0},{1,65},{65,1},{2,66},{66,2},{3,67},{67,3},{4,68},{68... | collective-permute-start | bytes 331784 | tf_op jit(solution)/shard_map/ppermute | solution.py:347
  17.9 17.2 %copy-start.8 = (bf16[1024,128]{1,0:T(8,128)(2,1)S(1)}, bf16[1024,128]{1,0:T(8,128)(2,1)}, u32[]{:S(2)}) copy-start(bf16[1024,128]{1,0:T(8,128)(2,1)} %param.24) | copy-start | bytes 786436
  18.1 25.9 %copy-start.9 = (s32[512]{0:T(512)S(1)}, s32[512]{0:T(512)}, u32[]{:S(2)}) copy-start(s32[512]{0:T(512)} %param.20) | copy-start | bytes 6148
  18.1 26.6 %copy-start = (bf16[32,64,128]{2,1,0:T(8,128)(2,1)S(1)}, bf16[32,64,128]{2,1,0:T(8,128)(2,1)}, u32[]{:S(2)}) copy-start(bf16[32,64,128]{2,1,0:T(8,128)(2,1)} %refs_6_.1) | copy-start | bytes 1572868
  18.1 26.6 %copy-start.1 = (bf16[128,8]{0,1:T(8,128)(2,1)S(1)}, bf16[128,8]{0,1:T(8,128)(2,1)}, u32[]{:S(2)}) copy-start(bf16[128,8]{0,1:T(8,128)(2,1)} %param.25) | copy-start | bytes 6148
  21.8 20.5 %all-to-all-start = ((bf16[8,48,1152]{2,1,0:T(8,128)(2,1)}), bf16[8,48,1152]{2,1,0:T(8,128)(2,1)S(1)}, u32[]{:S(2)}, u32[]{:S(2)}) async-start(bf16[8,48,1152]{2,1,0:T(8,128)(2,1)} %broadcast_in_dim.5), calls=%async_computation | async-start | bytes 1769472 | tf_op jit(solution)/shard_map/all_to_all | solution.py:281
  30.9 10.7 %collective-permute-start.9 = (bf16[2,48,1152]{2,1,0:T(8,128)(2,1)S(1)}, bf16[2,48,1152]{2,1,0:T(8,128)(2,1)S(1)}, u32[]{:S(2)}, u32[]{:S(2)}) collective-permute-start(bf16[2,48,1152]{2,1,0:T(8,128)(2,1)S(1)} %pad_maximum_fusion.1.refs_0_), channel_id=1, source_target_pairs={{0,48},{16,32},{32,16},{48,0},{1,49},{17,33},{33,17},{49,1},{2,50}... | collective-permute-start | bytes 663560 | tf_op jit(solution)/shard_map/ppermute | solution.py:352
  32.0 9.6 %collective-permute-start.8 = (bf16[2,48,1152]{2,1,0:T(8,128)(2,1)S(1)}, bf16[2,48,1152]{2,1,0:T(8,128)(2,1)S(1)}, u32[]{:S(2)}, u32[]{:S(2)}) collective-permute-start(bf16[2,48,1152]{2,1,0:T(8,128)(2,1)S(1)} %pad_maximum_fusion.1.refs_0_), channel_id=1, source_target_pairs={{0,32},{16,48},{32,0},{48,16},{1,33},{17,49},{33,1},{49,17},{2,34}... | collective-permute-start | bytes 663560 | tf_op jit(solution)/shard_map/ppermute | solution.py:352
  33.7 8.6 %collective-permute-start.7 = (bf16[2,48,1152]{2,1,0:T(8,128)(2,1)S(1)}, bf16[2,48,1152]{2,1,0:T(8,128)(2,1)S(1)}, u32[]{:S(2)}, u32[]{:S(2)}) collective-permute-start(bf16[2,48,1152]{2,1,0:T(8,128)(2,1)S(1)} %pad_maximum_fusion.1.refs_0_), channel_id=1, source_target_pairs={{0,16},{16,0},{32,48},{48,32},{1,17},{17,1},{33,49},{49,33},{2,18}... | collective-permute-start | bytes 663560 | tf_op jit(solution)/shard_map/ppermute | solution.py:352
  42.2 2.4 %collective-permute-start.10 = (bf16[8,48,1152]{2,1,0:T(8,128)(2,1)S(1)}, bf16[8,48,1152]{2,1,0:T(8,128)(2,1)S(1)}, u32[]{:S(2)}, u32[]{:S(2)}) collective-permute-start(bf16[8,48,1152]{2,1,0:T(8,128)(2,1)S(1)} %all-to-all-done.refs_4_), channel_id=1, source_target_pairs={{0,1},{1,0},{2,3},{3,2},{4,5},{5,4},{6,7},{7,6},{8,9},{9,8},{10,11... | collective-permute-start | bytes 2654216 | tf_op jit(solution)/shard_map/ppermute | solution.py:357
  42.2 22.1 %collective-permute-start.6 = (bf16[4,416,256]{2,1,0:T(8,128)(2,1)}, bf16[4,416,256]{2,1,0:T(8,128)(2,1)}, u32[]{:S(2)}, u32[]{:S(2)}) collective-permute-start(bf16[4,416,256]{2,1,0:T(8,128)(2,1)} %bitcast.52), channel_id=1, source_target_pairs={{0,2},{2,0},{1,3},{3,1},{4,6},{6,4},{5,7},{7,5},{8,10},{10,8},{9,1... | collective-permute-start | bytes 2555912 | tf_op jit(solution)/shard_map/ppermute | solution.py:358
  43.7 20.6 %collective-permute-start.5 = (bf16[4,416,256]{2,1,0:T(8,128)(2,1)}, bf16[4,416,256]{2,1,0:T(8,128)(2,1)}, u32[]{:S(2)}, u32[]{:S(2)}) collective-permute-start(bf16[4,416,256]{2,1,0:T(8,128)(2,1)} %bitcast.53), channel_id=1, source_target_pairs={{0,1},{1,0},{2,3},{3,2},{4,5},{5,4},{6,7},{7,6},{8,9},{9,8},{10,11... | collective-permute-start | bytes 2555912 | tf_op jit(solution)/shard_map/ppermute | solution.py:359
  51.4 28.7 %all-to-all-start.1 = ((bf16[32,8,16,128]{3,2,1,0:T(8,128)(2,1)}), bf16[32,8,16,128]{3,2,1,0:T(8,128)(2,1)S(1)}, u32[]{:S(2)}, u32[]{:S(2)}) async-start(bf16[32,8,16,128]{3,2,1,0:T(8,128)(2,1)} %get-tuple-element.35), calls=%async_computation.1 | async-start | bytes 2097152 | tf_op jit(solution)/shard_map/all_to_all | solution.py:430
  64.3 2.6 %collective-permute-start.11 = (bf16[4,416,256]{2,1,0:T(8,128)(2,1)}, bf16[4,416,256]{2,1,0:T(8,128)(2,1)S(1)}, u32[]{:S(2)}, u32[]{:S(2)}) collective-permute-start(bf16[4,416,256]{2,1,0:T(8,128)(2,1)} %collective-permute-done.6.refs_2_.refs_6_), channel_id=1, source_target_pairs={{0,1},{1,0},{2,3},{3,2},{4,5},{5,4},{6,7},{7,6},{8,9},{9,8},{10,11... | collective-permute-start | bytes 2555912 | tf_op jit(solution)/shard_map/ppermute | solution.py:398
  64.4 15.7 %copy-start.2 = (bf16[256,256]{1,0:T(8,128)(2,1)S(1)}, bf16[256,256]{1,0:T(8,128)(2,1)}, u32[]{:S(2)}) copy-start(bf16[256,256]{1,0:T(8,128)(2,1)} %wo_ref.2) | copy-start | bytes 393220
  92.6 19.8 %copy-start.3 = (bf16[256,256]{1,0:T(8,128)(2,1)S(1)}, bf16[256,256]{1,0:T(8,128)(2,1)}, u32[]{:S(2)}) copy-start(bf16[256,256]{1,0:T(8,128)(2,1)} %wq_ref.1) | copy-start | bytes 393220
  92.6 19.8 %copy-start.4 = (bf16[256,256]{1,0:T(8,128)(2,1)S(1)}, bf16[256,256]{1,0:T(8,128)(2,1)}, u32[]{:S(2)}) copy-start(bf16[256,256]{1,0:T(8,128)(2,1)} %wk_ref.1) | copy-start | bytes 393220
  92.6 19.8 %copy-start.5 = (bf16[256,256]{1,0:T(8,128)(2,1)S(1)}, bf16[256,256]{1,0:T(8,128)(2,1)}, u32[]{:S(2)}) copy-start(bf16[256,256]{1,0:T(8,128)(2,1)} %wv_ref.1) | copy-start | bytes 393220
  92.7 19.8 %copy-start.6 = (bf16[256,256]{1,0:T(8,128)(2,1)S(1)}, bf16[256,256]{1,0:T(8,128)(2,1)}, u32[]{:S(2)}) copy-start(bf16[256,256]{1,0:T(8,128)(2,1)} %wg_ref.1) | copy-start | bytes 393220
  92.7 19.7 %copy-start.7 = (bf16[256,256]{1,0:T(8,128)(2,1)S(1)}, bf16[256,256]{1,0:T(8,128)(2,1)}, u32[]{:S(2)}) copy-start(bf16[256,256]{1,0:T(8,128)(2,1)} %wo_ref.3) | copy-start | bytes 393220

commit v6 on v5

--- a/solution.py
+++ b/solution.py
@@ -14,8 +14,8 @@
 BF16 = jnp.bfloat16
 NEG = -1e9
 STEP = 3
-TURN = 4
-PICK = 2
+TURN = 6
+PICK = 4
 SEQ = ("yh", "z")
 RES = ("yl", "xh", "xl", "core")
 ALL = SEQ + RES
@@ -23,7 +23,7 @@
 PLANE = SEQ + TEAM
 NT = (((1,), (1,)), ((), ()))
 TN = (((0,), (0,)), ((), ()))
-VMEM_LIMIT = 24 * 1024 * 1024
+VMEM_LIMIT = 28 * 1024 * 1024
 LOG2E = math.log2(math.e)
 
 

time: 138 us -> 138 us (level)
  no operation moved by 1% of the time
where the time goes in v6:
time: 138 us; the launch traced here: 136 us
  Pallas kernels  37.4 us (27%)
  blocking collectives  35 us (25%)
  starting transfers between devices  32.1 us (23%)
  waiting for transfers between devices  24.2 us (18%)
  other arithmetic  3.52 us (3%)
  local copies, waits for them, and re-layouts  3.18 us (2%)
    all_to_all x1, blocking collectives, body(): lax.all_to_all(middle.reshape(32, 12, 4, 256), PLANE, split_axis=0, conca...  19.1 us
    all_to_all x1, blocking collectives, body(): lax.all_to_all(columns, SEQ, split_axis=0, concat_axis=0, tiled=True)  15.9 us
    pallas_call x1, Pallas kernels, body(): pl.pallas_call(row_kernel, out_shape=jax.ShapeDtypeStruct((12, 128, 256),...  12.4 us
    all_to_all x1, starting transfers between devices, spread(): return lax.all_to_all(wide, axes, split_axis=0, concat_axis=0, tiled=True)  9.07 us
    all_to_all x1, starting transfers between devices, body(): bias = lax.all_to_all(bias, PLANE, split_axis=0, concat_axis=0, tiled=True)  8.5 us
    pallas_call x1, Pallas kernels, body(): pl.pallas_call(ready_kernel, out_shape=[pltpu.HBM(shape, kind) for shape,...  8.2 us
    ppermute x3, waiting for transfers between devices, body(): lax.ppermute(left, 'z', [(z, z ^ k) for z in range(4)])  7.09 us
    pallas_call x1, Pallas kernels, body(): pl.pallas_call(column_kernel, out_shape=jax.ShapeDtypeStruct((4, 384, 256...  6.9 us
  transfers between devices with their start and end apart: 14, of which 8 were waited for; matrix products, arithmetic and copies ran while one was open for 1% of the time, Pallas kernels for 13%

profile of v6, /device:TPU:8, one launch (start us, length us, event | category | flops | bytes accessed | tf_op | source)
XLA Modules:
  0.0 136.3 jit_solution(4141229071202591090)
XLA Ops:
  0.7 0.7 bitcast_convert_fusion
  1.4 1.3 fusion.1
  2.7 3.1 %collective-permute-start.2 = (bf16[416,256]{1,0:T(8,128)(2,1)S(1)}, bf16[416,256]{1,0:T(8,128)(2,1)S(1)}, u32[]{:S(2)}, u32[]{:S(2)}) collective-permute-start(bf16[416,256]{1,0:T(8,128)(2,1)S(1)} %get-tuple-element.47), channel_id=1, source_target_pairs={{0,4},{4,0},{8,12},{12,8},{1,5},{5,1},{9,13},{13,9},{2,6},{6,2},{1... | collective-permute-start | bytes 638984 | tf_op jit(solution)/shard_map/ppermute | solution.py:321
  5.8 0.4 collective-permute-start.3
  6.2 1.5 %collective-permute-start.4 = (bf16[416,256]{1,0:T(8,128)(2,1)S(1)}, bf16[416,256]{1,0:T(8,128)(2,1)S(1)}, u32[]{:S(2)}, u32[]{:S(2)}) collective-permute-start(bf16[416,256]{1,0:T(8,128)(2,1)S(1)} %get-tuple-element.49), channel_id=1, source_target_pairs={{0,12},{4,8},{8,4},{12,0},{1,13},{5,9},{9,5},{13,1},{2,14},{6,10},... | collective-permute-start | bytes 638984 | tf_op jit(solution)/shard_map/ppermute | solution.py:321
  7.8 3.2 %factors.1 = (bf16[48,1152]{1,0:T(8,128)(2,1)S(1)}, bf16[48,1152]{1,0:T(8,128)(2,1)S(1)}) custom-call(bf16[48,32,256]{2,1,0:T(8,128)(2,1)} %x_ref.1, s32[32,48]{1,0:T(8,128)} %bitcast.70, bf16[32,256]{1,0:T(8,128)(2,1)} %bitcast.71, bf16[32,256]{1,0:T(8,128)(2,1)} %bitcast.72), custom_call_target="tpu_custom_call" | custom-call | tf_op jit(solution)/shard_map/factors/pallas_call | solution.py:327
  10.9 3.5 %collective-permute-start = (bf16[48,1152]{1,0:T(8,128)(2,1)S(1)}, bf16[48,1152]{1,0:T(8,128)(2,1)S(1)}, u32[]{:S(2)}, u32[]{:S(2)}) collective-permute-start(bf16[48,1152]{1,0:T(8,128)(2,1)S(1)} %get-tuple-element.24), channel_id=1, source_target_pairs={{0,0},{1,1},{2,18},{3,19},{4,36},{5,37},{6,54},{7,55},{8,64},{9,65... | collective-permute-start | bytes 331784 | tf_op jit(solution)/shard_map/ppermute | solution.py:346
  14.4 0.1 collective-permute-start.1
  14.5 3.2 %collective-permute-done.3 = bf16[416,256]{1,0:T(8,128)(2,1)S(1)} collective-permute-done((bf16[416,256]{1,0:T(8,128)(2,1)S(1)}, bf16[416,256]{1,0:T(8,128)(2,1)S(1)}, u32[]{:S(2)}, u32[]{:S(2)}) %collective-permute-start.3) | collective-permute-done | bytes 213024 | tf_op jit(solution)/shard_map/ppermute | solution.py:321
  17.8 0.1 pad_maximum_fusion
  17.9 0.0 copy-start.8
  17.9 0.2 reverse_select_fusion.1
  18.1 0.0 copy-start.1
  18.1 1.1 reverse_select_fusion
  19.2 1.6 %collective-permute-done.1 = bf16[48,1152]{1,0:T(8,128)(2,1)S(1)} collective-permute-done((bf16[48,1152]{1,0:T(8,128)(2,1)S(1)}, bf16[48,1152]{1,0:T(8,128)(2,1)S(1)}, u32[]{:S(2)}, u32[]{:S(2)}) %collective-permute-start.1) | collective-permute-done | bytes 110624 | tf_op jit(solution)/shard_map/ppermute | solution.py:347
  20.8 1.0 broadcast_in_dim.5
  21.8 9.1 %all-to-all-start = ((bf16[8,48,1152]{2,1,0:T(8,128)(2,1)}), bf16[8,48,1152]{2,1,0:T(8,128)(2,1)S(1)}, u32[]{:S(2)}, u32[]{:S(2)}) async-start(bf16[8,48,1152]{2,1,0:T(8,128)(2,1)} %broadcast_in_dim.5), calls=%async_computation | async-start | bytes 1769472 | tf_op jit(solution)/shard_map/all_to_all | solution.py:281
  30.9 1.2 collective-permute-start.9
  32.0 1.7 %collective-permute-start.8 = (bf16[2,48,1152]{2,1,0:T(8,128)(2,1)S(1)}, bf16[2,48,1152]{2,1,0:T(8,128)(2,1)S(1)}, u32[]{:S(2)}, u32[]{:S(2)}) collective-permute-start(bf16[2,48,1152]{2,1,0:T(8,128)(2,1)S(1)} %pad_maximum_fusion.1.refs_0_), channel_id=1, source_target_pairs={{0,32},{16,48},{32,0},{48,16},{1,33},{17,49},{33,1},{49,17},{2,34}... | collective-permute-start | bytes 663560 | tf_op jit(solution)/shard_map/ppermute | solution.py:352
  33.7 1.4 collective-permute-start.7
  35.0 0.1 copy.29
  35.1 6.4 %collective-permute-done.9.refs_3_ = bf16[2,48,1152]{2,1,0:T(8,128)(2,1)S(1)} collective-permute-done((bf16[2,48,1152]{2,1,0:T(8,128)(2,1)S(1)}, bf16[2,48,1152]{2,1,0:T(8,128)(2,1)S(1)}, u32[]{:S(2)}, u32[]{:S(2)}) %collective-permute-start.9) | collective-permute-done | bytes 221216 | tf_op jit(solution)/shard_map/ppermute | solution.py:352
  41.6 0.7 collective-permute-done.7.refs_1_
  42.2 1.5 %collective-permute-start.6 = (bf16[4,416,256]{2,1,0:T(8,128)(2,1)}, bf16[4,416,256]{2,1,0:T(8,128)(2,1)}, u32[]{:S(2)}, u32[]{:S(2)}) collective-permute-start(bf16[4,416,256]{2,1,0:T(8,128)(2,1)} %bitcast.52), channel_id=1, source_target_pairs={{0,2},{2,0},{1,3},{3,1},{4,6},{6,4},{5,7},{7,5},{8,10},{10,8},{9,1... | collective-permute-start | bytes 2555912 | tf_op jit(solution)/shard_map/ppermute | solution.py:358
  43.7 0.2 collective-permute-start.5
  43.9 0.1 dynamic-slice_bitcast_fusion
  44.0 0.1 copy.30.refs_8_
  44.1 0.1 dynamic-slice_bitcast_fusion.1.refs_7_
  44.2 0.1 pad_add_fusion.at_ref
  44.3 0.4 collective-permute-done.10.refs_5_
  44.7 6.8 %pair.1 = (bf16[32,64,128]{2,1,0:T(8,128)(2,1)}, bf16[32,8,16,128]{3,2,1,0:T(8,128)(2,1)}, f32[8,384]{1,0:T(8,128)S(1)}) custom-call(s32[2]{0:T(128)S(1)} %pad_add_fusion.at_ref, bf16[2,48,1152]{2,1,0:T(8,128)(2,1)S(1)} %pad_maximum_fusion.1.refs_0_, bf16[2,48,1152]{2,1,0:T(8,128)(2,1)S(1)} %collective-permute-done.7.refs_1_, ...), custom_call_target="tpu_custom_call" | custom-call | flops 1000 | bytes 1000 | tf_op jit(solution)/shard_map/pair/pallas_call | solution.py:367
  51.4 8.5 %all-to-all-start.1 = ((bf16[32,8,16,128]{3,2,1,0:T(8,128)(2,1)}), bf16[32,8,16,128]{3,2,1,0:T(8,128)(2,1)S(1)}, u32[]{:S(2)}, u32[]{:S(2)}) async-start(bf16[32,8,16,128]{3,2,1,0:T(8,128)(2,1)} %get-tuple-element.35), calls=%async_computation.1 | async-start | bytes 2097152 | tf_op jit(solution)/shard_map/all_to_all | solution.py:430
  59.9 4.4 %collective-permute-done.6.refs_2_.refs_6_ = bf16[4,416,256]{2,1,0:T(8,128)(2,1)} collective-permute-done((bf16[4,416,256]{2,1,0:T(8,128)(2,1)}, bf16[4,416,256]{2,1,0:T(8,128)(2,1)}, u32[]{:S(2)}, u32[]{:S(2)}) %collective-permute-start.6) | collective-permute-done | bytes 852000 | tf_op jit(solution)/shard_map/ppermute | solution.py:358
  64.3 0.1 pad_add_fusion.1.at_ref
  64.4 2.5 %collective-permute-done.11.refs_3_.refs_7_ = bf16[4,416,256]{2,1,0:T(8,128)(2,1)S(1)} collective-permute-done((bf16[4,416,256]{2,1,0:T(8,128)(2,1)}, bf16[4,416,256]{2,1,0:T(8,128)(2,1)S(1)}, u32[]{:S(2)}, u32[]{:S(2)}) %collective-permute-start.11) | collective-permute-done | bytes 852000 | tf_op jit(solution)/shard_map/ppermute | solution.py:398
  66.9 8.2 %ready.1 = (bf16[12,256,128]{2,1,0:T(8,128)(2,1)}, bf16[12,512,256]{2,1,0:T(8,128)(2,1)}, bf16[12,256,512]{2,1,0:T(8,128)(2,1)}, f32[12,256,128]{2,1,0:T(8,128)}, bf16[512,128]{1,0:T(8,128)(2,1)}) custom-call(s32[2]{0:T(128)S(1)} %pad_add_fusion.1.at_ref, bf16[4,416,256]{2,1,0:T(8,128)(2,1)} %bitcast.54, ...), custom_call_target="tpu_custom_call" | custom-call | flops 1000 | bytes 1000 | tf_op jit(solution)/shard_map/ready/pallas_call | solution.py:402
  75.1 5.0 %all-to-all-done.1 = bf16[32,8,16,128]{3,2,1,0:T(8,128)(2,1)S(1)} async-done(((bf16[32,8,16,128]{3,2,1,0:T(8,128)(2,1)}), bf16[32,8,16,128]{3,2,1,0:T(8,128)(2,1)S(1)}, u32[]{:S(2)}, u32[]{:S(2)}) %all-to-all-start.1) | async-done | bytes 1048608 | tf_op jit(solution)/shard_map/all_to_all | solution.py:430
  80.1 12.4 %rows.1 = bf16[12,128,256]{2,1,0:T(8,128)(2,1)S(1)} custom-call(s32[1]{0:T(128)} %bitcast.at_ref, bf16[4,416,256]{2,1,0:T(8,128)(2,1)} %bitcast.56, bf16[12,256,128]{2,1,0:T(8,128)(2,1)} %get-tuple-element.39.query_ref, bf16[12,512,256]{2,1,0:T(8,128)(2,1)} %get-tuple-element.40.key_ref, bf16[12,256,512]{2,1,0:T(8,128)(2,1)} %get-tuple-element.41.value_ref, ...), custom_call_target="tpu_custom_call" | custom-call | flops 8000000000 | bytes 12000000 | tf_op jit(solution)/shard_map/rows/pallas_call | solution.py:434
  92.5 0.0 copy-start.5
  92.5 0.0 copy-start.6
  92.6 0.2 reshape.57
  92.8 0.3 copy.31
  93.1 19.1 %all_to_all.20 = bf16[32,12,4,256]{3,2,1,0:T(4,128)(2,1)S(1)} all-to-all(bf16[32,12,4,256]{3,2,1,0:T(4,128)(2,1)S(1)} %bitcast.59), channel_id=1, replica_groups=mesh['yh'=2,'z'=4,'yl'=2,'xh'=2,'xl'=2,'core'=2] {'yh','z','yl','xh'}, dimensions={0} | all-to-all | bytes 1572864 | tf_op jit(solution)/shard_map/all_to_all | solution.py:451
  112.2 0.1 copy.40
  112.3 6.9 %columns.1 = bf16[4,384,256]{2,1,0:T(8,128)(2,1)S(1)} custom-call(bf16[4,384,256]{2,1,0:T(8,128)(2,1)S(1)} %bitcast.48, f32[8,384]{1,0:T(8,128)S(1)} %get-tuple-element.44.mask_ref, bf16[256,256]{1,0:T(8,128)(2,1)S(1)} %copy-done.3, bf16[256,256]{1,0:T(8,128)(2,1)S(1)} %copy-done.4, bf16[256,256]{1,0:T(8,128)(2,1)S(1)} %copy-done.5, ...), custom_call_target="tpu_custom_call" | custom-call | flops 8000000000 | bytes 2000000 | tf_op jit(solution)/shard_map/columns/pallas_call | solution.py:455
  119.2 0.1 copy.39
  119.3 15.9 %all_to_all.21 = bf16[8,4,48,256]{3,2,1,0:T(8,128)(2,1)S(1)} all-to-all(bf16[8,4,48,256]{3,2,1,0:T(8,128)(2,1)S(1)} %bitcast.61), channel_id=1, replica_groups=mesh['yh'=2,'z'=4,'yl'=2,'xh'=2,'xl'=2,'core'=2] {'yh','z'}, dimensions={0} | all-to-all | bytes 1572864 | tf_op jit(solution)/shard_map/all_to_all | solution.py:484
  135.2 1.1 copy.38
  (28 shorter events, 0.1 us)
Async XLA Ops:
  2.7 11.8 %collective-permute-start.2 = (bf16[416,256]{1,0:T(8,128)(2,1)S(1)}, bf16[416,256]{1,0:T(8,128)(2,1)S(1)}, u32[]{:S(2)}, u32[]{:S(2)}) collective-permute-start(bf16[416,256]{1,0:T(8,128)(2,1)S(1)} %get-tuple-element.47), channel_id=1, source_target_pairs={{0,4},{4,0},{8,12},{12,8},{1,5},{5,1},{9,13},{13,9},{2,6},{6,2},{1... | collective-permute-start | bytes 638984 | tf_op jit(solution)/shard_map/ppermute | solution.py:321
  5.8 12.0 %collective-permute-start.3 = (bf16[416,256]{1,0:T(8,128)(2,1)S(1)}, bf16[416,256]{1,0:T(8,128)(2,1)S(1)}, u32[]{:S(2)}, u32[]{:S(2)}) collective-permute-start(bf16[416,256]{1,0:T(8,128)(2,1)S(1)} %get-tuple-element.48), channel_id=1, source_target_pairs={{0,8},{4,12},{8,0},{12,4},{1,9},{5,13},{9,1},{13,5},{2,10},{6,14},... | collective-permute-start | bytes 638984 | tf_op jit(solution)/shard_map/ppermute | solution.py:321
  6.2 11.5 %collective-permute-start.4 = (bf16[416,256]{1,0:T(8,128)(2,1)S(1)}, bf16[416,256]{1,0:T(8,128)(2,1)S(1)}, u32[]{:S(2)}, u32[]{:S(2)}) collective-permute-start(bf16[416,256]{1,0:T(8,128)(2,1)S(1)} %get-tuple-element.49), channel_id=1, source_target_pairs={{0,12},{4,8},{8,4},{12,0},{1,13},{5,9},{9,5},{13,1},{2,14},{6,10},... | collective-permute-start | bytes 638984 | tf_op jit(solution)/shard_map/ppermute | solution.py:321
  10.9 8.2 %collective-permute-start = (bf16[48,1152]{1,0:T(8,128)(2,1)S(1)}, bf16[48,1152]{1,0:T(8,128)(2,1)S(1)}, u32[]{:S(2)}, u32[]{:S(2)}) collective-permute-start(bf16[48,1152]{1,0:T(8,128)(2,1)S(1)} %get-tuple-element.24), channel_id=1, source_target_pairs={{0,0},{1,1},{2,18},{3,19},{4,36},{5,37},{6,54},{7,55},{8,64},{9,65... | collective-permute-start | bytes 331784 | tf_op jit(solution)/shard_map/ppermute | solution.py:346
  14.4 6.3 %collective-permute-start.1 = (bf16[48,1152]{1,0:T(8,128)(2,1)S(1)}, bf16[48,1152]{1,0:T(8,128)(2,1)S(1)}, u32[]{:S(2)}, u32[]{:S(2)}) collective-permute-start(bf16[48,1152]{1,0:T(8,128)(2,1)S(1)} %get-tuple-element.25), channel_id=1, source_target_pairs={{0,64},{64,0},{1,65},{65,1},{2,66},{66,2},{3,67},{67,3},{4,68},{68... | collective-permute-start | bytes 331784 | tf_op jit(solution)/shard_map/ppermute | solution.py:347
  17.9 17.2 %copy-start.8 = (bf16[1024,128]{1,0:T(8,128)(2,1)S(1)}, bf16[1024,128]{1,0:T(8,128)(2,1)}, u32[]{:S(2)}) copy-start(bf16[1024,128]{1,0:T(8,128)(2,1)} %param.24) | copy-start | bytes 786436
  18.1 25.9 %copy-start.9 = (s32[512]{0:T(512)S(1)}, s32[512]{0:T(512)}, u32[]{:S(2)}) copy-start(s32[512]{0:T(512)} %param.20) | copy-start | bytes 6148
  18.1 26.6 %copy-start = (bf16[32,64,128]{2,1,0:T(8,128)(2,1)S(1)}, bf16[32,64,128]{2,1,0:T(8,128)(2,1)}, u32[]{:S(2)}) copy-start(bf16[32,64,128]{2,1,0:T(8,128)(2,1)} %refs_6_.1) | copy-start | bytes 1572868
  18.1 26.6 %copy-start.1 = (bf16[128,8]{0,1:T(8,128)(2,1)S(1)}, bf16[128,8]{0,1:T(8,128)(2,1)}, u32[]{:S(2)}) copy-start(bf16[128,8]{0,1:T(8,128)(2,1)} %param.25) | copy-start | bytes 6148
  21.8 20.5 %all-to-all-start = ((bf16[8,48,1152]{2,1,0:T(8,128)(2,1)}), bf16[8,48,1152]{2,1,0:T(8,128)(2,1)S(1)}, u32[]{:S(2)}, u32[]{:S(2)}) async-start(bf16[8,48,1152]{2,1,0:T(8,128)(2,1)} %broadcast_in_dim.5), calls=%async_computation | async-start | bytes 1769472 | tf_op jit(solution)/shard_map/all_to_all | solution.py:281
  30.9 10.7 %collective-permute-start.9 = (bf16[2,48,1152]{2,1,0:T(8,128)(2,1)S(1)}, bf16[2,48,1152]{2,1,0:T(8,128)(2,1)S(1)}, u32[]{:S(2)}, u32[]{:S(2)}) collective-permute-start(bf16[2,48,1152]{2,1,0:T(8,128)(2,1)S(1)} %pad_maximum_fusion.1.refs_0_), channel_id=1, source_target_pairs={{0,48},{16,32},{32,16},{48,0},{1,49},{17,33},{33,17},{49,1},{2,50}... | collective-permute-start | bytes 663560 | tf_op jit(solution)/shard_map/ppermute | solution.py:352
  32.0 9.6 %collective-permute-start.8 = (bf16[2,48,1152]{2,1,0:T(8,128)(2,1)S(1)}, bf16[2,48,1152]{2,1,0:T(8,128)(2,1)S(1)}, u32[]{:S(2)}, u32[]{:S(2)}) collective-permute-start(bf16[2,48,1152]{2,1,0:T(8,128)(2,1)S(1)} %pad_maximum_fusion.1.refs_0_), channel_id=1, source_target_pairs={{0,32},{16,48},{32,0},{48,16},{1,33},{17,49},{33,1},{49,17},{2,34}... | collective-permute-start | bytes 663560 | tf_op jit(solution)/shard_map/ppermute | solution.py:352
  33.7 8.6 %collective-permute-start.7 = (bf16[2,48,1152]{2,1,0:T(8,128)(2,1)S(1)}, bf16[2,48,1152]{2,1,0:T(8,128)(2,1)S(1)}, u32[]{:S(2)}, u32[]{:S(2)}) collective-permute-start(bf16[2,48,1152]{2,1,0:T(8,128)(2,1)S(1)} %pad_maximum_fusion.1.refs_0_), channel_id=1, source_target_pairs={{0,16},{16,0},{32,48},{48,32},{1,17},{17,1},{33,49},{49,33},{2,18}... | collective-permute-start | bytes 663560 | tf_op jit(solution)/shard_map/ppermute | solution.py:352
  42.2 2.4 %collective-permute-start.10 = (bf16[8,48,1152]{2,1,0:T(8,128)(2,1)S(1)}, bf16[8,48,1152]{2,1,0:T(8,128)(2,1)S(1)}, u32[]{:S(2)}, u32[]{:S(2)}) collective-permute-start(bf16[8,48,1152]{2,1,0:T(8,128)(2,1)S(1)} %all-to-all-done.refs_4_), channel_id=1, source_target_pairs={{0,1},{1,0},{2,3},{3,2},{4,5},{5,4},{6,7},{7,6},{8,9},{9,8},{10,11... | collective-permute-start | bytes 2654216 | tf_op jit(solution)/shard_map/ppermute | solution.py:357
  42.2 22.1 %collective-permute-start.6 = (bf16[4,416,256]{2,1,0:T(8,128)(2,1)}, bf16[4,416,256]{2,1,0:T(8,128)(2,1)}, u32[]{:S(2)}, u32[]{:S(2)}) collective-permute-start(bf16[4,416,256]{2,1,0:T(8,128)(2,1)} %bitcast.52), channel_id=1, source_target_pairs={{0,2},{2,0},{1,3},{3,1},{4,6},{6,4},{5,7},{7,5},{8,10},{10,8},{9,1... | collective-permute-start | bytes 2555912 | tf_op jit(solution)/shard_map/ppermute | solution.py:358
  43.7 20.6 %collective-permute-start.5 = (bf16[4,416,256]{2,1,0:T(8,128)(2,1)}, bf16[4,416,256]{2,1,0:T(8,128)(2,1)}, u32[]{:S(2)}, u32[]{:S(2)}) collective-permute-start(bf16[4,416,256]{2,1,0:T(8,128)(2,1)} %bitcast.53), channel_id=1, source_target_pairs={{0,1},{1,0},{2,3},{3,2},{4,5},{5,4},{6,7},{7,6},{8,9},{9,8},{10,11... | collective-permute-start | bytes 2555912 | tf_op jit(solution)/shard_map/ppermute | solution.py:359
  51.4 28.7 %all-to-all-start.1 = ((bf16[32,8,16,128]{3,2,1,0:T(8,128)(2,1)}), bf16[32,8,16,128]{3,2,1,0:T(8,128)(2,1)S(1)}, u32[]{:S(2)}, u32[]{:S(2)}) async-start(bf16[32,8,16,128]{3,2,1,0:T(8,128)(2,1)} %get-tuple-element.35), calls=%async_computation.1 | async-start | bytes 2097152 | tf_op jit(solution)/shard_map/all_to_all | solution.py:430
  64.3 2.6 %collective-permute-start.11 = (bf16[4,416,256]{2,1,0:T(8,128)(2,1)}, bf16[4,416,256]{2,1,0:T(8,128)(2,1)S(1)}, u32[]{:S(2)}, u32[]{:S(2)}) collective-permute-start(bf16[4,416,256]{2,1,0:T(8,128)(2,1)} %collective-permute-done.6.refs_2_.refs_6_), channel_id=1, source_target_pairs={{0,1},{1,0},{2,3},{3,2},{4,5},{5,4},{6,7},{7,6},{8,9},{9,8},{10,11... | collective-permute-start | bytes 2555912 | tf_op jit(solution)/shard_map/ppermute | solution.py:398
  64.4 15.7 %copy-start.2 = (bf16[256,256]{1,0:T(8,128)(2,1)S(1)}, bf16[256,256]{1,0:T(8,128)(2,1)}, u32[]{:S(2)}) copy-start(bf16[256,256]{1,0:T(8,128)(2,1)} %wo_ref.2) | copy-start | bytes 393220
  92.5 19.8 %copy-start.3 = (bf16[256,256]{1,0:T(8,128)(2,1)S(1)}, bf16[256,256]{1,0:T(8,128)(2,1)}, u32[]{:S(2)}) copy-start(bf16[256,256]{1,0:T(8,128)(2,1)} %wq_ref.1) | copy-start | bytes 393220
  92.5 19.8 %copy-start.4 = (bf16[256,256]{1,0:T(8,128)(2,1)S(1)}, bf16[256,256]{1,0:T(8,128)(2,1)}, u32[]{:S(2)}) copy-start(bf16[256,256]{1,0:T(8,128)(2,1)} %wk_ref.1) | copy-start | bytes 393220
  92.5 19.8 %copy-start.5 = (bf16[256,256]{1,0:T(8,128)(2,1)S(1)}, bf16[256,256]{1,0:T(8,128)(2,1)}, u32[]{:S(2)}) copy-start(bf16[256,256]{1,0:T(8,128)(2,1)} %wv_ref.1) | copy-start | bytes 393220
  92.5 19.8 %copy-start.6 = (bf16[256,256]{1,0:T(8,128)(2,1)S(1)}, bf16[256,256]{1,0:T(8,128)(2,1)}, u32[]{:S(2)}) copy-start(bf16[256,256]{1,0:T(8,128)(2,1)} %wg_ref.1) | copy-start | bytes 393220
  92.6 19.8 %copy-start.7 = (bf16[256,256]{1,0:T(8,128)(2,1)S(1)}, bf16[256,256]{1,0:T(8,128)(2,1)}, u32[]{:S(2)}) copy-start(bf16[256,256]{1,0:T(8,128)(2,1)} %wo_ref.3) | copy-start | bytes 393220

commit v7 on v6

--- a/solution.py
+++ b/solution.py
@@ -86,14 +86,22 @@
 
 def run_pipelined(attentions, finish):
     units = [(a, unit) for a in attentions for unit in range(a.units)]
+
+    def close(attention, unit, weights):
+        attention.mix(unit, weights)
+        if unit == attention.units - 1:
+            finish(attentions.index(attention), attention.result())
+
     ahead = units[0][0].score(0)
+    behind = None
     for place, (attention, unit) in enumerate(units):
         scores = ahead
         if place + 1 < len(units):
             ahead = units[place + 1][0].score(units[place + 1][1])
-        attention.mix(unit, attention.weigh(unit, scores))
-        if unit == attention.units - 1:
-            finish(attentions.index(attention), attention.result())
+        if behind is not None:
+            close(*behind)
+        behind = (attention, unit, attention.weigh(unit, scores))
+    close(*behind)
 
 
 def mask_columns(mask_row):

time: 138 us -> 137 us (level)
  no operation moved by 1% of the time
where the time goes in v7:
time: 137 us; the launch traced here: 136 us
  Pallas kernels  37.2 us (27%)
  blocking collectives  35 us (26%)
  starting transfers between devices  32.1 us (23%)
  waiting for transfers between devices  24.2 us (18%)
  other arithmetic  3.52 us (3%)
  local copies, waits for them, and re-layouts  3.18 us (2%)
    all_to_all x1, blocking collectives, body(): lax.all_to_all(middle.reshape(32, 12, 4, 256), PLANE, split_axis=0, conca...  19.1 us
    all_to_all x1, blocking collectives, body(): lax.all_to_all(columns, SEQ, split_axis=0, concat_axis=0, tiled=True)  15.9 us
    pallas_call x1, Pallas kernels, body(): pl.pallas_call(row_kernel, out_shape=jax.ShapeDtypeStruct((12, 128, 256),...  12.3 us
    all_to_all x1, starting transfers between devices, spread(): return lax.all_to_all(wide, axes, split_axis=0, concat_axis=0, tiled=True)  9.07 us
    all_to_all x1, starting transfers between devices, body(): bias = lax.all_to_all(bias, PLANE, split_axis=0, concat_axis=0, tiled=True)  8.5 us
    pallas_call x1, Pallas kernels, body(): pl.pallas_call(ready_kernel, out_shape=[pltpu.HBM(shape, kind) for shape,...  8.2 us
    ppermute x3, waiting for transfers between devices, body(): lax.ppermute(left, 'z', [(z, z ^ k) for z in range(4)])  7.09 us
    pallas_call x1, Pallas kernels, body(): pl.pallas_call(column_kernel, out_shape=jax.ShapeDtypeStruct((4, 384, 256...  6.78 us
  transfers between devices with their start and end apart: 14, of which 8 were waited for; matrix products, arithmetic and copies ran while one was open for 1% of the time, Pallas kernels for 13%

profile of v7, /device:TPU:8, one launch (start us, length us, event | category | flops | bytes accessed | tf_op | source)
XLA Modules:
  0.0 136.1 jit_solution(17094307629982089093)
XLA Ops:
  0.7 0.7 bitcast_convert_fusion
  1.4 1.3 fusion.1
  2.7 3.1 %collective-permute-start.2 = (bf16[416,256]{1,0:T(8,128)(2,1)S(1)}, bf16[416,256]{1,0:T(8,128)(2,1)S(1)}, u32[]{:S(2)}, u32[]{:S(2)}) collective-permute-start(bf16[416,256]{1,0:T(8,128)(2,1)S(1)} %get-tuple-element.47), channel_id=1, source_target_pairs={{0,4},{4,0},{8,12},{12,8},{1,5},{5,1},{9,13},{13,9},{2,6},{6,2},{1... | collective-permute-start | bytes 638984 | tf_op jit(solution)/shard_map/ppermute | solution.py:329
  5.8 0.4 collective-permute-start.3
  6.2 1.5 %collective-permute-start.4 = (bf16[416,256]{1,0:T(8,128)(2,1)S(1)}, bf16[416,256]{1,0:T(8,128)(2,1)S(1)}, u32[]{:S(2)}, u32[]{:S(2)}) collective-permute-start(bf16[416,256]{1,0:T(8,128)(2,1)S(1)} %get-tuple-element.49), channel_id=1, source_target_pairs={{0,12},{4,8},{8,4},{12,0},{1,13},{5,9},{9,5},{13,1},{2,14},{6,10},... | collective-permute-start | bytes 638984 | tf_op jit(solution)/shard_map/ppermute | solution.py:329
  7.8 3.2 %factors.1 = (bf16[48,1152]{1,0:T(8,128)(2,1)S(1)}, bf16[48,1152]{1,0:T(8,128)(2,1)S(1)}) custom-call(bf16[48,32,256]{2,1,0:T(8,128)(2,1)} %x_ref.1, s32[32,48]{1,0:T(8,128)} %bitcast.70, bf16[32,256]{1,0:T(8,128)(2,1)} %bitcast.71, bf16[32,256]{1,0:T(8,128)(2,1)} %bitcast.72), custom_call_target="tpu_custom_call" | custom-call | tf_op jit(solution)/shard_map/factors/pallas_call | solution.py:335
  10.9 3.5 %collective-permute-start = (bf16[48,1152]{1,0:T(8,128)(2,1)S(1)}, bf16[48,1152]{1,0:T(8,128)(2,1)S(1)}, u32[]{:S(2)}, u32[]{:S(2)}) collective-permute-start(bf16[48,1152]{1,0:T(8,128)(2,1)S(1)} %get-tuple-element.24), channel_id=1, source_target_pairs={{0,0},{1,1},{2,18},{3,19},{4,36},{5,37},{6,54},{7,55},{8,64},{9,65... | collective-permute-start | bytes 331784 | tf_op jit(solution)/shard_map/ppermute | solution.py:354
  14.4 0.1 collective-permute-start.1
  14.5 3.2 %collective-permute-done.3 = bf16[416,256]{1,0:T(8,128)(2,1)S(1)} collective-permute-done((bf16[416,256]{1,0:T(8,128)(2,1)S(1)}, bf16[416,256]{1,0:T(8,128)(2,1)S(1)}, u32[]{:S(2)}, u32[]{:S(2)}) %collective-permute-start.3) | collective-permute-done | bytes 213024 | tf_op jit(solution)/shard_map/ppermute | solution.py:329
  17.8 0.1 pad_maximum_fusion
  17.9 0.0 copy-start.8
  17.9 0.2 reverse_select_fusion.1
  18.1 0.0 copy-start.9
  18.1 1.1 reverse_select_fusion
  19.2 1.6 %collective-permute-done.1 = bf16[48,1152]{1,0:T(8,128)(2,1)S(1)} collective-permute-done((bf16[48,1152]{1,0:T(8,128)(2,1)S(1)}, bf16[48,1152]{1,0:T(8,128)(2,1)S(1)}, u32[]{:S(2)}, u32[]{:S(2)}) %collective-permute-start.1) | collective-permute-done | bytes 110624 | tf_op jit(solution)/shard_map/ppermute | solution.py:355
  20.8 1.0 broadcast_in_dim.5
  21.8 9.1 %all-to-all-start = ((bf16[8,48,1152]{2,1,0:T(8,128)(2,1)}), bf16[8,48,1152]{2,1,0:T(8,128)(2,1)S(1)}, u32[]{:S(2)}, u32[]{:S(2)}) async-start(bf16[8,48,1152]{2,1,0:T(8,128)(2,1)} %broadcast_in_dim.5), calls=%async_computation | async-start | bytes 1769472 | tf_op jit(solution)/shard_map/all_to_all | solution.py:289
  30.9 1.2 collective-permute-start.9
  32.0 1.7 %collective-permute-start.8 = (bf16[2,48,1152]{2,1,0:T(8,128)(2,1)S(1)}, bf16[2,48,1152]{2,1,0:T(8,128)(2,1)S(1)}, u32[]{:S(2)}, u32[]{:S(2)}) collective-permute-start(bf16[2,48,1152]{2,1,0:T(8,128)(2,1)S(1)} %pad_maximum_fusion.1.refs_0_), channel_id=1, source_target_pairs={{0,32},{16,48},{32,0},{48,16},{1,33},{17,49},{33,1},{49,17},{2,34}... | collective-permute-start | bytes 663560 | tf_op jit(solution)/shard_map/ppermute | solution.py:360
  33.7 1.4 collective-permute-start.7
  35.0 0.1 copy.29
  35.1 6.4 %collective-permute-done.9.refs_3_ = bf16[2,48,1152]{2,1,0:T(8,128)(2,1)S(1)} collective-permute-done((bf16[2,48,1152]{2,1,0:T(8,128)(2,1)S(1)}, bf16[2,48,1152]{2,1,0:T(8,128)(2,1)S(1)}, u32[]{:S(2)}, u32[]{:S(2)}) %collective-permute-start.9) | collective-permute-done | bytes 221216 | tf_op jit(solution)/shard_map/ppermute | solution.py:360
  41.6 0.7 collective-permute-done.7.refs_1_
  42.2 1.5 %collective-permute-start.6 = (bf16[4,416,256]{2,1,0:T(8,128)(2,1)}, bf16[4,416,256]{2,1,0:T(8,128)(2,1)}, u32[]{:S(2)}, u32[]{:S(2)}) collective-permute-start(bf16[4,416,256]{2,1,0:T(8,128)(2,1)} %bitcast.52), channel_id=1, source_target_pairs={{0,2},{2,0},{1,3},{3,1},{4,6},{6,4},{5,7},{7,5},{8,10},{10,8},{9,1... | collective-permute-start | bytes 2555912 | tf_op jit(solution)/shard_map/ppermute | solution.py:366
  43.7 0.2 collective-permute-start.5
  43.9 0.1 dynamic-slice_bitcast_fusion
  44.0 0.1 copy.30.refs_8_
  44.1 0.1 dynamic-slice_bitcast_fusion.1.refs_7_
  44.2 0.1 pad_add_fusion.at_ref
  44.3 0.4 collective-permute-done.10.refs_5_
  44.7 6.8 %pair.1 = (bf16[32,64,128]{2,1,0:T(8,128)(2,1)}, bf16[32,8,16,128]{3,2,1,0:T(8,128)(2,1)}, f32[8,384]{1,0:T(8,128)S(1)}) custom-call(s32[2]{0:T(128)S(1)} %pad_add_fusion.at_ref, bf16[2,48,1152]{2,1,0:T(8,128)(2,1)S(1)} %pad_maximum_fusion.1.refs_0_, bf16[2,48,1152]{2,1,0:T(8,128)(2,1)S(1)} %collective-permute-done.7.refs_1_, ...), custom_call_target="tpu_custom_call" | custom-call | flops 1000 | bytes 1000 | tf_op jit(solution)/shard_map/pair/pallas_call | solution.py:375
  51.4 8.5 %all-to-all-start.1 = ((bf16[32,8,16,128]{3,2,1,0:T(8,128)(2,1)}), bf16[32,8,16,128]{3,2,1,0:T(8,128)(2,1)S(1)}, u32[]{:S(2)}, u32[]{:S(2)}) async-start(bf16[32,8,16,128]{3,2,1,0:T(8,128)(2,1)} %get-tuple-element.35), calls=%async_computation.1 | async-start | bytes 2097152 | tf_op jit(solution)/shard_map/all_to_all | solution.py:438
  59.9 4.4 %collective-permute-done.6.refs_2_.refs_6_ = bf16[4,416,256]{2,1,0:T(8,128)(2,1)} collective-permute-done((bf16[4,416,256]{2,1,0:T(8,128)(2,1)}, bf16[4,416,256]{2,1,0:T(8,128)(2,1)}, u32[]{:S(2)}, u32[]{:S(2)}) %collective-permute-start.6) | collective-permute-done | bytes 852000 | tf_op jit(solution)/shard_map/ppermute | solution.py:366
  64.3 0.1 pad_add_fusion.1.at_ref
  64.4 2.5 %collective-permute-done.11.refs_3_.refs_7_ = bf16[4,416,256]{2,1,0:T(8,128)(2,1)S(1)} collective-permute-done((bf16[4,416,256]{2,1,0:T(8,128)(2,1)}, bf16[4,416,256]{2,1,0:T(8,128)(2,1)S(1)}, u32[]{:S(2)}, u32[]{:S(2)}) %collective-permute-start.11) | collective-permute-done | bytes 852000 | tf_op jit(solution)/shard_map/ppermute | solution.py:406
  66.9 8.2 %ready.1 = (bf16[12,256,128]{2,1,0:T(8,128)(2,1)}, bf16[12,512,256]{2,1,0:T(8,128)(2,1)}, bf16[12,256,512]{2,1,0:T(8,128)(2,1)}, f32[12,256,128]{2,1,0:T(8,128)}, bf16[512,128]{1,0:T(8,128)(2,1)}) custom-call(s32[2]{0:T(128)S(1)} %pad_add_fusion.1.at_ref, bf16[4,416,256]{2,1,0:T(8,128)(2,1)} %bitcast.54, ...), custom_call_target="tpu_custom_call" | custom-call | flops 1000 | bytes 1000 | tf_op jit(solution)/shard_map/ready/pallas_call | solution.py:410
  75.1 5.0 %all-to-all-done.1 = bf16[32,8,16,128]{3,2,1,0:T(8,128)(2,1)S(1)} async-done(((bf16[32,8,16,128]{3,2,1,0:T(8,128)(2,1)}), bf16[32,8,16,128]{3,2,1,0:T(8,128)(2,1)S(1)}, u32[]{:S(2)}, u32[]{:S(2)}) %all-to-all-start.1) | async-done | bytes 1048608 | tf_op jit(solution)/shard_map/all_to_all | solution.py:438
  80.1 12.3 %rows.1 = bf16[12,128,256]{2,1,0:T(8,128)(2,1)S(1)} custom-call(s32[1]{0:T(128)} %bitcast.at_ref, bf16[4,416,256]{2,1,0:T(8,128)(2,1)} %bitcast.56, bf16[12,256,128]{2,1,0:T(8,128)(2,1)} %get-tuple-element.39.query_ref, bf16[12,512,256]{2,1,0:T(8,128)(2,1)} %get-tuple-element.40.key_ref, bf16[12,256,512]{2,1,0:T(8,128)(2,1)} %get-tuple-element.41.value_ref, ...), custom_call_target="tpu_custom_call" | custom-call | flops 8000000000 | bytes 12000000 | tf_op jit(solution)/shard_map/rows/pallas_call | solution.py:442
  92.4 0.0 copy-start.4
  92.5 0.0 copy-start.5
  92.5 0.2 reshape.57
  92.7 0.3 copy.31
  93.0 19.1 %all_to_all.20 = bf16[32,12,4,256]{3,2,1,0:T(4,128)(2,1)S(1)} all-to-all(bf16[32,12,4,256]{3,2,1,0:T(4,128)(2,1)S(1)} %bitcast.59), channel_id=1, replica_groups=mesh['yh'=2,'z'=4,'yl'=2,'xh'=2,'xl'=2,'core'=2] {'yh','z','yl','xh'}, dimensions={0} | all-to-all | bytes 1572864 | tf_op jit(solution)/shard_map/all_to_all | solution.py:459
  112.1 0.1 copy.40
  112.2 6.8 %columns.1 = bf16[4,384,256]{2,1,0:T(8,128)(2,1)S(1)} custom-call(bf16[4,384,256]{2,1,0:T(8,128)(2,1)S(1)} %bitcast.48, f32[8,384]{1,0:T(8,128)S(1)} %get-tuple-element.44.mask_ref, bf16[256,256]{1,0:T(8,128)(2,1)S(1)} %copy-done.3, bf16[256,256]{1,0:T(8,128)(2,1)S(1)} %copy-done.4, bf16[256,256]{1,0:T(8,128)(2,1)S(1)} %copy-done.5, ...), custom_call_target="tpu_custom_call" | custom-call | flops 8000000000 | bytes 2000000 | tf_op jit(solution)/shard_map/columns/pallas_call | solution.py:463
  119.0 0.1 copy.39
  119.1 15.9 %all_to_all.21 = bf16[8,4,48,256]{3,2,1,0:T(8,128)(2,1)S(1)} all-to-all(bf16[8,4,48,256]{3,2,1,0:T(8,128)(2,1)S(1)} %bitcast.61), channel_id=1, replica_groups=mesh['yh'=2,'z'=4,'yl'=2,'xh'=2,'xl'=2,'core'=2] {'yh','z'}, dimensions={0} | all-to-all | bytes 1572864 | tf_op jit(solution)/shard_map/all_to_all | solution.py:492
  135.0 1.1 copy.38
  (28 shorter events, 0.1 us)
Async XLA Ops:
  2.7 11.8 %collective-permute-start.2 = (bf16[416,256]{1,0:T(8,128)(2,1)S(1)}, bf16[416,256]{1,0:T(8,128)(2,1)S(1)}, u32[]{:S(2)}, u32[]{:S(2)}) collective-permute-start(bf16[416,256]{1,0:T(8,128)(2,1)S(1)} %get-tuple-element.47), channel_id=1, source_target_pairs={{0,4},{4,0},{8,12},{12,8},{1,5},{5,1},{9,13},{13,9},{2,6},{6,2},{1... | collective-permute-start | bytes 638984 | tf_op jit(solution)/shard_map/ppermute | solution.py:329
  5.8 12.0 %collective-permute-start.3 = (bf16[416,256]{1,0:T(8,128)(2,1)S(1)}, bf16[416,256]{1,0:T(8,128)(2,1)S(1)}, u32[]{:S(2)}, u32[]{:S(2)}) collective-permute-start(bf16[416,256]{1,0:T(8,128)(2,1)S(1)} %get-tuple-element.48), channel_id=1, source_target_pairs={{0,8},{4,12},{8,0},{12,4},{1,9},{5,13},{9,1},{13,5},{2,10},{6,14},... | collective-permute-start | bytes 638984 | tf_op jit(solution)/shard_map/ppermute | solution.py:329
  6.2 11.5 %collective-permute-start.4 = (bf16[416,256]{1,0:T(8,128)(2,1)S(1)}, bf16[416,256]{1,0:T(8,128)(2,1)S(1)}, u32[]{:S(2)}, u32[]{:S(2)}) collective-permute-start(bf16[416,256]{1,0:T(8,128)(2,1)S(1)} %get-tuple-element.49), channel_id=1, source_target_pairs={{0,12},{4,8},{8,4},{12,0},{1,13},{5,9},{9,5},{13,1},{2,14},{6,10},... | collective-permute-start | bytes 638984 | tf_op jit(solution)/shard_map/ppermute | solution.py:329
  10.9 8.2 %collective-permute-start = (bf16[48,1152]{1,0:T(8,128)(2,1)S(1)}, bf16[48,1152]{1,0:T(8,128)(2,1)S(1)}, u32[]{:S(2)}, u32[]{:S(2)}) collective-permute-start(bf16[48,1152]{1,0:T(8,128)(2,1)S(1)} %get-tuple-element.24), channel_id=1, source_target_pairs={{0,0},{1,1},{2,18},{3,19},{4,36},{5,37},{6,54},{7,55},{8,64},{9,65... | collective-permute-start | bytes 331784 | tf_op jit(solution)/shard_map/ppermute | solution.py:354
  14.4 6.3 %collective-permute-start.1 = (bf16[48,1152]{1,0:T(8,128)(2,1)S(1)}, bf16[48,1152]{1,0:T(8,128)(2,1)S(1)}, u32[]{:S(2)}, u32[]{:S(2)}) collective-permute-start(bf16[48,1152]{1,0:T(8,128)(2,1)S(1)} %get-tuple-element.25), channel_id=1, source_target_pairs={{0,64},{64,0},{1,65},{65,1},{2,66},{66,2},{3,67},{67,3},{4,68},{68... | collective-permute-start | bytes 331784 | tf_op jit(solution)/shard_map/ppermute | solution.py:355
  17.9 17.2 %copy-start.8 = (bf16[1024,128]{1,0:T(8,128)(2,1)S(1)}, bf16[1024,128]{1,0:T(8,128)(2,1)}, u32[]{:S(2)}) copy-start(bf16[1024,128]{1,0:T(8,128)(2,1)} %param.24) | copy-start | bytes 786436
  18.1 25.9 %copy-start.9 = (s32[512]{0:T(512)S(1)}, s32[512]{0:T(512)}, u32[]{:S(2)}) copy-start(s32[512]{0:T(512)} %param.20) | copy-start | bytes 6148
  18.1 26.6 %copy-start = (bf16[32,64,128]{2,1,0:T(8,128)(2,1)S(1)}, bf16[32,64,128]{2,1,0:T(8,128)(2,1)}, u32[]{:S(2)}) copy-start(bf16[32,64,128]{2,1,0:T(8,128)(2,1)} %refs_6_.1) | copy-start | bytes 1572868
  18.1 26.6 %copy-start.1 = (bf16[128,8]{0,1:T(8,128)(2,1)S(1)}, bf16[128,8]{0,1:T(8,128)(2,1)}, u32[]{:S(2)}) copy-start(bf16[128,8]{0,1:T(8,128)(2,1)} %param.25) | copy-start | bytes 6148
  21.8 20.5 %all-to-all-start = ((bf16[8,48,1152]{2,1,0:T(8,128)(2,1)}), bf16[8,48,1152]{2,1,0:T(8,128)(2,1)S(1)}, u32[]{:S(2)}, u32[]{:S(2)}) async-start(bf16[8,48,1152]{2,1,0:T(8,128)(2,1)} %broadcast_in_dim.5), calls=%async_computation | async-start | bytes 1769472 | tf_op jit(solution)/shard_map/all_to_all | solution.py:289
  30.9 10.7 %collective-permute-start.9 = (bf16[2,48,1152]{2,1,0:T(8,128)(2,1)S(1)}, bf16[2,48,1152]{2,1,0:T(8,128)(2,1)S(1)}, u32[]{:S(2)}, u32[]{:S(2)}) collective-permute-start(bf16[2,48,1152]{2,1,0:T(8,128)(2,1)S(1)} %pad_maximum_fusion.1.refs_0_), channel_id=1, source_target_pairs={{0,48},{16,32},{32,16},{48,0},{1,49},{17,33},{33,17},{49,1},{2,50}... | collective-permute-start | bytes 663560 | tf_op jit(solution)/shard_map/ppermute | solution.py:360
  32.0 9.6 %collective-permute-start.8 = (bf16[2,48,1152]{2,1,0:T(8,128)(2,1)S(1)}, bf16[2,48,1152]{2,1,0:T(8,128)(2,1)S(1)}, u32[]{:S(2)}, u32[]{:S(2)}) collective-permute-start(bf16[2,48,1152]{2,1,0:T(8,128)(2,1)S(1)} %pad_maximum_fusion.1.refs_0_), channel_id=1, source_target_pairs={{0,32},{16,48},{32,0},{48,16},{1,33},{17,49},{33,1},{49,17},{2,34}... | collective-permute-start | bytes 663560 | tf_op jit(solution)/shard_map/ppermute | solution.py:360
  33.7 8.6 %collective-permute-start.7 = (bf16[2,48,1152]{2,1,0:T(8,128)(2,1)S(1)}, bf16[2,48,1152]{2,1,0:T(8,128)(2,1)S(1)}, u32[]{:S(2)}, u32[]{:S(2)}) collective-permute-start(bf16[2,48,1152]{2,1,0:T(8,128)(2,1)S(1)} %pad_maximum_fusion.1.refs_0_), channel_id=1, source_target_pairs={{0,16},{16,0},{32,48},{48,32},{1,17},{17,1},{33,49},{49,33},{2,18}... | collective-permute-start | bytes 663560 | tf_op jit(solution)/shard_map/ppermute | solution.py:360
  42.2 2.4 %collective-permute-start.10 = (bf16[8,48,1152]{2,1,0:T(8,128)(2,1)S(1)}, bf16[8,48,1152]{2,1,0:T(8,128)(2,1)S(1)}, u32[]{:S(2)}, u32[]{:S(2)}) collective-permute-start(bf16[8,48,1152]{2,1,0:T(8,128)(2,1)S(1)} %all-to-all-done.refs_4_), channel_id=1, source_target_pairs={{0,1},{1,0},{2,3},{3,2},{4,5},{5,4},{6,7},{7,6},{8,9},{9,8},{10,11... | collective-permute-start | bytes 2654216 | tf_op jit(solution)/shard_map/ppermute | solution.py:365
  42.2 22.1 %collective-permute-start.6 = (bf16[4,416,256]{2,1,0:T(8,128)(2,1)}, bf16[4,416,256]{2,1,0:T(8,128)(2,1)}, u32[]{:S(2)}, u32[]{:S(2)}) collective-permute-start(bf16[4,416,256]{2,1,0:T(8,128)(2,1)} %bitcast.52), channel_id=1, source_target_pairs={{0,2},{2,0},{1,3},{3,1},{4,6},{6,4},{5,7},{7,5},{8,10},{10,8},{9,1... | collective-permute-start | bytes 2555912 | tf_op jit(solution)/shard_map/ppermute | solution.py:366
  43.7 20.6 %collective-permute-start.5 = (bf16[4,416,256]{2,1,0:T(8,128)(2,1)}, bf16[4,416,256]{2,1,0:T(8,128)(2,1)}, u32[]{:S(2)}, u32[]{:S(2)}) collective-permute-start(bf16[4,416,256]{2,1,0:T(8,128)(2,1)} %bitcast.53), channel_id=1, source_target_pairs={{0,1},{1,0},{2,3},{3,2},{4,5},{5,4},{6,7},{7,6},{8,9},{9,8},{10,11... | collective-permute-start | bytes 2555912 | tf_op jit(solution)/shard_map/ppermute | solution.py:367
  51.4 28.7 %all-to-all-start.1 = ((bf16[32,8,16,128]{3,2,1,0:T(8,128)(2,1)}), bf16[32,8,16,128]{3,2,1,0:T(8,128)(2,1)S(1)}, u32[]{:S(2)}, u32[]{:S(2)}) async-start(bf16[32,8,16,128]{3,2,1,0:T(8,128)(2,1)} %get-tuple-element.35), calls=%async_computation.1 | async-start | bytes 2097152 | tf_op jit(solution)/shard_map/all_to_all | solution.py:438
  64.3 2.6 %collective-permute-start.11 = (bf16[4,416,256]{2,1,0:T(8,128)(2,1)}, bf16[4,416,256]{2,1,0:T(8,128)(2,1)S(1)}, u32[]{:S(2)}, u32[]{:S(2)}) collective-permute-start(bf16[4,416,256]{2,1,0:T(8,128)(2,1)} %collective-permute-done.6.refs_2_.refs_6_), channel_id=1, source_target_pairs={{0,1},{1,0},{2,3},{3,2},{4,5},{5,4},{6,7},{7,6},{8,9},{9,8},{10,11... | collective-permute-start | bytes 2555912 | tf_op jit(solution)/shard_map/ppermute | solution.py:406
  64.4 15.7 %copy-start.2 = (bf16[256,256]{1,0:T(8,128)(2,1)S(1)}, bf16[256,256]{1,0:T(8,128)(2,1)}, u32[]{:S(2)}) copy-start(bf16[256,256]{1,0:T(8,128)(2,1)} %wo_ref.2) | copy-start | bytes 393220
  92.4 19.8 %copy-start.3 = (bf16[256,256]{1,0:T(8,128)(2,1)S(1)}, bf16[256,256]{1,0:T(8,128)(2,1)}, u32[]{:S(2)}) copy-start(bf16[256,256]{1,0:T(8,128)(2,1)} %wq_ref.1) | copy-start | bytes 393220
  92.4 19.8 %copy-start.4 = (bf16[256,256]{1,0:T(8,128)(2,1)S(1)}, bf16[256,256]{1,0:T(8,128)(2,1)}, u32[]{:S(2)}) copy-start(bf16[256,256]{1,0:T(8,128)(2,1)} %wk_ref.1) | copy-start | bytes 393220
  92.5 19.8 %copy-start.5 = (bf16[256,256]{1,0:T(8,128)(2,1)S(1)}, bf16[256,256]{1,0:T(8,128)(2,1)}, u32[]{:S(2)}) copy-start(bf16[256,256]{1,0:T(8,128)(2,1)} %wv_ref.1) | copy-start | bytes 393220
  92.5 19.8 %copy-start.6 = (bf16[256,256]{1,0:T(8,128)(2,1)S(1)}, bf16[256,256]{1,0:T(8,128)(2,1)}, u32[]{:S(2)}) copy-start(bf16[256,256]{1,0:T(8,128)(2,1)} %wg_ref.1) | copy-start | bytes 393220
  92.5 19.7 %copy-start.7 = (bf16[256,256]{1,0:T(8,128)(2,1)S(1)}, bf16[256,256]{1,0:T(8,128)(2,1)}, u32[]{:S(2)}) copy-start(bf16[256,256]{1,0:T(8,128)(2,1)} %wo_ref.3) | copy-start | bytes 393220

commit v8 on v6

--- a/solution.py
+++ b/solution.py
@@ -13,7 +13,7 @@
 F32 = jnp.float32
 BF16 = jnp.bfloat16
 NEG = -1e9
-STEP = 3
+STEP = 6
 TURN = 6
 PICK = 4
 SEQ = ("yh", "z")

time: 138 us -> 139 us (level)
  transfers between devices with their start and end apart: 14 -> 14, of which waited for: 8 -> 8; matrix products, arithmetic and copies ran while one was open for 1% -> 1% of each run, Pallas kernels for 13% -> 14%
where the time goes in v8:
time: 139 us; the launch traced here: 137 us
  Pallas kernels  38.2 us (27%)
  blocking collectives  35.7 us (26%)
  starting transfers between devices  32.1 us (23%)
  waiting for transfers between devices  23.4 us (17%)
  other arithmetic  3.52 us (3%)
  local copies, waits for them, and re-layouts  3.18 us (2%)
    all_to_all x1, blocking collectives, body(): lax.all_to_all(middle.reshape(32, 12, 4, 256), PLANE, split_axis=0, conca...  19.7 us
    all_to_all x1, blocking collectives, body(): lax.all_to_all(columns, SEQ, split_axis=0, concat_axis=0, tiled=True)  16 us
    pallas_call x1, Pallas kernels, body(): pl.pallas_call(row_kernel, out_shape=jax.ShapeDtypeStruct((12, 128, 256),...  12.4 us
    all_to_all x1, starting transfers between devices, spread(): return lax.all_to_all(wide, axes, split_axis=0, concat_axis=0, tiled=True)  9.07 us
    pallas_call x1, Pallas kernels, body(): pl.pallas_call(ready_kernel, out_shape=[pltpu.HBM(shape, kind) for shape,...  8.98 us
    all_to_all x1, starting transfers between devices, body(): bias = lax.all_to_all(bias, PLANE, split_axis=0, concat_axis=0, tiled=True)  8.5 us
    ppermute x3, waiting for transfers between devices, body(): lax.ppermute(left, 'z', [(z, z ^ k) for z in range(4)])  7.09 us
    pallas_call x1, Pallas kernels, body(): pl.pallas_call(column_kernel, out_shape=jax.ShapeDtypeStruct((4, 384, 256...  6.9 us
  transfers between devices with their start and end apart: 14, of which 8 were waited for; matrix products, arithmetic and copies ran while one was open for 1% of the time, Pallas kernels for 14%

profile of v8, /device:TPU:8, one launch (start us, length us, event | category | flops | bytes accessed | tf_op | source)
XLA Modules:
  0.0 137.0 jit_solution(7093961986732733024)
XLA Ops:
  0.7 0.7 bitcast_convert_fusion
  1.4 1.3 fusion.1
  2.7 3.1 %collective-permute-start.2 = (bf16[416,256]{1,0:T(8,128)(2,1)S(1)}, bf16[416,256]{1,0:T(8,128)(2,1)S(1)}, u32[]{:S(2)}, u32[]{:S(2)}) collective-permute-start(bf16[416,256]{1,0:T(8,128)(2,1)S(1)} %get-tuple-element.47), channel_id=1, source_target_pairs={{0,4},{4,0},{8,12},{12,8},{1,5},{5,1},{9,13},{13,9},{2,6},{6,2},{1... | collective-permute-start | bytes 638984 | tf_op jit(solution)/shard_map/ppermute | solution.py:321
  5.8 0.4 collective-permute-start.3
  6.2 1.5 %collective-permute-start.4 = (bf16[416,256]{1,0:T(8,128)(2,1)S(1)}, bf16[416,256]{1,0:T(8,128)(2,1)S(1)}, u32[]{:S(2)}, u32[]{:S(2)}) collective-permute-start(bf16[416,256]{1,0:T(8,128)(2,1)S(1)} %get-tuple-element.49), channel_id=1, source_target_pairs={{0,12},{4,8},{8,4},{12,0},{1,13},{5,9},{9,5},{13,1},{2,14},{6,10},... | collective-permute-start | bytes 638984 | tf_op jit(solution)/shard_map/ppermute | solution.py:321
  7.8 3.2 %factors.1 = (bf16[48,1152]{1,0:T(8,128)(2,1)S(1)}, bf16[48,1152]{1,0:T(8,128)(2,1)S(1)}) custom-call(bf16[48,32,256]{2,1,0:T(8,128)(2,1)} %x_ref.1, s32[32,48]{1,0:T(8,128)} %bitcast.70, bf16[32,256]{1,0:T(8,128)(2,1)} %bitcast.71, bf16[32,256]{1,0:T(8,128)(2,1)} %bitcast.72), custom_call_target="tpu_custom_call" | custom-call | tf_op jit(solution)/shard_map/factors/pallas_call | solution.py:327
  10.9 3.5 %collective-permute-start = (bf16[48,1152]{1,0:T(8,128)(2,1)S(1)}, bf16[48,1152]{1,0:T(8,128)(2,1)S(1)}, u32[]{:S(2)}, u32[]{:S(2)}) collective-permute-start(bf16[48,1152]{1,0:T(8,128)(2,1)S(1)} %get-tuple-element.24), channel_id=1, source_target_pairs={{0,0},{1,1},{2,18},{3,19},{4,36},{5,37},{6,54},{7,55},{8,64},{9,65... | collective-permute-start | bytes 331784 | tf_op jit(solution)/shard_map/ppermute | solution.py:346
  14.4 0.1 collective-permute-start.1
  14.5 3.2 %collective-permute-done.3 = bf16[416,256]{1,0:T(8,128)(2,1)S(1)} collective-permute-done((bf16[416,256]{1,0:T(8,128)(2,1)S(1)}, bf16[416,256]{1,0:T(8,128)(2,1)S(1)}, u32[]{:S(2)}, u32[]{:S(2)}) %collective-permute-start.3) | collective-permute-done | bytes 213024 | tf_op jit(solution)/shard_map/ppermute | solution.py:321
  17.8 0.1 pad_maximum_fusion
  17.9 0.2 reverse_select_fusion.1
  18.1 0.0 copy-start
  18.1 0.0 copy-start.1
  18.1 1.1 reverse_select_fusion
  19.2 1.6 %collective-permute-done.1 = bf16[48,1152]{1,0:T(8,128)(2,1)S(1)} collective-permute-done((bf16[48,1152]{1,0:T(8,128)(2,1)S(1)}, bf16[48,1152]{1,0:T(8,128)(2,1)S(1)}, u32[]{:S(2)}, u32[]{:S(2)}) %collective-permute-start.1) | collective-permute-done | bytes 110624 | tf_op jit(solution)/shard_map/ppermute | solution.py:347
  20.8 1.0 broadcast_in_dim.5
  21.8 9.1 %all-to-all-start = ((bf16[8,48,1152]{2,1,0:T(8,128)(2,1)}), bf16[8,48,1152]{2,1,0:T(8,128)(2,1)S(1)}, u32[]{:S(2)}, u32[]{:S(2)}) async-start(bf16[8,48,1152]{2,1,0:T(8,128)(2,1)} %broadcast_in_dim.5), calls=%async_computation | async-start | bytes 1769472 | tf_op jit(solution)/shard_map/all_to_all | solution.py:281
  30.9 1.2 collective-permute-start.9
  32.0 1.7 %collective-permute-start.8 = (bf16[2,48,1152]{2,1,0:T(8,128)(2,1)S(1)}, bf16[2,48,1152]{2,1,0:T(8,128)(2,1)S(1)}, u32[]{:S(2)}, u32[]{:S(2)}) collective-permute-start(bf16[2,48,1152]{2,1,0:T(8,128)(2,1)S(1)} %pad_maximum_fusion.1.refs_0_), channel_id=1, source_target_pairs={{0,32},{16,48},{32,0},{48,16},{1,33},{17,49},{33,1},{49,17},{2,34}... | collective-permute-start | bytes 663560 | tf_op jit(solution)/shard_map/ppermute | solution.py:352
  33.7 1.4 collective-permute-start.7
  35.0 0.1 copy.29
  35.1 6.4 %collective-permute-done.9.refs_3_ = bf16[2,48,1152]{2,1,0:T(8,128)(2,1)S(1)} collective-permute-done((bf16[2,48,1152]{2,1,0:T(8,128)(2,1)S(1)}, bf16[2,48,1152]{2,1,0:T(8,128)(2,1)S(1)}, u32[]{:S(2)}, u32[]{:S(2)}) %collective-permute-start.9) | collective-permute-done | bytes 221216 | tf_op jit(solution)/shard_map/ppermute | solution.py:352
  41.6 0.7 collective-permute-done.7.refs_1_
  42.2 1.5 %collective-permute-start.6 = (bf16[4,416,256]{2,1,0:T(8,128)(2,1)}, bf16[4,416,256]{2,1,0:T(8,128)(2,1)}, u32[]{:S(2)}, u32[]{:S(2)}) collective-permute-start(bf16[4,416,256]{2,1,0:T(8,128)(2,1)} %bitcast.52), channel_id=1, source_target_pairs={{0,2},{2,0},{1,3},{3,1},{4,6},{6,4},{5,7},{7,5},{8,10},{10,8},{9,1... | collective-permute-start | bytes 2555912 | tf_op jit(solution)/shard_map/ppermute | solution.py:358
  43.7 0.2 collective-permute-start.5
  43.9 0.1 dynamic-slice_bitcast_fusion
  44.0 0.1 copy.30.refs_8_
  44.1 0.1 dynamic-slice_bitcast_fusion.1.refs_7_
  44.2 0.1 pad_add_fusion.at_ref
  44.3 0.4 collective-permute-done.10.refs_5_
  44.7 6.8 %pair.1 = (bf16[32,64,128]{2,1,0:T(8,128)(2,1)}, bf16[32,8,16,128]{3,2,1,0:T(8,128)(2,1)}, f32[8,384]{1,0:T(8,128)S(1)}) custom-call(s32[2]{0:T(128)S(1)} %pad_add_fusion.at_ref, bf16[2,48,1152]{2,1,0:T(8,128)(2,1)S(1)} %pad_maximum_fusion.1.refs_0_, bf16[2,48,1152]{2,1,0:T(8,128)(2,1)S(1)} %collective-permute-done.7.refs_1_, ...), custom_call_target="tpu_custom_call" | custom-call | flops 1000 | bytes 1000 | tf_op jit(solution)/shard_map/pair/pallas_call | solution.py:367
  51.4 8.5 %all-to-all-start.1 = ((bf16[32,8,16,128]{3,2,1,0:T(8,128)(2,1)}), bf16[32,8,16,128]{3,2,1,0:T(8,128)(2,1)S(1)}, u32[]{:S(2)}, u32[]{:S(2)}) async-start(bf16[32,8,16,128]{3,2,1,0:T(8,128)(2,1)} %get-tuple-element.35), calls=%async_computation.1 | async-start | bytes 2097152 | tf_op jit(solution)/shard_map/all_to_all | solution.py:430
  59.9 4.4 %collective-permute-done.6.refs_2_.refs_6_ = bf16[4,416,256]{2,1,0:T(8,128)(2,1)} collective-permute-done((bf16[4,416,256]{2,1,0:T(8,128)(2,1)}, bf16[4,416,256]{2,1,0:T(8,128)(2,1)}, u32[]{:S(2)}, u32[]{:S(2)}) %collective-permute-start.6) | collective-permute-done | bytes 852000 | tf_op jit(solution)/shard_map/ppermute | solution.py:358
  64.3 0.1 pad_add_fusion.1.at_ref
  64.4 2.5 %collective-permute-done.11.refs_3_.refs_7_ = bf16[4,416,256]{2,1,0:T(8,128)(2,1)S(1)} collective-permute-done((bf16[4,416,256]{2,1,0:T(8,128)(2,1)}, bf16[4,416,256]{2,1,0:T(8,128)(2,1)S(1)}, u32[]{:S(2)}, u32[]{:S(2)}) %collective-permute-start.11) | collective-permute-done | bytes 852000 | tf_op jit(solution)/shard_map/ppermute | solution.py:398
  66.9 9.0 %ready.1 = (bf16[12,256,128]{2,1,0:T(8,128)(2,1)}, bf16[12,512,256]{2,1,0:T(8,128)(2,1)}, bf16[12,256,512]{2,1,0:T(8,128)(2,1)}, f32[12,256,128]{2,1,0:T(8,128)}, bf16[512,128]{1,0:T(8,128)(2,1)}) custom-call(s32[2]{0:T(128)S(1)} %pad_add_fusion.1.at_ref, bf16[4,416,256]{2,1,0:T(8,128)(2,1)} %bitcast.54, ...), custom_call_target="tpu_custom_call" | custom-call | flops 1000 | bytes 1000 | tf_op jit(solution)/shard_map/ready/pallas_call | solution.py:402
  75.9 4.2 %all-to-all-done.1 = bf16[32,8,16,128]{3,2,1,0:T(8,128)(2,1)S(1)} async-done(((bf16[32,8,16,128]{3,2,1,0:T(8,128)(2,1)}), bf16[32,8,16,128]{3,2,1,0:T(8,128)(2,1)S(1)}, u32[]{:S(2)}, u32[]{:S(2)}) %all-to-all-start.1) | async-done | bytes 1048608 | tf_op jit(solution)/shard_map/all_to_all | solution.py:430
  80.1 12.4 %rows.1 = bf16[12,128,256]{2,1,0:T(8,128)(2,1)S(1)} custom-call(s32[1]{0:T(128)} %bitcast.at_ref, bf16[4,416,256]{2,1,0:T(8,128)(2,1)} %bitcast.56, bf16[12,256,128]{2,1,0:T(8,128)(2,1)} %get-tuple-element.39.query_ref, bf16[12,512,256]{2,1,0:T(8,128)(2,1)} %get-tuple-element.40.key_ref, bf16[12,256,512]{2,1,0:T(8,128)(2,1)} %get-tuple-element.41.value_ref, ...), custom_call_target="tpu_custom_call" | custom-call | flops 8000000000 | bytes 12000000 | tf_op jit(solution)/shard_map/rows/pallas_call | solution.py:434
  92.5 0.0 copy-start.5
  92.5 0.0 copy-start.6
  92.6 0.2 reshape.57
  92.8 0.3 copy.31
  93.1 19.7 %all_to_all.20 = bf16[32,12,4,256]{3,2,1,0:T(4,128)(2,1)S(1)} all-to-all(bf16[32,12,4,256]{3,2,1,0:T(4,128)(2,1)S(1)} %bitcast.59), channel_id=1, replica_groups=mesh['yh'=2,'z'=4,'yl'=2,'xh'=2,'xl'=2,'core'=2] {'yh','z','yl','xh'}, dimensions={0} | all-to-all | bytes 1572864 | tf_op jit(solution)/shard_map/all_to_all | solution.py:451
  112.8 0.1 copy.40
  112.9 6.9 %columns.1 = bf16[4,384,256]{2,1,0:T(8,128)(2,1)S(1)} custom-call(bf16[4,384,256]{2,1,0:T(8,128)(2,1)S(1)} %bitcast.48, f32[8,384]{1,0:T(8,128)S(1)} %get-tuple-element.44.mask_ref, bf16[256,256]{1,0:T(8,128)(2,1)S(1)} %copy-done.3, bf16[256,256]{1,0:T(8,128)(2,1)S(1)} %copy-done.4, bf16[256,256]{1,0:T(8,128)(2,1)S(1)} %copy-done.5, ...), custom_call_target="tpu_custom_call" | custom-call | flops 8000000000 | bytes 2000000 | tf_op jit(solution)/shard_map/columns/pallas_call | solution.py:455
  119.8 0.1 copy.39
  119.9 16.0 %all_to_all.21 = bf16[8,4,48,256]{3,2,1,0:T(8,128)(2,1)S(1)} all-to-all(bf16[8,4,48,256]{3,2,1,0:T(8,128)(2,1)S(1)} %bitcast.61), channel_id=1, replica_groups=mesh['yh'=2,'z'=4,'yl'=2,'xh'=2,'xl'=2,'core'=2] {'yh','z'}, dimensions={0} | all-to-all | bytes 1572864 | tf_op jit(solution)/shard_map/all_to_all | solution.py:484
  135.9 1.1 copy.38
  (28 shorter events, 0.1 us)
Async XLA Ops:
  2.7 11.8 %collective-permute-start.2 = (bf16[416,256]{1,0:T(8,128)(2,1)S(1)}, bf16[416,256]{1,0:T(8,128)(2,1)S(1)}, u32[]{:S(2)}, u32[]{:S(2)}) collective-permute-start(bf16[416,256]{1,0:T(8,128)(2,1)S(1)} %get-tuple-element.47), channel_id=1, source_target_pairs={{0,4},{4,0},{8,12},{12,8},{1,5},{5,1},{9,13},{13,9},{2,6},{6,2},{1... | collective-permute-start | bytes 638984 | tf_op jit(solution)/shard_map/ppermute | solution.py:321
  5.8 12.0 %collective-permute-start.3 = (bf16[416,256]{1,0:T(8,128)(2,1)S(1)}, bf16[416,256]{1,0:T(8,128)(2,1)S(1)}, u32[]{:S(2)}, u32[]{:S(2)}) collective-permute-start(bf16[416,256]{1,0:T(8,128)(2,1)S(1)} %get-tuple-element.48), channel_id=1, source_target_pairs={{0,8},{4,12},{8,0},{12,4},{1,9},{5,13},{9,1},{13,5},{2,10},{6,14},... | collective-permute-start | bytes 638984 | tf_op jit(solution)/shard_map/ppermute | solution.py:321
  6.2 11.5 %collective-permute-start.4 = (bf16[416,256]{1,0:T(8,128)(2,1)S(1)}, bf16[416,256]{1,0:T(8,128)(2,1)S(1)}, u32[]{:S(2)}, u32[]{:S(2)}) collective-permute-start(bf16[416,256]{1,0:T(8,128)(2,1)S(1)} %get-tuple-element.49), channel_id=1, source_target_pairs={{0,12},{4,8},{8,4},{12,0},{1,13},{5,9},{9,5},{13,1},{2,14},{6,10},... | collective-permute-start | bytes 638984 | tf_op jit(solution)/shard_map/ppermute | solution.py:321
  10.9 8.2 %collective-permute-start = (bf16[48,1152]{1,0:T(8,128)(2,1)S(1)}, bf16[48,1152]{1,0:T(8,128)(2,1)S(1)}, u32[]{:S(2)}, u32[]{:S(2)}) collective-permute-start(bf16[48,1152]{1,0:T(8,128)(2,1)S(1)} %get-tuple-element.24), channel_id=1, source_target_pairs={{0,0},{1,1},{2,18},{3,19},{4,36},{5,37},{6,54},{7,55},{8,64},{9,65... | collective-permute-start | bytes 331784 | tf_op jit(solution)/shard_map/ppermute | solution.py:346
  14.4 6.3 %collective-permute-start.1 = (bf16[48,1152]{1,0:T(8,128)(2,1)S(1)}, bf16[48,1152]{1,0:T(8,128)(2,1)S(1)}, u32[]{:S(2)}, u32[]{:S(2)}) collective-permute-start(bf16[48,1152]{1,0:T(8,128)(2,1)S(1)} %get-tuple-element.25), channel_id=1, source_target_pairs={{0,64},{64,0},{1,65},{65,1},{2,66},{66,2},{3,67},{67,3},{4,68},{68... | collective-permute-start | bytes 331784 | tf_op jit(solution)/shard_map/ppermute | solution.py:347
  17.9 17.2 %copy-start.8 = (bf16[1024,128]{1,0:T(8,128)(2,1)S(1)}, bf16[1024,128]{1,0:T(8,128)(2,1)}, u32[]{:S(2)}) copy-start(bf16[1024,128]{1,0:T(8,128)(2,1)} %param.24) | copy-start | bytes 786436
  18.1 25.9 %copy-start.9 = (s32[512]{0:T(512)S(1)}, s32[512]{0:T(512)}, u32[]{:S(2)}) copy-start(s32[512]{0:T(512)} %param.20) | copy-start | bytes 6148
  18.1 26.6 %copy-start = (bf16[32,64,128]{2,1,0:T(8,128)(2,1)S(1)}, bf16[32,64,128]{2,1,0:T(8,128)(2,1)}, u32[]{:S(2)}) copy-start(bf16[32,64,128]{2,1,0:T(8,128)(2,1)} %refs_6_.1) | copy-start | bytes 1572868
  18.1 26.6 %copy-start.1 = (bf16[128,8]{0,1:T(8,128)(2,1)S(1)}, bf16[128,8]{0,1:T(8,128)(2,1)}, u32[]{:S(2)}) copy-start(bf16[128,8]{0,1:T(8,128)(2,1)} %param.25) | copy-start | bytes 6148
  21.8 20.5 %all-to-all-start = ((bf16[8,48,1152]{2,1,0:T(8,128)(2,1)}), bf16[8,48,1152]{2,1,0:T(8,128)(2,1)S(1)}, u32[]{:S(2)}, u32[]{:S(2)}) async-start(bf16[8,48,1152]{2,1,0:T(8,128)(2,1)} %broadcast_in_dim.5), calls=%async_computation | async-start | bytes 1769472 | tf_op jit(solution)/shard_map/all_to_all | solution.py:281
  30.9 10.7 %collective-permute-start.9 = (bf16[2,48,1152]{2,1,0:T(8,128)(2,1)S(1)}, bf16[2,48,1152]{2,1,0:T(8,128)(2,1)S(1)}, u32[]{:S(2)}, u32[]{:S(2)}) collective-permute-start(bf16[2,48,1152]{2,1,0:T(8,128)(2,1)S(1)} %pad_maximum_fusion.1.refs_0_), channel_id=1, source_target_pairs={{0,48},{16,32},{32,16},{48,0},{1,49},{17,33},{33,17},{49,1},{2,50}... | collective-permute-start | bytes 663560 | tf_op jit(solution)/shard_map/ppermute | solution.py:352
  32.0 9.6 %collective-permute-start.8 = (bf16[2,48,1152]{2,1,0:T(8,128)(2,1)S(1)}, bf16[2,48,1152]{2,1,0:T(8,128)(2,1)S(1)}, u32[]{:S(2)}, u32[]{:S(2)}) collective-permute-start(bf16[2,48,1152]{2,1,0:T(8,128)(2,1)S(1)} %pad_maximum_fusion.1.refs_0_), channel_id=1, source_target_pairs={{0,32},{16,48},{32,0},{48,16},{1,33},{17,49},{33,1},{49,17},{2,34}... | collective-permute-start | bytes 663560 | tf_op jit(solution)/shard_map/ppermute | solution.py:352
  33.7 8.6 %collective-permute-start.7 = (bf16[2,48,1152]{2,1,0:T(8,128)(2,1)S(1)}, bf16[2,48,1152]{2,1,0:T(8,128)(2,1)S(1)}, u32[]{:S(2)}, u32[]{:S(2)}) collective-permute-start(bf16[2,48,1152]{2,1,0:T(8,128)(2,1)S(1)} %pad_maximum_fusion.1.refs_0_), channel_id=1, source_target_pairs={{0,16},{16,0},{32,48},{48,32},{1,17},{17,1},{33,49},{49,33},{2,18}... | collective-permute-start | bytes 663560 | tf_op jit(solution)/shard_map/ppermute | solution.py:352
  42.2 2.4 %collective-permute-start.10 = (bf16[8,48,1152]{2,1,0:T(8,128)(2,1)S(1)}, bf16[8,48,1152]{2,1,0:T(8,128)(2,1)S(1)}, u32[]{:S(2)}, u32[]{:S(2)}) collective-permute-start(bf16[8,48,1152]{2,1,0:T(8,128)(2,1)S(1)} %all-to-all-done.refs_4_), channel_id=1, source_target_pairs={{0,1},{1,0},{2,3},{3,2},{4,5},{5,4},{6,7},{7,6},{8,9},{9,8},{10,11... | collective-permute-start | bytes 2654216 | tf_op jit(solution)/shard_map/ppermute | solution.py:357
  42.2 22.1 %collective-permute-start.6 = (bf16[4,416,256]{2,1,0:T(8,128)(2,1)}, bf16[4,416,256]{2,1,0:T(8,128)(2,1)}, u32[]{:S(2)}, u32[]{:S(2)}) collective-permute-start(bf16[4,416,256]{2,1,0:T(8,128)(2,1)} %bitcast.52), channel_id=1, source_target_pairs={{0,2},{2,0},{1,3},{3,1},{4,6},{6,4},{5,7},{7,5},{8,10},{10,8},{9,1... | collective-permute-start | bytes 2555912 | tf_op jit(solution)/shard_map/ppermute | solution.py:358
  43.7 20.6 %collective-permute-start.5 = (bf16[4,416,256]{2,1,0:T(8,128)(2,1)}, bf16[4,416,256]{2,1,0:T(8,128)(2,1)}, u32[]{:S(2)}, u32[]{:S(2)}) collective-permute-start(bf16[4,416,256]{2,1,0:T(8,128)(2,1)} %bitcast.53), channel_id=1, source_target_pairs={{0,1},{1,0},{2,3},{3,2},{4,5},{5,4},{6,7},{7,6},{8,9},{9,8},{10,11... | collective-permute-start | bytes 2555912 | tf_op jit(solution)/shard_map/ppermute | solution.py:359
  51.4 28.7 %all-to-all-start.1 = ((bf16[32,8,16,128]{3,2,1,0:T(8,128)(2,1)}), bf16[32,8,16,128]{3,2,1,0:T(8,128)(2,1)S(1)}, u32[]{:S(2)}, u32[]{:S(2)}) async-start(bf16[32,8,16,128]{3,2,1,0:T(8,128)(2,1)} %get-tuple-element.35), calls=%async_computation.1 | async-start | bytes 2097152 | tf_op jit(solution)/shard_map/all_to_all | solution.py:430
  64.3 2.6 %collective-permute-start.11 = (bf16[4,416,256]{2,1,0:T(8,128)(2,1)}, bf16[4,416,256]{2,1,0:T(8,128)(2,1)S(1)}, u32[]{:S(2)}, u32[]{:S(2)}) collective-permute-start(bf16[4,416,256]{2,1,0:T(8,128)(2,1)} %collective-permute-done.6.refs_2_.refs_6_), channel_id=1, source_target_pairs={{0,1},{1,0},{2,3},{3,2},{4,5},{5,4},{6,7},{7,6},{8,9},{9,8},{10,11... | collective-permute-start | bytes 2555912 | tf_op jit(solution)/shard_map/ppermute | solution.py:398
  64.4 15.7 %copy-start.2 = (bf16[256,256]{1,0:T(8,128)(2,1)S(1)}, bf16[256,256]{1,0:T(8,128)(2,1)}, u32[]{:S(2)}) copy-start(bf16[256,256]{1,0:T(8,128)(2,1)} %wo_ref.2) | copy-start | bytes 393220
  92.5 20.4 %copy-start.3 = (bf16[256,256]{1,0:T(8,128)(2,1)S(1)}, bf16[256,256]{1,0:T(8,128)(2,1)}, u32[]{:S(2)}) copy-start(bf16[256,256]{1,0:T(8,128)(2,1)} %wq_ref.1) | copy-start | bytes 393220
  92.5 20.4 %copy-start.4 = (bf16[256,256]{1,0:T(8,128)(2,1)S(1)}, bf16[256,256]{1,0:T(8,128)(2,1)}, u32[]{:S(2)}) copy-start(bf16[256,256]{1,0:T(8,128)(2,1)} %wk_ref.1) | copy-start | bytes 393220
  92.5 20.4 %copy-start.5 = (bf16[256,256]{1,0:T(8,128)(2,1)S(1)}, bf16[256,256]{1,0:T(8,128)(2,1)}, u32[]{:S(2)}) copy-start(bf16[256,256]{1,0:T(8,128)(2,1)} %wv_ref.1) | copy-start | bytes 393220
  92.5 20.4 %copy-start.6 = (bf16[256,256]{1,0:T(8,128)(2,1)S(1)}, bf16[256,256]{1,0:T(8,128)(2,1)}, u32[]{:S(2)}) copy-start(bf16[256,256]{1,0:T(8,128)(2,1)} %wg_ref.1) | copy-start | bytes 393220
  92.6 20.4 %copy-start.7 = (bf16[256,256]{1,0:T(8,128)(2,1)S(1)}, bf16[256,256]{1,0:T(8,128)(2,1)}, u32[]{:S(2)}) copy-start(bf16[256,256]{1,0:T(8,128)(2,1)} %wo_ref.3) | copy-start | bytes 393220
